TPU v7x, 256 devices: a whole 4x4x8 slice. The times are simulated.
256 devices in a mesh: grp: 2 (over core), dp: 64 (over z, x, y_lo), mp: 2 (over y_hi).
Axes of the slice: x: 4, y: 4 (y_hi: 2, y_lo: 2; y = y_hi * 2 + y_lo), z: 8, core: 2. Of those that a mesh axis runs over, the one named last changes fastest.
Arguments:
- image_features: bfloat16 [16384, 1152], P('dp'), may hold values from -8 to 8
- text_features: bfloat16 [16384, 1152], P('dp'), may hold values from -8 to 8
- norm_gain: float32 [2, 1152], P('grp'), may hold values from 0.25 to 1.75
- up_weight: bfloat16 [2, 1152, 4304], P('grp', None, 'mp'), may hold values from -0.1875 to 0.1875
- down_weight: bfloat16 [2, 4304, 1152], P('grp', 'mp'), may hold values from -0.09375 to 0.09375
- text_head: bfloat16 [2, 1152, 1152], P('grp', 'mp'), may hold values from -1 to 2
- sub_index: int32 [2048], replicated, may hold values from 0 to 16383, as said below
Outputs:
- learnability: float32 [16384], P(('dp', 'mp'))
- image_grad: float32 [16384, 1152], P(('dp', 'mp'), 'grp')
Inputs may be any that keep to these rules, and one draw needn't show every extreme that they name: `sub_index`: distinct rows in ascending order. Each aligned block of 128 rows holds at most 32 sub-batch rows, and some block holds exactly 32.
All inputs are finite; a program needn't handle non-finite values.
Results may differ from a plain program's by a relative error of at most 0.0067.
Values may be sent and summed in bfloat16 or wider, within the bound.
No kernel may reach another device: no remote copies, remote signals or barrier semaphores. Data moves between devices by JAX's collectives and lax.ppermute only.
A program may use at most 128 MiB of HBM per device.

v0:
```python
import jax
import jax.numpy as jnp
from jax import lax
from jax.sharding import PartitionSpec as P

SCALE = 117.0
BIAS = -12.9
EPS = 1e-06


def pair_terms(z_img, own_ids, piece, ids):
    logits = (
        SCALE * jnp.einsum("id,jd->ij", z_img, piece, preferred_element_type=jnp.float32) + BIAS
    )
    sign = jnp.where(own_ids[:, None] == ids[None, :], 1.0, -1.0).astype(jnp.float32)
    return (logits, sign)


def shards(image_features, text_features, norm_gain, up_weight, down_weight, text_head, sub_index):
    n_mp = lax.axis_size("mp")
    n_dp = lax.axis_size("dp")
    m_idx = lax.axis_index("mp")
    d_idx = lax.axis_index("dp")
    g_idx = lax.axis_index("grp")
    block_rows = image_features.shape[0]
    width = image_features.shape[1]
    rows = block_rows // n_mp
    total = block_rows * n_dp
    x = image_features.astype(jnp.float32)
    mean = jnp.mean(x, axis=1, keepdims=True)
    var = jnp.mean((x - mean) * (x - mean), axis=1, keepdims=True)
    normed = ((x - mean) * lax.rsqrt(var + EPS) * norm_gain[0][None, :]).astype(jnp.bfloat16)
    hidden = jax.nn.gelu(
        jnp.dot(normed, up_weight[0], preferred_element_type=jnp.float32), approximate=True
    ).astype(jnp.bfloat16)
    branch = jnp.dot(hidden, down_weight[0], preferred_element_type=jnp.float32)
    head_rows = text_head.shape[1]
    text_part = lax.dynamic_slice_in_dim(text_features, m_idx * head_rows, head_rows, 1)
    partial_value = jnp.dot(text_part, text_head[0], preferred_element_type=jnp.float32)
    img_sum, txt_sum = (
        lax.psum_scatter(branch, "mp", scatter_dimension=0, tiled=True),
        lax.psum_scatter(partial_value, "mp", scatter_dimension=0, tiled=True),
    )
    base = (d_idx * n_mp + m_idx) * rows
    e_img = lax.dynamic_slice_in_dim(x, m_idx * rows, rows, 0) + img_sum
    n_img = jnp.sqrt(jnp.sum(e_img * e_img, axis=1, keepdims=True) + EPS)
    unit = e_img / n_img
    z_img = unit.astype(jnp.bfloat16)
    n_txt = jnp.sqrt(jnp.sum(txt_sum * txt_sum, axis=1, keepdims=True) + EPS)
    z_txt = (txt_sum / n_txt).astype(jnp.bfloat16)
    chosen = jnp.zeros((total,), jnp.float32).at[sub_index].set(1.0)
    own_chosen = lax.dynamic_slice_in_dim(chosen, base, rows)
    own_ids = base + jnp.arange(rows, dtype=jnp.int32)
    all_ids = jnp.arange(total, dtype=jnp.int32)

    def make_fold(z_rows, row_ids, text_ids):

        def accumulate(carry, piece, start):
            logits, sign = pair_terms(z_rows, row_ids, piece, text_ids)
            loss = jnp.sum(jax.nn.softplus(-sign * logits), axis=1)
            return (loss,)

        return accumulate

    fold = make_fold(z_img, own_ids, all_ids)
    paired = lax.all_gather(z_txt, "mp", axis=0, tiled=True)
    folded = fold(
        (jnp.zeros((rows,), jnp.float32),),
        lax.all_gather(paired, "dp", axis=0, tiled=True),
        jnp.int32(0),
    )
    loss = folded[0]
    cap = rows // 4
    blocks = total // rows
    sub_count = sub_index.shape[0]
    starts = jnp.arange(blocks, dtype=jnp.int32) * rows
    before = jnp.sum((sub_index[None, :] < starts[:, None]).astype(jnp.int32), axis=1)
    slots = before[:, None] + jnp.arange(cap, dtype=jnp.int32)[None, :]
    slot_ids = sub_index[jnp.minimum(slots, sub_count - 1)]
    slot_live = (slots < sub_count) & (slot_ids < (starts + rows)[:, None])
    ids_flat = slot_ids.reshape(-1)
    live_flat = slot_live.reshape(-1).astype(jnp.float32)
    my_block = d_idx * n_mp + m_idx
    my_ids = lax.dynamic_slice_in_dim(ids_flat, my_block * cap, cap)
    my_live = lax.dynamic_slice_in_dim(live_flat, my_block * cap, cap)
    picked = jnp.take(z_txt, jnp.clip(my_ids - base, 0, rows - 1), axis=0)
    packed = jnp.where(my_live[:, None] > 0, picked, jnp.zeros_like(picked))
    piece = lax.all_gather(packed, ("dp", "mp"), axis=0, tiled=True)
    logits, sign = pair_terms(z_img, own_ids, piece, ids_flat)
    slope = (
        -sign * jax.nn.sigmoid(-sign * logits) * live_flat[None, :] * own_chosen[:, None]
    ).astype(jnp.bfloat16)
    slope_sum = jnp.dot(slope, piece, preferred_element_type=jnp.float32)
    grad_sum = SCALE * slope_sum
    grad = (grad_sum - unit * jnp.sum(unit * grad_sum, axis=1, keepdims=True)) / n_img
    learner = g_idx == 1
    signed_loss = jnp.where(learner, loss, -loss)
    learner_grad = jnp.where(learner, grad, jnp.zeros_like(grad))
    learnability, both_grad = lax.psum((signed_loss, learner_grad), "grp")
    half = width // 2
    image_grad = lax.dynamic_slice_in_dim(both_grad, g_idx * half, half, 1)
    return (learnability, image_grad)


def solution(mesh):
    in_specs = (
        P("dp", None),
        P("dp", None),
        P("grp", None),
        P("grp", None, "mp"),
        P("grp", "mp", None),
        P("grp", "mp", None),
        P(),
    )
    out_specs = (P(("dp", "mp")), P(("dp", "mp"), "grp"))
    return jax.shard_map(shards, mesh=mesh, in_specs=in_specs, out_specs=out_specs, check_vma=False)
```

profile of v0, /device:TPU:1, one launch (start us, length us, event | category | flops | bytes accessed | tf_op | source)
XLA Modules:
  0.0 1631.1 jit_solution(4555182654694744158)
XLA Ops:
  7.2 0.0 copy-start
  7.2 0.0 copy-start.4
  7.2 0.0 reduce-scatter.5.cloned.1.call-start
  7.3 1.2 copy-done
  8.5 2.7 fusion.29
  11.2 0.0 reduce-scatter.5.cloned.1.call-update
  11.2 0.0 reduce-scatter.3.cloned.1.call-start
  11.3 0.2 convert_reduce_fusion.1
  11.5 0.3 multiply_reduce_fusion
  11.8 0.0 copy-start.2
  11.8 10.8 fusion.3
  22.7 0.0 reduce-scatter.3.cloned.1.call-update
  22.7 0.0 all-gather.5.cloned.1.call-start
  22.8 0.2 convert_reduce_fusion
  23.0 0.1 compare_select_fusion.1
  23.1 0.1 reshape.125
  23.2 23.0 %gather_fusion = s32[4096]{0:T(1024)S(1)} fusion(s32[2048]{0:T(1024)S(1)} %copy-done.2, s32[4096]{0:T(1024)S(1)} %broadcast_clamp_fusion), kind=kCustom, calls=%fused_computation | custom fusion | bytes 49152 | tf_op jit(solution)/shard_map/gather | solution.py:79
  46.3 0.1 add_compare_fusion
  46.4 0.1 lt.88
  46.5 0.1 lt.89
  46.5 0.1 lt.90
  46.6 0.1 compare_and_fusion
  46.7 0.0 reduce-scatter.5.cloned.1.call-done
  46.8 1.2 multiply_reduce_fusion.2
  48.0 1.2 divide_convert_fusion
  49.1 0.6 gather_fusion.1
  49.8 0.7 select_select_fusion
  50.5 0.0 all-gather.5.cloned.1.call-update
  50.5 0.0 all-reduce.2.cloned.1.call-start
  50.6 0.1 convert_element_type.28
  50.7 8.3 scatter_custom_fusion
  59.0 0.1 dynamic_slice.22
  59.1 15.0 reduce-scatter.3.cloned.1.call-done
  74.0 1.2 multiply_reduce_fusion.3
  75.2 1.2 broadcast_divide_fusion
  76.4 585.9 %all-gather.5.cloned.1.call-done = bf16[4096,1152]{1,0:T(8,128)(2,1)} async-done(((bf16[32,1152]{1,0:T(8,128)(2,1)}), bf16[4096,1152]{1,0:T(8,128)(2,1)}) %all-gather.5.cloned.1.call-update) | async-done | bytes 9437200 | tf_op jit(solution)/shard_map/all_gather | solution.py:88
  662.3 11.0 multiply_reduce_fusion.1
  673.4 1.0 divide_select_fusion
  674.4 0.0 all-reduce.2.cloned.1.call-update
  674.4 0.0 all-gather.3.cloned.1.call-start
  674.5 8.7 all_gather.9
  683.1 0.0 all-gather.3.cloned.1.call-update
  683.1 105.0 %all-reduce.2.cloned.1.call-done = f32[128,1152]{1,0:T(8,128)} async-done(((f32[128,1152]{1,0:T(8,128)}), f32[128,1152]{1,0:T(8,128)}) %all-reduce.2.cloned.1.call-update) | async-done | bytes 589840 | tf_op jit(solution)/shard_map/psum | solution.py:99
  788.1 1.1 constant_dynamic-slice_fusion
  789.2 0.9 copy.11
  790.1 813.6 %all-gather.3.cloned.1.call-done = bf16[16384,1152]{1,0:T(8,128)(2,1)} async-done(((bf16[256,1152]{1,0:T(8,128)(2,1)}), bf16[16384,1152]{1,0:T(8,128)(2,1)}) %all-gather.3.cloned.1.call-update) | async-done | bytes 37748752 | tf_op jit(solution)/shard_map/all_gather | solution.py:69
  1603.7 17.4 %fusion.2 = f32[128]{0:T(128)S(1)} fusion(bf16[16384,1152]{1,0:T(8,128)(2,1)} %all-gather.3.cloned.1.call-done, s32[128]{0:T(128)S(1)} %iota_add_fusion, f32[128,1152]{1,0:T(8,128)S(1)} %broadcast_divide_fusion), kind=kOutput, calls=%fused_computation.7 | convolution fusion | flops 4859248640 | bytes 38339584 | tf_op jit(solution)/shard_map/id,jd->ij/dot_general | solution.py:13
  1621.1 3.5 psum.14
  (20 shorter events, 0.1 us)
Async XLA Ops:
  7.2 1.3 copy-start
  7.2 4.1 copy-start.4
  7.2 4.1 copy-start.3
  7.2 39.6 %reduce-scatter.5.cloned.1.call-start = ((), (), s32[]{:S(2)}) async-start(), calls=%async_computation.3 | async-start | bytes 1769472 | tf_op jit(solution)/shard_map/reduce_scatter | solution.py:42
  11.2 62.8 %reduce-scatter.3.cloned.1.call-start = ((), (), s32[]{:S(2)}) async-start(), calls=%async_computation.2 | async-start | bytes 1769472 | tf_op jit(solution)/shard_map/reduce_scatter | solution.py:41
  11.8 10.9 copy-start.2
  22.7 639.6 %all-gather.5.cloned.1.call-start = ((), (), s32[]{:S(2)}) async-start(), calls=%async_computation.5 | async-start | bytes 9510912 | tf_op jit(solution)/shard_map/all_gather | solution.py:88
  50.5 737.6 %all-reduce.2.cloned.1.call-start = ((), (), s32[]{:S(2)}) async-start(), calls=%async_computation.6 | async-start | bytes 1179648 | tf_op jit(solution)/shard_map/psum | solution.py:99
  674.4 929.3 %all-gather.3.cloned.1.call-start = ((), (), s32[]{:S(2)}) async-start(), calls=%async_computation.4 | async-start | bytes 38338560 | tf_op jit(solution)/shard_map/all_gather | solution.py:69
  1603.7 20.9 %copy-start.1 = (bf16[1,576,1152]{2,1,0:T(8,128)(2,1)S(1)}, bf16[1,576,1152]{2,1,0:T(8,128)(2,1)}, u32[]{:S(2)}) copy-start(bf16[1,576,1152]{2,1,0:T(8,128)(2,1)} %param.12) | copy-start | bytes 3981316
Sparse Core Ops, SparseCore 0:
  11.4 32.1 reduce-scatter.4
  46.2 27.7 reduce-scatter.2
  76.4 585.9 all-gather.4
  674.5 113.5 all-reduce.1
  789.9 813.7 all-gather.2
where the time goes:
time: 1630 us
  waiting for transfers between devices  1520 us (93%)
  matrix products  42 us (3%)
  local copies, waits for them, and re-layouts  35.6 us (2%)
    all_gather x1, waiting for transfers between devices, shards(): lax.all_gather(paired, 'dp', axis=0, tiled=True)  814 us
    all_gather x1, waiting for transfers between devices, shards(): piece = lax.all_gather(packed, ('dp', 'mp'), axis=0, tiled=True)  586 us
    psum x1, waiting for transfers between devices, shards(): learnability, both_grad = lax.psum((signed_loss, learner_grad), 'grp')  105 us
  transfers between devices with their start and end apart: 5, of which 4 were waited for; matrix products, arithmetic and copies ran while one was open for 3% of the time, Pallas kernels for 0%

commit v1 on v0

v1 whole, which is shorter than its diff:
```python
import jax
import jax.numpy as jnp
from jax import lax
from jax.experimental import pallas as pl
from jax.experimental.pallas import tpu as pltpu
from jax.sharding import Mesh, PartitionSpec as P

SCALE = 117.0
BIAS = -12.9
EPS = 1e-06
LOG2E = 1.4426950408889634
LN2 = 0.6931471805599453
NZ, NX, NY = 8, 4, 4
ROWS = 128
CAP = 32
AXES = ("grp", "z", "x", "ylo", "yhi")
ZOFF = (0, -1, 1, -2, 2, -3, 3, 4)
POFF = (0, -1, 1, 2)
EXACT = lax.Precision.HIGHEST


def place(g, z, x, y):
    return ((g * NZ + z) * NX + x) * NY + (y % 2) * 2 + y // 2


def permute(v, target, cores=(0, 1)):
    perm = [
        (place(g, z, x, y), place(*target(g, z, x, y)))
        for g in cores
        for z in range(NZ)
        for x in range(NX)
        for y in range(NY)
    ]
    return lax.ppermute(v, AXES, perm)


def over_mp(v):
    return permute(v, lambda g, z, x, y: (g, z, x, (y + 2) % NY))


def over_z(v, shifts, cores=(0, 1)):
    return permute(v, lambda g, z, x, y: (g, (z + shifts[g]) % NZ, x, y), cores)


def over_plane(v, shift, first):
    def target(g, z, x, y):
        if g == first:
            return (g, z, (x + shift) % NX, y)
        return (g, z, x, (y + shift) % NY)

    return permute(v, target)


def swap_cores(v):
    return permute(v, lambda g, z, x, y: (1 - g, z, x, y))


def to_reference(v):
    return permute(v, lambda g, z, x, y: (0, z, x, y), (1,))


def ring8(v):
    back, ahead = [v], [v]
    for _ in range(3):
        back.append(over_z(back[-1], (1, 1)))
        ahead.append(over_z(ahead[-1], (-1, -1)))
    return back, ahead


def shape(dims, dtype=jnp.float32):
    return jax.ShapeDtypeStruct(dims, dtype)


def call(kernel, scalars, arrays, outs, flops, mib=8, transcendentals=0, scratch=()):
    vmem = pl.BlockSpec(memory_space=pltpu.VMEM)
    return pl.pallas_call(
        kernel,
        in_specs=[pl.BlockSpec(memory_space=pltpu.SMEM)] * len(scalars) + [vmem] * len(arrays),
        out_specs=[vmem] * len(outs),
        out_shape=outs,
        scratch_shapes=scratch,
        compiler_params=pltpu.CompilerParams(vmem_limit_bytes=mib * 1024 * 1024),
        cost_estimate=pl.CostEstimate(
            flops=flops, bytes_accessed=1 << 20, transcendentals=transcendentals
        ),
    )(*scalars, *arrays)


def index_kernel(sub_ref, chosen_ref, place_ref):
    sub = sub_ref[...]
    line = lax.broadcasted_iota(jnp.int32, (ROWS, sub.shape[1]), 0)
    in_block = jnp.where((sub >> 7) == line, 1.0, 0.0).astype(jnp.bfloat16)
    at_off = jnp.where((sub & 127) == line, 1.0, 0.0).astype(jnp.bfloat16)
    chosen = lax.dot_general(
        in_block, at_off, (((1,), (1,)), ((), ())), preferred_element_type=jnp.float32
    )
    row = lax.broadcasted_iota(jnp.int32, (ROWS, ROWS), 0)
    col = lax.broadcasted_iota(jnp.int32, (ROWS, ROWS), 1)
    upper = jnp.where(row < col, 1.0, 0.0).astype(jnp.bfloat16)
    rank = jnp.dot(chosen.astype(jnp.bfloat16), upper, preferred_element_type=jnp.float32)
    chosen_ref[...] = chosen
    place_ref[...] = jnp.where(chosen > 0.5, rank, -1.0)


def split_rows(acc_ref, m, own_ref, other_ref):
    rows = own_ref.shape[0]
    own_ref[...] = acc_ref[pl.ds(pl.multiple_of(m * rows, rows), rows), :]
    other = acc_ref[pl.ds(pl.multiple_of((1 - m) * rows, rows), rows), :]
    other_ref[...] = other.astype(jnp.bfloat16)


def text_kernel(pos_ref, text_ref, head_ref, own_ref, other_ref, acc_ref):
    depth = head_ref.shape[0]
    m = pos_ref[0]
    text = text_ref[...]
    part = jnp.where(m == 0, text[:, :depth], text[:, depth:])
    acc_ref[...] = jnp.dot(part, head_ref[...], preferred_element_type=jnp.float32)
    split_rows(acc_ref, m, own_ref, other_ref)


def mlp_kernel(
    pos_ref, gain_ref, x_hbm, up_hbm, down_hbm, own_ref, other_ref,
    x_ref, up_ref, down_ref, normed_ref, hidden_ref, acc_ref, sems,
):
    copies = [
        pltpu.make_async_copy(source, target, sems.at[k])
        for k, (source, target) in enumerate(
            [(x_hbm, x_ref), (up_hbm, up_ref), (down_hbm, down_ref)]
        )
    ]
    for c in copies:
        c.start()
    copies[0].wait()
    x = x_ref[...].astype(jnp.float32)
    mean = jnp.mean(x, axis=1, keepdims=True)
    gap = x - mean
    var = jnp.mean(gap * gap, axis=1, keepdims=True)
    normed_ref[...] = (gap * lax.rsqrt(var + EPS) * gain_ref[...]).astype(jnp.bfloat16)
    copies[1].wait()
    total, block = up_ref.shape[0], 512
    for start in range(0, total, block):
        stop = min(start + block, total)
        acc = lax.dot_general(
            normed_ref[...],
            up_ref[start:stop, :],
            (((1,), (1,)), ((), ())),
            preferred_element_type=jnp.float32,
        )
        hidden_ref[:, start:stop] = jax.nn.gelu(acc, approximate=True).astype(jnp.bfloat16)
    copies[2].wait()
    block = 384
    for start in range(0, acc_ref.shape[1], block):
        acc_ref[:, start : start + block] = jnp.dot(
            hidden_ref[...], down_ref[:, start : start + block], preferred_element_type=jnp.float32
        )
    split_rows(acc_ref, pos_ref[0], own_ref, other_ref)


def image_mlp(pos, gain, x, up, down):
    rows, width = x.shape
    hidden = up.shape[0]
    bf16 = jnp.bfloat16
    vmem, hbm = pl.BlockSpec(memory_space=pltpu.VMEM), pl.BlockSpec(memory_space=pl.ANY)
    return pl.pallas_call(
        mlp_kernel,
        in_specs=[pl.BlockSpec(memory_space=pltpu.SMEM), vmem, hbm, hbm, hbm],
        out_specs=[vmem, vmem],
        out_shape=[shape((rows // 2, width)), shape((rows // 2, width), bf16)],
        scratch_shapes=[
            pltpu.VMEM((rows, width), bf16),
            pltpu.VMEM((hidden, width), bf16),
            pltpu.VMEM((hidden, width), bf16),
            pltpu.VMEM((rows, width), bf16),
            pltpu.VMEM((rows, hidden), bf16),
            pltpu.VMEM((rows, width), jnp.float32),
            pltpu.SemaphoreType.DMA((3,)),
        ],
        compiler_params=pltpu.CompilerParams(vmem_limit_bytes=52 * 1024 * 1024),
        cost_estimate=pl.CostEstimate(
            flops=4 * rows * width * hidden, bytes_accessed=11 << 20, transcendentals=rows * hidden
        ),
    )(pos, gain, x, up, down)


def text_unit_kernel(own_ref, recv_ref, z_ref):
    e = own_ref[...] + recv_ref[...].astype(jnp.float32)
    n = jnp.sqrt(jnp.sum(e * e, axis=1, keepdims=True) + EPS)
    z_ref[...] = (e / n).astype(jnp.bfloat16)


def own_pick(place_row):
    slot = lax.broadcasted_iota(jnp.int32, (CAP, ROWS), 0).astype(jnp.float32)
    return jnp.where(place_row == slot, 1.0, 0.0)


def image_unit_kernel(
    pos_ref, own_ref, recv_ref, x_ref, place_ref, z_ref, unit_ref, n_ref, give_ref
):
    rows = own_ref.shape[0]
    x = x_ref[pl.ds(pl.multiple_of(pos_ref[0] * rows, rows), rows), :].astype(jnp.float32)
    e = x + (own_ref[...] + recv_ref[...].astype(jnp.float32))
    n = jnp.sqrt(jnp.sum(e * e, axis=1, keepdims=True) + EPS)
    unit = e / n
    z_ref[...] = unit.astype(jnp.bfloat16)
    pick = own_pick(place_ref[pl.ds(pos_ref[1] * (NX * NY) + pos_ref[4], 1), :])
    unit = jnp.dot(pick, unit, precision=EXACT, preferred_element_type=jnp.float32)
    n_rows = jnp.broadcast_to(n, (rows, n_ref.shape[1]))
    n_sub = jnp.dot(pick, n_rows, precision=EXACT, preferred_element_type=jnp.float32)
    n_sub = jnp.where(n_sub > 0.0, n_sub, 1.0)
    unit_ref[...] = unit
    n_ref[...] = n_sub
    cut = unit.shape[1] // 2
    give_ref[:, :cut] = unit[:, :cut]
    give_ref[:, cut:] = n_sub


def join_kernel(*refs):
    refs[-1][...] = jnp.concatenate([r[...] for r in refs[:-1]], axis=0)


def fold_terms(e):
    n = e.shape[0]
    while n > 1:
        n //= 2
        a, b = e[:n], e[n:]
        e = a + (b + a * b)
    return e[0]


def tile_loss(text, img, own):
    rows, width = text.shape[0], img.shape[0]
    t = lax.dot_general(text, img, (((1,), (1,)), ((), ())), preferred_element_type=jnp.float32)
    t = t * (SCALE * LOG2E) + (BIAS * LOG2E)
    if own:
        row = lax.broadcasted_iota(jnp.int32, (ROWS, width), 0)
        col = lax.broadcasted_iota(jnp.int32, (ROWS, width), 1)
        t = jnp.concatenate([jnp.where(col == row, -t[:ROWS], t[:ROWS]), t[ROWS:]], axis=0)
    t = t.reshape(rows // 8, 8, width)
    high = jnp.sum(jnp.maximum(t, 0.0), axis=0)
    low = jnp.log1p(fold_terms(jnp.exp2(-jnp.abs(t))))
    return high * LN2 + low


def image_row(z, offset):
    return lax.rem(z + (offset + NZ), NZ)


def pair_kernel(pos_ref, chosen_ref, place_ref, *refs):
    images, texts, (loss_ref, keep_ref, give_ref) = refs[:NZ], refs[NZ:-3], refs[-3:]
    z, x, y, xy = pos_ref[1], pos_ref[2], pos_ref[3], pos_ref[4]
    planes = NX * NY
    block = 256
    pieces = [(ref, s) for ref in texts for s in range(0, ref.shape[0], block)]

    picks = [own_pick(place_ref[pl.ds(image_row(z, o) * planes + xy, 1), :]) for o in ZOFF]
    packed = jnp.concatenate(
        [
            jnp.dot(p.astype(jnp.bfloat16), images[k][...], preferred_element_type=jnp.float32)
            for k, p in enumerate(picks)
        ],
        axis=0,
    ).astype(jnp.bfloat16)

    def text_row(dx, dy):
        tx, ty = lax.rem(x + (dx + NX), NX), lax.rem(y + (dy + NY), NY)
        row = z * planes + tx * NY + lax.rem(ty, 2) * 2 + ty // 2
        return chosen_ref[pl.ds(row, 1), :]

    lines = [text_row(dx, dy) for dx in POFF for dy in POFF]
    total = jnp.zeros(packed.shape, jnp.float32)
    for k, (ref, s) in enumerate(pieces):
        text = ref[s : s + block, :]
        mask = jnp.concatenate(lines[2 * k : 2 * k + 2], axis=1)
        t = lax.dot_general(
            packed, text, (((1,), (1,)), ((), ())), preferred_element_type=jnp.float32
        )
        t = t * SCALE + BIAS
        sign = jnp.ones(t.shape, jnp.float32)
        if k == 0:
            own = jnp.concatenate([1.0 - 2.0 * picks[0], sign[:CAP, ROWS:]], axis=1)
            sign = jnp.concatenate([own, sign[CAP:]], axis=0)
        t = sign * t
        e = jnp.exp(-jnp.abs(t))
        s = jnp.where(t >= 0, 1.0, e) / (1.0 + e)
        slope = (sign * s * mask).astype(jnp.bfloat16)
        total = total + jnp.dot(slope, text, preferred_element_type=jnp.float32)
    total = total.astype(jnp.bfloat16)
    cut = keep_ref.shape[1]
    for k, o in enumerate(ZOFF):
        rows = pl.ds(pl.multiple_of(image_row(z, o) * CAP, CAP), CAP)
        give_ref[rows, :] = total[k * CAP : (k + 1) * CAP, :cut]
        keep_ref[rows, :] = total[k * CAP : (k + 1) * CAP, cut:]

    for number in range(NZ // 2):
        img = jnp.concatenate([images[2 * number][...], images[2 * number + 1][...]], axis=0)
        total = jnp.zeros((8, img.shape[0]), jnp.float32)
        for k, (ref, s) in enumerate(pieces):
            total = total + tile_loss(ref[s : s + block, :], img, number == 0 and k == 0)
        total = jnp.sum(total, axis=0, keepdims=True)
        for k in range(2):
            row = image_row(z, ZOFF[2 * number + k])
            loss_ref[pl.ds(row, 1), :] = total[:, k * ROWS : (k + 1) * ROWS]


def load_kernel(pos_ref, keep_ref, recv_ref, loss_ref, out_ref):
    learner = pos_ref[5] == 1
    loss = loss_ref[...]
    parts = []
    for _ in range(3):
        part = loss.astype(jnp.bfloat16)
        loss = loss - part.astype(jnp.float32)
        parts.append(part.astype(jnp.float32))
    side = ROWS // 2
    for z in range(NZ):
        rows = slice(z * CAP, (z + 1) * CAP)
        halves = [p[z : z + 1, k * side : (k + 1) * side] for p in parts for k in range(2)]
        beside = jnp.concatenate(halves + [jnp.zeros((CAP - 6, side), jnp.float32)], axis=0)
        grad = jnp.where(learner, keep_ref[rows, :], recv_ref[rows, :])
        out_ref[rows, :] = jnp.concatenate([grad, beside.astype(jnp.bfloat16)], axis=1)


def finish_kernel(pos_ref, load_ref, unit_ref, given_ref, n_ref, g_ref, msg_ref):
    learner = pos_ref[5] == 1
    cut = g_ref.shape[1]
    total = load_ref[:CAP, :].astype(jnp.float32)
    for z in range(1, NZ):
        total = total + load_ref[z * CAP : (z + 1) * CAP, :].astype(jnp.float32)
    g = SCALE * total[:, :cut]
    unit = jnp.where(learner, unit_ref[:, cut:], given_ref[:, :cut])
    n = jnp.where(learner, n_ref[...], given_ref[:, cut:])
    g_ref[...] = g
    dots = jnp.sum(unit * g, axis=1, keepdims=True)
    beside = total[:, cut:]
    loss = jnp.concatenate(
        [beside[k : k + 1] + beside[k + 2 : k + 3] + beside[k + 4 : k + 5] for k in range(2)], axis=1
    )
    msg_ref[:CAP, :] = jnp.broadcast_to(dots, (CAP, ROWS))
    msg_ref[CAP:, :] = jnp.broadcast_to(loss, (8, ROWS))


def spread_kernel(
    pos_ref, g_ref, unit_ref, given_ref, n_ref, own_ref, other_ref, place_ref, learn_ref, out_ref
):
    learner = pos_ref[5] == 1
    cut = g_ref.shape[1]
    unit = jnp.where(learner, unit_ref[:, cut:], given_ref[:, :cut])
    n = jnp.where(learner, n_ref[...], given_ref[:, cut:])[:, :1]
    dots = (own_ref[:CAP, :] + other_ref[:CAP, :])[:, :1]
    grad = (g_ref[...] - unit * dots) / n
    pick = own_pick(place_ref[pl.ds(pos_ref[1] * (NX * NY) + pos_ref[4], 1), :])
    out_ref[...] = lax.dot_general(
        pick, grad, (((0,), (0,)), ((), ())), precision=EXACT, preferred_element_type=jnp.float32
    )
    own, other = own_ref[CAP : CAP + 1, :], other_ref[CAP : CAP + 1, :]
    learn_ref[...] = jnp.where(learner, own - other, other - own)


def shards(image_features, text_features, norm_gain, up_weight, down_weight, text_head, sub_index):
    g_idx = lax.axis_index("grp")
    z_idx = lax.axis_index("z")
    x_idx = lax.axis_index("x")
    m_idx = lax.axis_index("yhi")
    l_idx = lax.axis_index("ylo")
    width = image_features.shape[1]
    rows = image_features.shape[0] // 2
    blocks = NZ * NX * NY
    cut = width // 2
    bf16 = jnp.bfloat16
    pos = [m_idx, z_idx, x_idx, m_idx * 2 + l_idx, (x_idx * 2 + l_idx) * 2 + m_idx, g_idx]
    pos = jnp.stack([p.astype(jnp.int32) for p in pos])
    cells = rows * width

    own_img, other_img = image_mlp(pos, norm_gain, image_features, up_weight[0].T, down_weight[0])
    recv_img = over_mp(other_img)
    features, own_img = lax.optimization_barrier((text_features, own_img))
    own_text, other_text = call(
        text_kernel,
        [pos],
        [features, text_head[0]],
        [shape((rows, width)), shape((rows, width), bf16)],
        2 * cells * width,
        scratch=[pltpu.VMEM((2 * rows, width), jnp.float32)],
    )
    recv_text = over_mp(other_text)
    chosen, place_of = call(
        index_kernel, [], [sub_index.reshape(1, -1)], [shape((blocks, rows))] * 2, 100 << 20
    )
    z_img, unit_sub, n_sub, give = call(
        image_unit_kernel,
        [pos],
        [own_img, recv_img, image_features, place_of],
        [shape((rows, width), bf16), shape((CAP, width)), shape((CAP, rows)), shape((CAP, cut + rows))],
        400 * cells,
    )
    own_text, z_img = lax.optimization_barrier((own_text, z_img))
    (z_txt,) = call(
        text_unit_kernel, [], [own_text, recv_text], [shape((rows, width), bf16)], 20 * cells
    )
    line = [z_txt] + [over_plane(z_txt, shift, 0) for shift in (1, -1, 2)]
    (joined,) = call(join_kernel, [], line, [shape((4 * rows, width), bf16)], cells)
    back, ahead = over_plane(joined, 1, 1), over_plane(joined, -1, 1)
    far_top = over_plane(back[: 2 * rows], 1, 1)
    far_low = over_plane(ahead[2 * rows :], -1, 1)
    texts = [joined, back, ahead, far_top, far_low]

    from_back, from_ahead = ring8(z_img)
    last = jnp.where(g_idx == 0, from_back[3], from_ahead[3])
    images = [z_img, from_back[1], from_ahead[1], from_back[2], from_ahead[2]]
    images += [from_back[3], from_ahead[3], over_z(last, (1, -1))]

    given = to_reference(give)

    n_text, n_img = NX * NY * rows, NZ * rows
    loss_part, g_keep, g_give = call(
        pair_kernel,
        [pos],
        [chosen, place_of] + images + texts,
        [shape((NZ, rows))] + [shape((NZ * CAP, cut), bf16)] * 2,
        (2 * n_img + 4 * NZ * CAP) * width * n_text,
        mib=16,
        transcendentals=(n_img + NZ * CAP) * n_text,
    )
    (load,) = call(
        load_kernel,
        [pos],
        [g_keep, to_reference(g_give), loss_part],
        [shape((NZ * CAP, cut + rows // 2), bf16)],
        cells,
    )
    load = lax.all_to_all(load, "z", 0, 0, tiled=True)
    g_sum, msg = call(
        finish_kernel,
        [pos],
        [load, unit_sub, given, n_sub],
        [shape((CAP, cut)), shape((CAP + 8, rows))],
        10 * cells,
    )
    learn, image_grad = call(
        spread_kernel,
        [pos],
        [g_sum, unit_sub, given, n_sub, msg, swap_cores(msg), place_of],
        [shape((1, rows)), shape((rows, cut))],
        200 * cells,
    )
    return (learn.reshape(rows), image_grad)


def solution(mesh):
    fine = Mesh(mesh.devices.reshape(2, NZ, NX, 2, 2), AXES)
    dp = ("z", "x", "ylo")
    in_specs = (
        P(dp, None),
        P(dp, None),
        P("grp", None),
        P("grp", None, "yhi"),
        P("grp", "yhi", None),
        P("grp", "yhi", None),
        P(),
    )
    out_specs = (P(dp + ("yhi",)), P(dp + ("yhi",), "grp"))
    return jax.shard_map(shards, mesh=fine, in_specs=in_specs, out_specs=out_specs, check_vma=False)
```

time: 1630 us -> 124 us (0.08)
  waiting for transfers between devices: 1520 us -> 44 us
  starting transfers between devices: 0.21 us -> 46 us
  matrix products: 42 us -> 0 us
  local copies, waits for them, and re-layouts: 35.6 us -> 5.95 us
  Pallas kernels: 0 us -> 26.9 us
    all_gather x2 -> x0, waiting for transfers between devices: 1400 us -> none  [the longest x1 814 us: shards(): lax.all_gather(paired, 'dp', axis=0, tiled=True)]
    psum x1 -> x0, waiting for transfers between devices: 105 us -> none  [shards(): learnability, both_grad = lax.psum((signed_loss, learner_grad), 'grp')]
    dot_general x4 -> x0, matrix products: 42 us -> none  [the longest x1 17.4 us: pair_terms(): jnp.einsum('id,jd->ij', z_img, piece, preferred_element_type=jnp.float32)]
    ppermute x0 -> x19, starting transfers between devices: none -> 41.8 us  [permute(): return lax.ppermute(v, AXES, perm)]
    ppermute x0 -> x19, waiting for transfers between devices: none -> 33.9 us  [permute(): return lax.ppermute(v, AXES, perm)]
    pallas_call x0 -> x10, Pallas kernels: none -> 26.9 us  [the longest x9 19.7 us: call(): pl.pallas_call(kernel, in_specs=[pl.BlockSpec(memory_space=pltpu.SMEM)] *...]
    gather x2 -> x0, local copies, waits for them, and re-layouts: 23.7 us -> none  [the longest x1 23 us: shards(): slot_ids = sub_index[jnp.minimum(slots, sub_count - 1)]]
  transfers between devices with their start and end apart: 5 -> 20, of which waited for: 4 -> 14; matrix products, arithmetic and copies ran while one was open for 3% -> 1% of each run, Pallas kernels for 0% -> 2%
where the time goes in v1:
time: 124 us
  starting transfers between devices  46 us (37%)
  waiting for transfers between devices  44 us (35%)
  Pallas kernels  26.9 us (22%)
  local copies, waits for them, and re-layouts  5.95 us (5%)
    ppermute x19, starting transfers between devices, permute(): return lax.ppermute(v, AXES, perm)  41.8 us
    ppermute x19, waiting for transfers between devices, permute(): return lax.ppermute(v, AXES, perm)  33.9 us
    pallas_call x9, Pallas kernels, call(): pl.pallas_call(kernel, in_specs=[pl.BlockSpec(memory_space=pltpu.SMEM)] *...  19.7 us
    all_to_all x1, waiting for transfers between devices, shards(): load = lax.all_to_all(load, 'z', 0, 0, tiled=True)  10.1 us
    pallas_call x1, Pallas kernels, image_mlp(): pl.pallas_call(mlp_kernel, in_specs=[pl.BlockSpec(memory_space=pltpu.SMEM...  7.24 us
    unnamed x23, local copies, waits for them, and re-layouts  4.7 us
    all_to_all x1, starting transfers between devices, shards(): load = lax.all_to_all(load, 'z', 0, 0, tiled=True)  4.23 us
  transfers between devices with their start and end apart: 20, of which 14 were waited for; matrix products, arithmetic and copies ran while one was open for 1% of the time, Pallas kernels for 2%

profile of v1, /device:TPU:1, one launch (start us, length us, event | category | flops | bytes accessed | tf_op | source)
XLA Modules:
  0.0 123.7 jit_solution(1945093315000770485)
XLA Ops:
  0.6 0.1 stack.27.pos_ref
  0.7 1.1 copy-done
  1.8 0.7 copy-done.3
  2.5 7.2 %shard_map.87 = (f32[128,1152]{1,0:T(8,128)S(1)}, bf16[128,1152]{1,0:T(8,128)(2,1)S(1)}) custom-call(s32[6]{0:T(128)S(1)} %stack.27.pos_ref, f32[1,1152]{1,0:T(1,128)S(1)} %copy-done.3, bf16[256,1152]{1,0:T(8,128)(2,1)S(1)} %copy-done, bf16[2152,1152]{1,0:T(8,128)(2,1)} %bitcast.18, bf16[2152,1152]{1,0:T(8,128)(2,1)} %bitcast.19), custom_call_target="tpu_custom_call" | custom-call | flops 2538602496 | bytes 11534336 | tf_op jit(solution)/shard_map/pallas_call | solution.py:164
  9.7 3.8 %collective-permute-start = (bf16[128,1152]{1,0:T(8,128)(2,1)S(1)}, bf16[128,1152]{1,0:T(8,128)(2,1)S(1)}, u32[]{:S(2)}, u32[]{:S(2)}) collective-permute-start(bf16[128,1152]{1,0:T(8,128)(2,1)S(1)} %get-tuple-element.29), channel_id=1, source_target_pairs={{0,1},{2,3},{1,0},{3,2},{4,5},{6,7},{5,4},{7,6},{8,9},{10,11},{9,8... | collective-permute-start | bytes 884744 | tf_op jit(solution)/shard_map/ppermute | solution.py:34
  13.6 1.3 %shard_map.88 = (f32[128,1152]{1,0:T(8,128)S(1)}, bf16[128,1152]{1,0:T(8,128)(2,1)S(1)}) custom-call(s32[6]{0:T(128)S(1)} %stack.27.pos_ref, bf16[256,1152]{1,0:T(8,128)(2,1)S(1)} %copy-done.2, bf16[576,1152]{1,0:T(8,128)(2,1)S(1)} %bitcast.15), custom_call_target="tpu_custom_call" | custom-call | flops 339738624 | bytes 1048576 | tf_op jit(solution)/shard_map/pallas_call | solution.py:76
  14.9 0.1 collective-permute-start.8
  15.0 0.5 shard_map.86
  15.5 3.8 %collective-permute-done.recv_ref = bf16[128,1152]{1,0:T(8,128)(2,1)S(1)} collective-permute-done((bf16[128,1152]{1,0:T(8,128)(2,1)S(1)}, bf16[128,1152]{1,0:T(8,128)(2,1)S(1)}, u32[]{:S(2)}, u32[]{:S(2)}) %collective-permute-start) | collective-permute-done | bytes 294944 | tf_op jit(solution)/shard_map/ppermute | solution.py:34
  19.3 1.3 %shard_map.89 = (bf16[128,1152]{1,0:T(8,128)(2,1)S(1)}, f32[32,1152]{1,0:T(8,128)S(1)}, f32[32,128]{1,0:T(8,128)S(1)}, f32[32,704]{1,0:T(8,128)S(1)}) custom-call(s32[6]{0:T(128)S(1)} %stack.27.pos_ref, f32[128,1152]{1,0:T(8,128)S(1)} %get-tuple-element.28.own_ref, bf16[128,1152]{1,0:T(8,128)(2,1)S(1)} %collective-permute-done.recv_ref, ...), custom_call_target="tpu_custom_call" | custom-call | flops 58982400 | bytes 1048576 | tf_op jit(solution)/shard_map/pallas_call | solution.py:76
  20.5 0.6 copy-done.8
  21.2 4.4 %collective-permute-done.8.recv_ref = bf16[128,1152]{1,0:T(8,128)(2,1)S(1)} collective-permute-done((bf16[128,1152]{1,0:T(8,128)(2,1)S(1)}, bf16[128,1152]{1,0:T(8,128)(2,1)S(1)}, u32[]{:S(2)}, u32[]{:S(2)}) %collective-permute-start.8) | collective-permute-done | bytes 294944 | tf_op jit(solution)/shard_map/ppermute | solution.py:34
  25.6 0.2 shard_map.90.refs_0_
  25.8 3.8 %collective-permute-start.11 = (bf16[128,1152]{1,0:T(8,128)(2,1)S(1)}, bf16[128,1152]{1,0:T(8,128)(2,1)S(1)}, u32[]{:S(2)}, u32[]{:S(2)}) collective-permute-start(bf16[128,1152]{1,0:T(8,128)(2,1)S(1)} %shard_map.90.refs_0_), channel_id=1, source_target_pairs={{0,8},{2,10},{1,9},{3,11},{4,12},{6,14},{5,13},{7,15},{8,0},{10,2}... | collective-permute-start | bytes 884744 | tf_op jit(solution)/shard_map/ppermute | solution.py:34
  29.5 0.8 collective-permute-start.10
  30.3 0.7 collective-permute-start.9
  31.0 2.9 %collective-permute-done.11.refs_3_ = bf16[128,1152]{1,0:T(8,128)(2,1)S(1)} collective-permute-done((bf16[128,1152]{1,0:T(8,128)(2,1)S(1)}, bf16[128,1152]{1,0:T(8,128)(2,1)S(1)}, u32[]{:S(2)}, u32[]{:S(2)}) %collective-permute-start.11) | collective-permute-done | bytes 294944 | tf_op jit(solution)/shard_map/ppermute | solution.py:34
  34.0 3.6 %collective-permute-done.10.refs_2_ = bf16[128,1152]{1,0:T(8,128)(2,1)S(1)} collective-permute-done((bf16[128,1152]{1,0:T(8,128)(2,1)S(1)}, bf16[128,1152]{1,0:T(8,128)(2,1)S(1)}, u32[]{:S(2)}, u32[]{:S(2)}) %collective-permute-start.10) | collective-permute-done | bytes 294944 | tf_op jit(solution)/shard_map/ppermute | solution.py:34
  37.6 0.1 shard_map.91.refs_8_
  37.6 2.6 %collective-permute-start.13 = (bf16[512,1152]{1,0:T(8,128)(2,1)S(1)}, bf16[512,1152]{1,0:T(8,128)(2,1)S(1)}, u32[]{:S(2)}, u32[]{:S(2)}) collective-permute-start(bf16[512,1152]{1,0:T(8,128)(2,1)S(1)} %shard_map.91.refs_8_), channel_id=1, source_target_pairs={{0,3},{2,0},{1,2},{3,1},{4,7},{6,4},{5,6},{7,5},{8,11},{10,8},{9,1... | collective-permute-start | bytes 3538952 | tf_op jit(solution)/shard_map/ppermute | solution.py:34
  40.2 5.6 %collective-permute-start.2 = (bf16[128,1152]{1,0:T(8,128)(2,1)S(1)}, bf16[128,1152]{1,0:T(8,128)(2,1)S(1)}, u32[]{:S(2)}, u32[]{:S(2)}) collective-permute-start(bf16[128,1152]{1,0:T(8,128)(2,1)S(1)} %get-tuple-element.31.refs_0_), channel_id=1, source_target_pairs={{0,112},{2,114},{1,113},{3,115},{4,116},{6,118},{5,117},{7,119},{8... | collective-permute-start | bytes 884744 | tf_op jit(solution)/shard_map/ppermute | solution.py:34
  45.8 3.7 %collective-permute-done.2.refs_2_ = bf16[128,1152]{1,0:T(8,128)(2,1)S(1)} collective-permute-done((bf16[128,1152]{1,0:T(8,128)(2,1)S(1)}, bf16[128,1152]{1,0:T(8,128)(2,1)S(1)}, u32[]{:S(2)}, u32[]{:S(2)}) %collective-permute-start.2) | collective-permute-done | bytes 294944 | tf_op jit(solution)/shard_map/ppermute | solution.py:34
  49.4 3.1 %collective-permute-start.4 = (bf16[128,1152]{1,0:T(8,128)(2,1)S(1)}, bf16[128,1152]{1,0:T(8,128)(2,1)}, u32[]{:S(2)}, u32[]{:S(2)}) collective-permute-start(bf16[128,1152]{1,0:T(8,128)(2,1)S(1)} %collective-permute-done.2.refs_2_), channel_id=1, source_target_pairs={{0,112},{2,114},{1,113},{3,115},{4,116},{6,118},{5,117},{7,119},{8... | collective-permute-start | bytes 884744 | tf_op jit(solution)/shard_map/ppermute | solution.py:34
  52.6 0.7 copy-done.4
  53.3 0.7 copy-done.6
  54.0 2.3 %collective-permute-done.4.refs_4_ = bf16[128,1152]{1,0:T(8,128)(2,1)} collective-permute-done((bf16[128,1152]{1,0:T(8,128)(2,1)S(1)}, bf16[128,1152]{1,0:T(8,128)(2,1)}, u32[]{:S(2)}, u32[]{:S(2)}) %collective-permute-start.4) | collective-permute-done | bytes 294944 | tf_op jit(solution)/shard_map/ppermute | solution.py:34
  56.3 3.5 %collective-permute-start.6 = (bf16[128,1152]{1,0:T(8,128)(2,1)}, bf16[128,1152]{1,0:T(8,128)(2,1)S(1)}, u32[]{:S(2)}, u32[]{:S(2)}) collective-permute-start(bf16[128,1152]{1,0:T(8,128)(2,1)} %collective-permute-done.4.refs_4_), channel_id=1, source_target_pairs={{0,112},{2,114},{1,113},{3,115},{4,116},{6,118},{5,117},{7,119},{8... | collective-permute-start | bytes 884744 | tf_op jit(solution)/shard_map/ppermute | solution.py:34
  59.8 0.6 collective-permute-done.3.refs_3_
  60.5 3.1 %collective-permute-start.15 = (bf16[256,1152]{1,0:T(8,128)(2,1)S(1)}, bf16[256,1152]{1,0:T(8,128)(2,1)S(1)}, u32[]{:S(2)}, u32[]{:S(2)}) collective-permute-start(bf16[256,1152]{1,0:T(8,128)(2,1)S(1)} %slice.9), channel_id=1, source_target_pairs={{0,3},{2,0},{1,2},{3,1},{4,7},{6,4},{5,6},{7,5},{8,11},{10,8},{9,1... | collective-permute-start | bytes 1769480 | tf_op jit(solution)/shard_map/ppermute | solution.py:34
  63.7 1.1 slice.8
  64.8 0.1 collective-permute-start.14
  64.9 3.5 %collective-permute-done.5.refs_5_ = bf16[128,1152]{1,0:T(8,128)(2,1)S(1)} collective-permute-done((bf16[128,1152]{1,0:T(8,128)(2,1)}, bf16[128,1152]{1,0:T(8,128)(2,1)S(1)}, u32[]{:S(2)}, u32[]{:S(2)}) %collective-permute-start.5) | collective-permute-done | bytes 294944 | tf_op jit(solution)/shard_map/ppermute | solution.py:34
  68.4 0.3 collective-permute-start.7
  68.8 5.9 %collective-permute-done.7.refs_7_ = bf16[128,1152]{1,0:T(8,128)(2,1)S(1)} collective-permute-done((bf16[128,1152]{1,0:T(8,128)(2,1)S(1)}, bf16[128,1152]{1,0:T(8,128)(2,1)S(1)}, u32[]{:S(2)}, u32[]{:S(2)}) %collective-permute-start.7) | collective-permute-done | bytes 294944 | tf_op jit(solution)/shard_map/ppermute | solution.py:34
  74.6 0.2 collective-permute-done.14.refs_11_
  74.8 12.6 %shard_map.92 = (f32[8,128]{1,0:T(8,128)S(1)}, bf16[256,576]{1,0:T(8,128)(2,1)S(1)}, bf16[256,576]{1,0:T(8,128)(2,1)S(1)}) custom-call(s32[6]{0:T(128)S(1)} %stack.27.pos_ref, f32[128,128]{1,0:T(8,128)S(1)} %get-tuple-element.23.chosen_ref, f32[128,128]{1,0:T(8,128)S(1)} %get-tuple-element.24.place_ref, bf16[128,1152]{1,0:T(8,128)(2,1)S(1)} %get-tuple-element.31.refs_0_, ...), custom_call_target="tpu_custom_call" | custom-call | flops 7247757312 | bytes 1048576 | tf_op jit(solution)/shard_map/pallas_call | solution.py:76
  87.5 11.1 %collective-permute-start.16 = (bf16[256,576]{1,0:T(8,128)(2,1)S(1)}, bf16[256,576]{1,0:T(8,128)(2,1)S(1)}, u32[]{:S(2)}, u32[]{:S(2)}) collective-permute-start(bf16[256,576]{1,0:T(8,128)(2,1)S(1)} %get-tuple-element.35), channel_id=1, source_target_pairs={{128,0},{130,2},{129,1},{131,3},{132,4},{134,6},{133,5},{135,7},{1... | collective-permute-start | bytes 884744 | tf_op jit(solution)/shard_map/ppermute | solution.py:34
  98.6 1.2 collective-permute-done.16.recv_ref
  99.8 1.4 %shard_map.93 = bf16[256,640]{1,0:T(8,128)(2,1)} custom-call(s32[6]{0:T(128)S(1)} %stack.27.pos_ref, bf16[256,576]{1,0:T(8,128)(2,1)S(1)} %get-tuple-element.34.keep_ref, bf16[256,576]{1,0:T(8,128)(2,1)S(1)} %collective-permute-done.16.recv_ref, f32[8,128]{1,0:T(8,128)S(1)} %get-tuple-element.36.loss_ref), custom_call_target="tpu_custom_call" | custom-call | flops 147456 | bytes 1048576 | tf_op jit(solution)/shard_map/pallas_call | solution.py:76
  101.2 4.2 %all-to-all-start = ((bf16[8,32,640]{2,1,0:T(8,128)(2,1)}), bf16[8,32,640]{2,1,0:T(8,128)(2,1)S(1)}, u32[]{:S(2)}, u32[]{:S(2)}) async-start(bf16[8,32,640]{2,1,0:T(8,128)(2,1)} %bitcast.11), calls=%async_computation | async-start | bytes 655360 | tf_op jit(solution)/shard_map/all_to_all | solution.py:430
  105.4 2.6 %collective-permute-start.17 = (f32[32,704]{1,0:T(8,128)S(1)}, f32[32,704]{1,0:T(8,128)S(1)}, u32[]{:S(2)}, u32[]{:S(2)}) collective-permute-start(f32[32,704]{1,0:T(8,128)S(1)} %copy-done.9), channel_id=1, source_target_pairs={{128,0},{130,2},{129,1},{131,3},{132,4},{134,6},{133,5},{135,7},{1... | collective-permute-start | bytes 270344 | tf_op jit(solution)/shard_map/ppermute | solution.py:34
  108.0 0.9 collective-permute-done.17.given_ref
  108.9 10.1 %all-to-all-done = bf16[8,32,640]{2,1,0:T(8,128)(2,1)S(1)} async-done(((bf16[8,32,640]{2,1,0:T(8,128)(2,1)}), bf16[8,32,640]{2,1,0:T(8,128)(2,1)S(1)}, u32[]{:S(2)}, u32[]{:S(2)}) %all-to-all-start) | async-done | bytes 327712 | tf_op jit(solution)/shard_map/all_to_all | solution.py:430
  119.1 0.8 shard_map.94
  119.9 0.6 collective-permute-start.18
  120.5 0.8 collective-permute-done.18.other_ref
  121.3 1.5 %shard_map.95 = (f32[1,128]{1,0:T(1,128)}, f32[128,576]{1,0:T(8,128)S(1)}) custom-call(s32[6]{0:T(128)S(1)} %stack.27.pos_ref, f32[32,576]{1,0:T(8,128)S(1)} %get-tuple-element.40.g_ref, f32[32,1152]{1,0:T(8,128)S(1)} %get-tuple-element.37.unit_ref, f32[32,704]{1,0:T(8,128)S(1)} %collective-permute-done.17.given_ref, f32[32,128]{1,0:T(8,128)S(1)} %get-tuple-element.39.n_ref, ...), custom_call_target="tpu_custom_call" | custom-call | flops 29491200 | bytes 1048576 | tf_op jit(solution)/shard_map/pallas_call | solution.py:76
  122.9 0.9 copy.9
  (29 shorter events, 0.1 us)
Async XLA Ops:
  0.7 1.1 copy-start
  1.8 0.7 copy-start.3
  2.5 11.1 %copy-start.1 = (bf16[1,576,1152]{2,1,0:T(8,128)(2,1)S(1)}, bf16[1,576,1152]{2,1,0:T(8,128)(2,1)}, u32[]{:S(2)}) copy-start(bf16[1,576,1152]{2,1,0:T(8,128)(2,1)} %param.12) | copy-start | bytes 3981316
  2.5 11.1 %copy-start.2 = (bf16[256,1152]{1,0:T(8,128)(2,1)S(1)}, bf16[256,1152]{1,0:T(8,128)(2,1)}, u32[]{:S(2)}) copy-start(bf16[256,1152]{1,0:T(8,128)(2,1)} %text_ref) | copy-start | bytes 1769476
  9.7 5.3 %copy-start.10 = (s32[2048]{0:T(1024)S(1)}, s32[2048]{0:T(1024)}, u32[]{:S(2)}) copy-start(s32[2048]{0:T(1024)} %param.13) | copy-start | bytes 24580
  9.7 9.5 %collective-permute-start = (bf16[128,1152]{1,0:T(8,128)(2,1)S(1)}, bf16[128,1152]{1,0:T(8,128)(2,1)S(1)}, u32[]{:S(2)}, u32[]{:S(2)}) collective-permute-start(bf16[128,1152]{1,0:T(8,128)(2,1)S(1)} %get-tuple-element.29), channel_id=1, source_target_pairs={{0,1},{2,3},{1,0},{3,2},{4,5},{6,7},{5,4},{7,6},{8,9},{10,11},{9,8... | collective-permute-start | bytes 884744 | tf_op jit(solution)/shard_map/ppermute | solution.py:34
  14.9 10.7 %collective-permute-start.8 = (bf16[128,1152]{1,0:T(8,128)(2,1)S(1)}, bf16[128,1152]{1,0:T(8,128)(2,1)S(1)}, u32[]{:S(2)}, u32[]{:S(2)}) collective-permute-start(bf16[128,1152]{1,0:T(8,128)(2,1)S(1)} %get-tuple-element.33), channel_id=1, source_target_pairs={{0,1},{2,3},{1,0},{3,2},{4,5},{6,7},{5,4},{7,6},{8,9},{10,11},{9,8... | collective-permute-start | bytes 884744 | tf_op jit(solution)/shard_map/ppermute | solution.py:34
  20.5 0.6 copy-start.8
  25.8 8.2 %collective-permute-start.11 = (bf16[128,1152]{1,0:T(8,128)(2,1)S(1)}, bf16[128,1152]{1,0:T(8,128)(2,1)S(1)}, u32[]{:S(2)}, u32[]{:S(2)}) collective-permute-start(bf16[128,1152]{1,0:T(8,128)(2,1)S(1)} %shard_map.90.refs_0_), channel_id=1, source_target_pairs={{0,8},{2,10},{1,9},{3,11},{4,12},{6,14},{5,13},{7,15},{8,0},{10,2}... | collective-permute-start | bytes 884744 | tf_op jit(solution)/shard_map/ppermute | solution.py:34
  29.5 8.0 %collective-permute-start.10 = (bf16[128,1152]{1,0:T(8,128)(2,1)S(1)}, bf16[128,1152]{1,0:T(8,128)(2,1)S(1)}, u32[]{:S(2)}, u32[]{:S(2)}) collective-permute-start(bf16[128,1152]{1,0:T(8,128)(2,1)S(1)} %shard_map.90.refs_0_), channel_id=1, source_target_pairs={{0,12},{2,14},{1,13},{3,15},{4,0},{6,2},{5,1},{7,3},{8,4},{10,6},{... | collective-permute-start | bytes 884744 | tf_op jit(solution)/shard_map/ppermute | solution.py:34
  30.3 7.2 %collective-permute-start.9 = (bf16[128,1152]{1,0:T(8,128)(2,1)S(1)}, bf16[128,1152]{1,0:T(8,128)(2,1)S(1)}, u32[]{:S(2)}, u32[]{:S(2)}) collective-permute-start(bf16[128,1152]{1,0:T(8,128)(2,1)S(1)} %shard_map.90.refs_0_), channel_id=1, source_target_pairs={{0,4},{2,6},{1,5},{3,7},{4,8},{6,10},{5,9},{7,11},{8,12},{10,14},{... | collective-permute-start | bytes 884744 | tf_op jit(solution)/shard_map/ppermute | solution.py:34
  37.6 22.8 %collective-permute-start.13 = (bf16[512,1152]{1,0:T(8,128)(2,1)S(1)}, bf16[512,1152]{1,0:T(8,128)(2,1)S(1)}, u32[]{:S(2)}, u32[]{:S(2)}) collective-permute-start(bf16[512,1152]{1,0:T(8,128)(2,1)S(1)} %shard_map.91.refs_8_), channel_id=1, source_target_pairs={{0,3},{2,0},{1,2},{3,1},{4,7},{6,4},{5,6},{7,5},{8,11},{10,8},{9,1... | collective-permute-start | bytes 3538952 | tf_op jit(solution)/shard_map/ppermute | solution.py:34
  40.2 23.5 %collective-permute-start.12 = (bf16[512,1152]{1,0:T(8,128)(2,1)S(1)}, bf16[512,1152]{1,0:T(8,128)(2,1)}, u32[]{:S(2)}, u32[]{:S(2)}) collective-permute-start(bf16[512,1152]{1,0:T(8,128)(2,1)S(1)} %shard_map.91.refs_8_), channel_id=1, source_target_pairs={{0,2},{2,1},{1,3},{3,0},{4,6},{6,5},{5,7},{7,4},{8,10},{10,9},{9,1... | collective-permute-start | bytes 3538952 | tf_op jit(solution)/shard_map/ppermute | solution.py:34
  40.2 9.2 %collective-permute-start.2 = (bf16[128,1152]{1,0:T(8,128)(2,1)S(1)}, bf16[128,1152]{1,0:T(8,128)(2,1)S(1)}, u32[]{:S(2)}, u32[]{:S(2)}) collective-permute-start(bf16[128,1152]{1,0:T(8,128)(2,1)S(1)} %get-tuple-element.31.refs_0_), channel_id=1, source_target_pairs={{0,112},{2,114},{1,113},{3,115},{4,116},{6,118},{5,117},{7,119},{8... | collective-permute-start | bytes 884744 | tf_op jit(solution)/shard_map/ppermute | solution.py:34
  45.8 7.5 %collective-permute-start.1 = (bf16[128,1152]{1,0:T(8,128)(2,1)S(1)}, bf16[128,1152]{1,0:T(8,128)(2,1)S(1)}, u32[]{:S(2)}, u32[]{:S(2)}) collective-permute-start(bf16[128,1152]{1,0:T(8,128)(2,1)S(1)} %get-tuple-element.31.refs_0_), channel_id=1, source_target_pairs={{0,16},{2,18},{1,17},{3,19},{4,20},{6,22},{5,21},{7,23},{8,24},{10... | collective-permute-start | bytes 884744 | tf_op jit(solution)/shard_map/ppermute | solution.py:34
  49.4 6.9 %collective-permute-start.4 = (bf16[128,1152]{1,0:T(8,128)(2,1)S(1)}, bf16[128,1152]{1,0:T(8,128)(2,1)}, u32[]{:S(2)}, u32[]{:S(2)}) collective-permute-start(bf16[128,1152]{1,0:T(8,128)(2,1)S(1)} %collective-permute-done.2.refs_2_), channel_id=1, source_target_pairs={{0,112},{2,114},{1,113},{3,115},{4,116},{6,118},{5,117},{7,119},{8... | collective-permute-start | bytes 884744 | tf_op jit(solution)/shard_map/ppermute | solution.py:34
  52.6 0.7 copy-start.4
  53.3 7.2 %collective-permute-start.3 = (bf16[128,1152]{1,0:T(8,128)(2,1)S(1)}, bf16[128,1152]{1,0:T(8,128)(2,1)}, u32[]{:S(2)}, u32[]{:S(2)}) collective-permute-start(bf16[128,1152]{1,0:T(8,128)(2,1)S(1)} %collective-permute-done.1.refs_1_), channel_id=1, source_target_pairs={{0,16},{2,18},{1,17},{3,19},{4,20},{6,22},{5,21},{7,23},{8,24},{10... | collective-permute-start | bytes 884744 | tf_op jit(solution)/shard_map/ppermute | solution.py:34
  53.3 0.7 copy-start.6
  56.3 8.6 %collective-permute-start.6 = (bf16[128,1152]{1,0:T(8,128)(2,1)}, bf16[128,1152]{1,0:T(8,128)(2,1)S(1)}, u32[]{:S(2)}, u32[]{:S(2)}) collective-permute-start(bf16[128,1152]{1,0:T(8,128)(2,1)} %collective-permute-done.4.refs_4_), channel_id=1, source_target_pairs={{0,112},{2,114},{1,113},{3,115},{4,116},{6,118},{5,117},{7,119},{8... | collective-permute-start | bytes 884744 | tf_op jit(solution)/shard_map/ppermute | solution.py:34
  60.5 7.9 %collective-permute-start.5 = (bf16[128,1152]{1,0:T(8,128)(2,1)}, bf16[128,1152]{1,0:T(8,128)(2,1)S(1)}, u32[]{:S(2)}, u32[]{:S(2)}) collective-permute-start(bf16[128,1152]{1,0:T(8,128)(2,1)} %collective-permute-done.3.refs_3_), channel_id=1, source_target_pairs={{0,16},{2,18},{1,17},{3,19},{4,20},{6,22},{5,21},{7,23},{8,24},{10... | collective-permute-start | bytes 884744 | tf_op jit(solution)/shard_map/ppermute | solution.py:34
  60.5 14.3 %copy-start.5 = (bf16[128,1152]{1,0:T(8,128)(2,1)S(1)}, bf16[128,1152]{1,0:T(8,128)(2,1)}, u32[]{:S(2)}) copy-start(bf16[128,1152]{1,0:T(8,128)(2,1)} %copy-done.4) | copy-start | bytes 884740
  60.5 14.3 %copy-start.7 = (bf16[128,1152]{1,0:T(8,128)(2,1)S(1)}, bf16[128,1152]{1,0:T(8,128)(2,1)}, u32[]{:S(2)}) copy-start(bf16[128,1152]{1,0:T(8,128)(2,1)} %copy-done.6) | copy-start | bytes 884740
  60.5 14.1 %collective-permute-start.15 = (bf16[256,1152]{1,0:T(8,128)(2,1)S(1)}, bf16[256,1152]{1,0:T(8,128)(2,1)S(1)}, u32[]{:S(2)}, u32[]{:S(2)}) collective-permute-start(bf16[256,1152]{1,0:T(8,128)(2,1)S(1)} %slice.9), channel_id=1, source_target_pairs={{0,3},{2,0},{1,2},{3,1},{4,7},{6,4},{5,6},{7,5},{8,11},{10,8},{9,1... | collective-permute-start | bytes 1769480 | tf_op jit(solution)/shard_map/ppermute | solution.py:34
  64.8 10.0 %collective-permute-start.14 = (bf16[256,1152]{1,0:T(8,128)(2,1)S(1)}, bf16[256,1152]{1,0:T(8,128)(2,1)S(1)}, u32[]{:S(2)}, u32[]{:S(2)}) collective-permute-start(bf16[256,1152]{1,0:T(8,128)(2,1)S(1)} %slice.8), channel_id=1, source_target_pairs={{0,2},{2,1},{1,3},{3,0},{4,6},{6,5},{5,7},{7,4},{8,10},{10,9},{9,1... | collective-permute-start | bytes 1769480 | tf_op jit(solution)/shard_map/ppermute | solution.py:34
  68.4 6.2 %collective-permute-start.7 = (bf16[128,1152]{1,0:T(8,128)(2,1)S(1)}, bf16[128,1152]{1,0:T(8,128)(2,1)S(1)}, u32[]{:S(2)}, u32[]{:S(2)}) collective-permute-start(bf16[128,1152]{1,0:T(8,128)(2,1)S(1)} %broadcast_select_fusion), channel_id=1, source_target_pairs={{0,16},{2,18},{1,17},{3,19},{4,20},{6,22},{5,21},{7,23},{8,24},{10... | collective-permute-start | bytes 884744 | tf_op jit(solution)/shard_map/ppermute | solution.py:34
  87.5 18.0 %copy-start.9 = (f32[32,704]{1,0:T(8,128)S(1)}, f32[32,704]{1,0:T(8,128)}, u32[]{:S(2)}) copy-start(f32[32,704]{1,0:T(8,128)} %copy-done.8) | copy-start | bytes 270340
  87.5 12.3 %collective-permute-start.16 = (bf16[256,576]{1,0:T(8,128)(2,1)S(1)}, bf16[256,576]{1,0:T(8,128)(2,1)S(1)}, u32[]{:S(2)}, u32[]{:S(2)}) collective-permute-start(bf16[256,576]{1,0:T(8,128)(2,1)S(1)} %get-tuple-element.35), channel_id=1, source_target_pairs={{128,0},{130,2},{129,1},{131,3},{132,4},{134,6},{133,5},{135,7},{1... | collective-permute-start | bytes 884744 | tf_op jit(solution)/shard_map/ppermute | solution.py:34
  101.2 17.9 %all-to-all-start = ((bf16[8,32,640]{2,1,0:T(8,128)(2,1)}), bf16[8,32,640]{2,1,0:T(8,128)(2,1)S(1)}, u32[]{:S(2)}, u32[]{:S(2)}) async-start(bf16[8,32,640]{2,1,0:T(8,128)(2,1)} %bitcast.11), calls=%async_computation | async-start | bytes 655360 | tf_op jit(solution)/shard_map/all_to_all | solution.py:430
  105.4 3.5 %collective-permute-start.17 = (f32[32,704]{1,0:T(8,128)S(1)}, f32[32,704]{1,0:T(8,128)S(1)}, u32[]{:S(2)}, u32[]{:S(2)}) collective-permute-start(f32[32,704]{1,0:T(8,128)S(1)} %copy-done.9), channel_id=1, source_target_pairs={{128,0},{130,2},{129,1},{131,3},{132,4},{134,6},{133,5},{135,7},{1... | collective-permute-start | bytes 270344 | tf_op jit(solution)/shard_map/ppermute | solution.py:34
  119.9 1.5 %collective-permute-start.18 = (f32[40,128]{1,0:T(8,128)S(1)}, f32[40,128]{1,0:T(8,128)S(1)}, u32[]{:S(2)}, u32[]{:S(2)}) collective-permute-start(f32[40,128]{1,0:T(8,128)S(1)} %get-tuple-element.41.own_ref), channel_id=1, source_target_pairs={{0,128},{2,130},{1,129},{3,131},{4,132},{6,134},{5,133},{7,135},{8... | collective-permute-start | bytes 61448 | tf_op jit(solution)/shard_map/ppermute | solution.py:34

commit v2 on v1

--- a/solution.py
+++ b/solution.py
@@ -53,18 +53,6 @@
 
 def swap_cores(v):
     return permute(v, lambda g, z, x, y: (1 - g, z, x, y))
-
-
-def to_reference(v):
-    return permute(v, lambda g, z, x, y: (0, z, x, y), (1,))
-
-
-def ring8(v):
-    back, ahead = [v], [v]
-    for _ in range(3):
-        back.append(over_z(back[-1], (1, 1)))
-        ahead.append(over_z(ahead[-1], (-1, -1)))
-    return back, ahead
 
 
 def shape(dims, dtype=jnp.float32):
@@ -109,7 +97,17 @@
     other_ref[...] = other.astype(jnp.bfloat16)
 
 
-def text_kernel(pos_ref, text_ref, head_ref, own_ref, other_ref, acc_ref):
+def text_kernel(
+    pos_ref, text_hbm, head_hbm, own_ref, other_ref, text_ref, head_ref, acc_ref, sems
+):
+    copies = [
+        pltpu.make_async_copy(text_hbm, text_ref, sems.at[0]),
+        pltpu.make_async_copy(head_hbm, head_ref, sems.at[1]),
+    ]
+    for c in copies:
+        c.start()
+    for c in copies:
+        c.wait()
     depth = head_ref.shape[0]
     m = pos_ref[0]
     text = text_ref[...]
@@ -119,13 +117,13 @@
 
 
 def mlp_kernel(
-    pos_ref, gain_ref, x_hbm, up_hbm, down_hbm, own_ref, other_ref,
-    x_ref, up_ref, down_ref, normed_ref, hidden_ref, acc_ref, sems,
+    pos_ref, gain_hbm, x_hbm, up_hbm, down_hbm, own_ref, other_ref,
+    gain_ref, x_ref, up_ref, down_ref, normed_ref, hidden_ref, acc_ref, sems,
 ):
     copies = [
         pltpu.make_async_copy(source, target, sems.at[k])
         for k, (source, target) in enumerate(
-            [(x_hbm, x_ref), (up_hbm, up_ref), (down_hbm, down_ref)]
+            [(x_hbm, x_ref), (up_hbm, up_ref), (down_hbm, down_ref), (gain_hbm, gain_ref)]
         )
     ]
     for c in copies:
@@ -135,6 +133,7 @@
     mean = jnp.mean(x, axis=1, keepdims=True)
     gap = x - mean
     var = jnp.mean(gap * gap, axis=1, keepdims=True)
+    copies[3].wait()
     normed_ref[...] = (gap * lax.rsqrt(var + EPS) * gain_ref[...]).astype(jnp.bfloat16)
     copies[1].wait()
     total, block = up_ref.shape[0], 512
@@ -154,32 +153,24 @@
             hidden_ref[...], down_ref[:, start : start + block], preferred_element_type=jnp.float32
         )
     split_rows(acc_ref, pos_ref[0], own_ref, other_ref)
-
-
-def image_mlp(pos, gain, x, up, down):
-    rows, width = x.shape
-    hidden = up.shape[0]
-    bf16 = jnp.bfloat16
+    rows = own_ref.shape[0]
+    x = x_ref[pl.ds(pl.multiple_of(pos_ref[0] * rows, rows), rows), :]
+    own_ref[...] = own_ref[...] + x.astype(jnp.float32)
+
+
+def from_hbm(kernel, pos, arrays, rows, width, scratch, flops):
     vmem, hbm = pl.BlockSpec(memory_space=pltpu.VMEM), pl.BlockSpec(memory_space=pl.ANY)
     return pl.pallas_call(
-        mlp_kernel,
-        in_specs=[pl.BlockSpec(memory_space=pltpu.SMEM), vmem, hbm, hbm, hbm],
+        kernel,
+        in_specs=[pl.BlockSpec(memory_space=pltpu.SMEM)] + [hbm] * len(arrays),
         out_specs=[vmem, vmem],
-        out_shape=[shape((rows // 2, width)), shape((rows // 2, width), bf16)],
-        scratch_shapes=[
-            pltpu.VMEM((rows, width), bf16),
-            pltpu.VMEM((hidden, width), bf16),
-            pltpu.VMEM((hidden, width), bf16),
-            pltpu.VMEM((rows, width), bf16),
-            pltpu.VMEM((rows, hidden), bf16),
-            pltpu.VMEM((rows, width), jnp.float32),
-            pltpu.SemaphoreType.DMA((3,)),
-        ],
+        out_shape=[shape((rows, width)), shape((rows, width), jnp.bfloat16)],
+        scratch_shapes=[pltpu.VMEM(a.shape, a.dtype) for a in arrays]
+        + scratch
+        + [pltpu.VMEM((2 * rows, width), jnp.float32), pltpu.SemaphoreType.DMA((len(arrays),))],
         compiler_params=pltpu.CompilerParams(vmem_limit_bytes=52 * 1024 * 1024),
-        cost_estimate=pl.CostEstimate(
-            flops=4 * rows * width * hidden, bytes_accessed=11 << 20, transcendentals=rows * hidden
-        ),
-    )(pos, gain, x, up, down)
+        cost_estimate=pl.CostEstimate(flops=flops, bytes_accessed=11 << 20, transcendentals=0),
+    )(pos, *arrays)
 
 
 def text_unit_kernel(own_ref, recv_ref, z_ref):
@@ -193,25 +184,22 @@
     return jnp.where(place_row == slot, 1.0, 0.0)
 
 
-def image_unit_kernel(
-    pos_ref, own_ref, recv_ref, x_ref, place_ref, z_ref, unit_ref, n_ref, give_ref
-):
-    rows = own_ref.shape[0]
-    x = x_ref[pl.ds(pl.multiple_of(pos_ref[0] * rows, rows), rows), :].astype(jnp.float32)
-    e = x + (own_ref[...] + recv_ref[...].astype(jnp.float32))
+def image_unit_kernel(own_ref, recv_ref, z_ref, unit_ref, n_ref):
+    e = own_ref[...] + recv_ref[...].astype(jnp.float32)
     n = jnp.sqrt(jnp.sum(e * e, axis=1, keepdims=True) + EPS)
     unit = e / n
     z_ref[...] = unit.astype(jnp.bfloat16)
+    unit_ref[...] = unit
+    n_ref[...] = jnp.broadcast_to(n, n_ref.shape)
+
+
+def sub_unit_kernel(pos_ref, unit_ref, n_ref, place_ref, unit_sub_ref, n_sub_ref):
     pick = own_pick(place_ref[pl.ds(pos_ref[1] * (NX * NY) + pos_ref[4], 1), :])
-    unit = jnp.dot(pick, unit, precision=EXACT, preferred_element_type=jnp.float32)
-    n_rows = jnp.broadcast_to(n, (rows, n_ref.shape[1]))
-    n_sub = jnp.dot(pick, n_rows, precision=EXACT, preferred_element_type=jnp.float32)
-    n_sub = jnp.where(n_sub > 0.0, n_sub, 1.0)
-    unit_ref[...] = unit
-    n_ref[...] = n_sub
-    cut = unit.shape[1] // 2
-    give_ref[:, :cut] = unit[:, :cut]
-    give_ref[:, cut:] = n_sub
+    unit_sub_ref[...] = jnp.dot(
+        pick, unit_ref[...], precision=EXACT, preferred_element_type=jnp.float32
+    )
+    n_sub = jnp.dot(pick, n_ref[...], precision=EXACT, preferred_element_type=jnp.float32)
+    n_sub_ref[...] = jnp.where(n_sub > 0.0, n_sub, 1.0)
 
 
 def join_kernel(*refs):
@@ -246,7 +234,7 @@
 
 
 def pair_kernel(pos_ref, chosen_ref, place_ref, *refs):
-    images, texts, (loss_ref, keep_ref, give_ref) = refs[:NZ], refs[NZ:-3], refs[-3:]
+    images, texts, load_ref = refs[:NZ], refs[NZ:-1], refs[-1]
     z, x, y, xy = pos_ref[1], pos_ref[2], pos_ref[3], pos_ref[4]
     planes = NX * NY
     block = 256
@@ -285,11 +273,10 @@
         slope = (sign * s * mask).astype(jnp.bfloat16)
         total = total + jnp.dot(slope, text, preferred_element_type=jnp.float32)
     total = total.astype(jnp.bfloat16)
-    cut = keep_ref.shape[1]
+    width = total.shape[1]
     for k, o in enumerate(ZOFF):
         rows = pl.ds(pl.multiple_of(image_row(z, o) * CAP, CAP), CAP)
-        give_ref[rows, :] = total[k * CAP : (k + 1) * CAP, :cut]
-        keep_ref[rows, :] = total[k * CAP : (k + 1) * CAP, cut:]
+        load_ref[rows, :width] = total[k * CAP : (k + 1) * CAP, :]
 
     for number in range(NZ // 2):
         img = jnp.concatenate([images[2 * number][...], images[2 * number + 1][...]], axis=0)
@@ -298,61 +285,61 @@
             total = total + tile_loss(ref[s : s + block, :], img, number == 0 and k == 0)
         total = jnp.sum(total, axis=0, keepdims=True)
         for k in range(2):
+            loss = total[:, k * ROWS : (k + 1) * ROWS]
+            parts = []
+            for _ in range(3):
+                part = loss.astype(jnp.bfloat16).astype(jnp.float32)
+                loss = loss - part
+                parts.append(part)
+            parts.append(jnp.zeros((CAP - 3, ROWS), jnp.float32))
+            beside = jnp.concatenate(parts, axis=0).astype(jnp.bfloat16)
             row = image_row(z, ZOFF[2 * number + k])
-            loss_ref[pl.ds(row, 1), :] = total[:, k * ROWS : (k + 1) * ROWS]
-
-
-def load_kernel(pos_ref, keep_ref, recv_ref, loss_ref, out_ref):
-    learner = pos_ref[5] == 1
-    loss = loss_ref[...]
-    parts = []
-    for _ in range(3):
-        part = loss.astype(jnp.bfloat16)
-        loss = loss - part.astype(jnp.float32)
-        parts.append(part.astype(jnp.float32))
-    side = ROWS // 2
-    for z in range(NZ):
-        rows = slice(z * CAP, (z + 1) * CAP)
-        halves = [p[z : z + 1, k * side : (k + 1) * side] for p in parts for k in range(2)]
-        beside = jnp.concatenate(halves + [jnp.zeros((CAP - 6, side), jnp.float32)], axis=0)
-        grad = jnp.where(learner, keep_ref[rows, :], recv_ref[rows, :])
-        out_ref[rows, :] = jnp.concatenate([grad, beside.astype(jnp.bfloat16)], axis=1)
-
-
-def finish_kernel(pos_ref, load_ref, unit_ref, given_ref, n_ref, g_ref, msg_ref):
-    learner = pos_ref[5] == 1
-    cut = g_ref.shape[1]
+            load_ref[pl.ds(pl.multiple_of(row * CAP, CAP), CAP), width:] = beside
+
+
+def finish_kernel(load_ref, unit_ref, n_ref, keep_ref, msg_ref):
+    width = unit_ref.shape[1]
+    cut = width // 2
     total = load_ref[:CAP, :].astype(jnp.float32)
     for z in range(1, NZ):
         total = total + load_ref[z * CAP : (z + 1) * CAP, :].astype(jnp.float32)
-    g = SCALE * total[:, :cut]
-    unit = jnp.where(learner, unit_ref[:, cut:], given_ref[:, :cut])
-    n = jnp.where(learner, n_ref[...], given_ref[:, cut:])
-    g_ref[...] = g
-    dots = jnp.sum(unit * g, axis=1, keepdims=True)
-    beside = total[:, cut:]
-    loss = jnp.concatenate(
-        [beside[k : k + 1] + beside[k + 2 : k + 3] + beside[k + 4 : k + 5] for k in range(2)], axis=1
-    )
-    msg_ref[:CAP, :] = jnp.broadcast_to(dots, (CAP, ROWS))
-    msg_ref[CAP:, :] = jnp.broadcast_to(loss, (8, ROWS))
-
-
-def spread_kernel(
-    pos_ref, g_ref, unit_ref, given_ref, n_ref, own_ref, other_ref, place_ref, learn_ref, out_ref
-):
+    g = SCALE * total[:, :width]
+    unit = unit_ref[...]
+    grad = (g - unit * jnp.sum(unit * g, axis=1, keepdims=True)) / n_ref[:, :1]
+    loss = total[0:1, width:] + total[1:2, width:] + total[2:3, width:]
+    line = jnp.concatenate([loss, jnp.zeros((1, cut - ROWS), jnp.float32)], axis=1)
+    keep_ref[:CAP, :] = grad[:, cut:]
+    keep_ref[CAP:, :] = jnp.broadcast_to(line, (8, cut))
+    msg_ref[:CAP, :] = grad[:, :cut]
+    msg_ref[CAP:, :] = jnp.broadcast_to(line, (8, cut))
+
+
+def spread_kernel(pos_ref, keep_ref, recv_ref, place_ref, learn_ref, out_hbm, out_ref, sem):
     learner = pos_ref[5] == 1
-    cut = g_ref.shape[1]
-    unit = jnp.where(learner, unit_ref[:, cut:], given_ref[:, :cut])
-    n = jnp.where(learner, n_ref[...], given_ref[:, cut:])[:, :1]
-    dots = (own_ref[:CAP, :] + other_ref[:CAP, :])[:, :1]
-    grad = (g_ref[...] - unit * dots) / n
+    half = jnp.where(learner, keep_ref[:CAP, :], recv_ref[:CAP, :])
     pick = own_pick(place_ref[pl.ds(pos_ref[1] * (NX * NY) + pos_ref[4], 1), :])
     out_ref[...] = lax.dot_general(
-        pick, grad, (((0,), (0,)), ((), ())), precision=EXACT, preferred_element_type=jnp.float32
-    )
-    own, other = own_ref[CAP : CAP + 1, :], other_ref[CAP : CAP + 1, :]
+        pick, half, (((0,), (0,)), ((), ())), precision=EXACT, preferred_element_type=jnp.float32
+    )
+    copy = pltpu.make_async_copy(out_ref, out_hbm, sem)
+    copy.start()
+    own, other = keep_ref[CAP : CAP + 1, :ROWS], recv_ref[CAP : CAP + 1, :ROWS]
     learn_ref[...] = jnp.where(learner, own - other, other - own)
+    copy.wait()
+
+
+def spread(pos, keep, recv, place_of):
+    vmem, hbm = pl.BlockSpec(memory_space=pltpu.VMEM), pl.BlockSpec(memory_space=pl.ANY)
+    cut = keep.shape[1]
+    return pl.pallas_call(
+        spread_kernel,
+        in_specs=[pl.BlockSpec(memory_space=pltpu.SMEM)] + [vmem] * 3,
+        out_specs=[vmem, hbm],
+        out_shape=[shape((1, ROWS)), shape((ROWS, cut))],
+        scratch_shapes=[pltpu.VMEM((ROWS, cut), jnp.float32), pltpu.SemaphoreType.DMA(())],
+        compiler_params=pltpu.CompilerParams(vmem_limit_bytes=56 * 1024 * 1024),
+        cost_estimate=pl.CostEstimate(flops=1 << 24, bytes_accessed=1 << 20, transcendentals=0),
+    )(pos, keep, recv, place_of)
 
 
 def shards(image_features, text_features, norm_gain, up_weight, down_weight, text_head, sub_index):
@@ -370,78 +357,80 @@
     pos = jnp.stack([p.astype(jnp.int32) for p in pos])
     cells = rows * width
 
-    own_img, other_img = image_mlp(pos, norm_gain, image_features, up_weight[0].T, down_weight[0])
+    own_text, other_text = from_hbm(
+        text_kernel, pos, [text_features, text_head[0]], rows, width, [], 2 * cells * width
+    )
+    recv_text = over_mp(other_text)
+    features, own_text = lax.optimization_barrier((image_features, own_text))
+    hidden = up_weight.shape[2]
+    own_img, other_img = from_hbm(
+        mlp_kernel,
+        pos,
+        [norm_gain, features, up_weight[0].T, down_weight[0]],
+        rows,
+        width,
+        [pltpu.VMEM((2 * rows, width), bf16), pltpu.VMEM((2 * rows, hidden), bf16)],
+        8 * cells * hidden,
+    )
     recv_img = over_mp(other_img)
-    features, own_img = lax.optimization_barrier((text_features, own_img))
-    own_text, other_text = call(
-        text_kernel,
-        [pos],
-        [features, text_head[0]],
-        [shape((rows, width)), shape((rows, width), bf16)],
-        2 * cells * width,
-        scratch=[pltpu.VMEM((2 * rows, width), jnp.float32)],
-    )
-    recv_text = over_mp(other_text)
     chosen, place_of = call(
         index_kernel, [], [sub_index.reshape(1, -1)], [shape((blocks, rows))] * 2, 100 << 20
     )
-    z_img, unit_sub, n_sub, give = call(
+    z_img, unit, n_img = call(
         image_unit_kernel,
-        [pos],
-        [own_img, recv_img, image_features, place_of],
-        [shape((rows, width), bf16), shape((CAP, width)), shape((CAP, rows)), shape((CAP, cut + rows))],
-        400 * cells,
+        [],
+        [own_img, recv_img],
+        [shape((rows, width), bf16), shape((rows, width)), shape((rows, rows))],
+        20 * cells,
     )
     own_text, z_img = lax.optimization_barrier((own_text, z_img))
     (z_txt,) = call(
         text_unit_kernel, [], [own_text, recv_text], [shape((rows, width), bf16)], 20 * cells
     )
     line = [z_txt] + [over_plane(z_txt, shift, 0) for shift in (1, -1, 2)]
+    back, ahead = [z_img], [z_img]
+
+    def z_step():
+        back.append(over_z(back[-1], (1, 1)))
+        ahead.append(over_z(ahead[-1], (-1, -1)))
+
+    z_step()
+    line[0], back[1], ahead[1] = lax.optimization_barrier((line[0], back[1], ahead[1]))
     (joined,) = call(join_kernel, [], line, [shape((4 * rows, width), bf16)], cells)
-    back, ahead = over_plane(joined, 1, 1), over_plane(joined, -1, 1)
-    far_top = over_plane(back[: 2 * rows], 1, 1)
-    far_low = over_plane(ahead[2 * rows :], -1, 1)
-    texts = [joined, back, ahead, far_top, far_low]
-
-    from_back, from_ahead = ring8(z_img)
-    last = jnp.where(g_idx == 0, from_back[3], from_ahead[3])
-    images = [z_img, from_back[1], from_ahead[1], from_back[2], from_ahead[2]]
-    images += [from_back[3], from_ahead[3], over_z(last, (1, -1))]
-
-    given = to_reference(give)
-
-    n_text, n_img = NX * NY * rows, NZ * rows
-    loss_part, g_keep, g_give = call(
+    z_step()
+    text_back, text_ahead = over_plane(joined, 1, 1), over_plane(joined, -1, 1)
+    z_step()
+    text_back, text_ahead, back[3], ahead[3] = lax.optimization_barrier(
+        (text_back, text_ahead, back[3], ahead[3])
+    )
+    last = over_z(jnp.where(g_idx == 0, back[3], ahead[3]), (1, -1))
+    far_top = over_plane(text_back[: 2 * rows], 1, 1)
+    far_low = over_plane(text_ahead[2 * rows :], -1, 1)
+    texts = [joined, text_back, text_ahead, far_top, far_low]
+    images = [z_img, back[1], ahead[1], back[2], ahead[2], back[3], ahead[3], last]
+
+    n_pairs, n_text = (NZ * rows, NX * NY * rows)
+    (load,) = call(
         pair_kernel,
         [pos],
         [chosen, place_of] + images + texts,
-        [shape((NZ, rows))] + [shape((NZ * CAP, cut), bf16)] * 2,
-        (2 * n_img + 4 * NZ * CAP) * width * n_text,
+        [shape((NZ * CAP, width + rows), bf16)],
+        (2 * n_pairs + 4 * NZ * CAP) * width * n_text,
         mib=16,
-        transcendentals=(n_img + NZ * CAP) * n_text,
-    )
-    (load,) = call(
-        load_kernel,
+        transcendentals=(n_pairs + NZ * CAP) * n_text,
+    )
+    load = lax.all_to_all(load, "z", 0, 0, tiled=True)
+    unit_sub, n_sub = call(
+        sub_unit_kernel,
         [pos],
-        [g_keep, to_reference(g_give), loss_part],
-        [shape((NZ * CAP, cut + rows // 2), bf16)],
-        cells,
-    )
-    load = lax.all_to_all(load, "z", 0, 0, tiled=True)
-    g_sum, msg = call(
-        finish_kernel,
-        [pos],
-        [load, unit_sub, given, n_sub],
-        [shape((CAP, cut)), shape((CAP + 8, rows))],
-        10 * cells,
-    )
-    learn, image_grad = call(
-        spread_kernel,
-        [pos],
-        [g_sum, unit_sub, given, n_sub, msg, swap_cores(msg), place_of],
-        [shape((1, rows)), shape((rows, cut))],
-        200 * cells,
-    )
+        [unit, n_img, place_of],
+        [shape((CAP, width)), shape((CAP, rows))],
+        400 * cells,
+    )
+    keep, msg = call(
+        finish_kernel, [], [load, unit_sub, n_sub], [shape((CAP + 8, cut))] * 2, 10 * cells
+    )
+    learn, image_grad = spread(pos, keep, swap_cores(msg), place_of)
     return (learn.reshape(rows), image_grad)
 
 

time: 124 us -> 123 us (level)
  waiting for transfers between devices: 44 us -> 41.4 us
  Pallas kernels: 26.9 us -> 28.4 us
    pallas_call x1 -> x3, Pallas kernels: 7.24 us -> 12.8 us  [the longest x2 10.1 us: from_hbm(): pl.pallas_call(kernel, in_specs=[pl.BlockSpec(memory_space=pltpu.SMEM)] +...]
    ppermute x19 -> x17, waiting for transfers between devices: 33.9 us -> 28.7 us  [permute(): return lax.ppermute(v, AXES, perm)]
    pallas_call x9 -> x7, Pallas kernels: 19.7 us -> 15.6 us  [call(): pl.pallas_call(kernel, in_specs=[pl.BlockSpec(memory_space=pltpu.SMEM)] *...]
    all_to_all x1, waiting for transfers between devices: 10.1 us -> 12.7 us  [shards(): load = lax.all_to_all(load, 'z', 0, 0, tiled=True)]
    ppermute x19 -> x17, starting transfers between devices: 41.8 us -> 40.6 us  [permute(): return lax.ppermute(v, AXES, perm)]
    unnamed x23 -> x35, local copies, waits for them, and re-layouts: 4.7 us -> 4.32 us
  transfers between devices with their start and end apart: 20 -> 18, of which waited for: 14 -> 10; matrix products, arithmetic and copies ran while one was open for 1% -> 0% of each run, Pallas kernels for 2% -> 1%
where the time goes in v2:
time: 123 us; the launch traced here: 122 us
  starting transfers between devices  46 us (37%)
  waiting for transfers between devices  41.4 us (34%)
  Pallas kernels  28.4 us (23%)
  local copies, waits for them, and re-layouts  5.56 us (5%)
    ppermute x17, starting transfers between devices, permute(): return lax.ppermute(v, AXES, perm)  40.6 us
    ppermute x17, waiting for transfers between devices, permute(): return lax.ppermute(v, AXES, perm)  28.7 us
    pallas_call x7, Pallas kernels, call(): pl.pallas_call(kernel, in_specs=[pl.BlockSpec(memory_space=pltpu.SMEM)] *...  15.6 us
    all_to_all x1, waiting for transfers between devices, shards(): load = lax.all_to_all(load, 'z', 0, 0, tiled=True)  12.7 us
    pallas_call x2, Pallas kernels, from_hbm(): pl.pallas_call(kernel, in_specs=[pl.BlockSpec(memory_space=pltpu.SMEM)] +...  10.1 us
    all_to_all x1, starting transfers between devices, shards(): load = lax.all_to_all(load, 'z', 0, 0, tiled=True)  5.43 us
    unnamed x35, local copies, waits for them, and re-layouts  4.32 us
    pallas_call x1, Pallas kernels, spread(): pl.pallas_call(spread_kernel, in_specs=[pl.BlockSpec(memory_space=pltpu.S...  2.69 us
  transfers between devices with their start and end apart: 18, of which 10 were waited for; matrix products, arithmetic and copies ran while one was open for 0% of the time, Pallas kernels for 1%

profile of v2, /device:TPU:1, one launch (start us, length us, event | category | flops | bytes accessed | tf_op | source)
XLA Modules:
  0.0 122.3 jit_solution(12358491767228487249)
XLA Ops:
  0.7 0.1 stack.27.pos_ref
  0.7 1.1 copy-done.1
  1.9 2.8 %shard_map.87 = (f32[128,1152]{1,0:T(8,128)S(1)}, bf16[128,1152]{1,0:T(8,128)(2,1)S(1)}) custom-call(s32[6]{0:T(128)S(1)} %stack.27.pos_ref, bf16[256,1152]{1,0:T(8,128)(2,1)S(1)} %copy-done.1, bf16[576,1152]{1,0:T(8,128)(2,1)} %bitcast.19), custom_call_target="tpu_custom_call" | custom-call | flops 339738624 | bytes 11534336 | tf_op jit(solution)/shard_map/pallas_call | solution.py:163
  4.7 7.3 %shard_map.88 = (f32[128,1152]{1,0:T(8,128)S(1)}, bf16[128,1152]{1,0:T(8,128)(2,1)S(1)}) custom-call(s32[6]{0:T(128)S(1)} %stack.27.pos_ref, f32[1,1152]{1,0:T(1,128)S(1)} %copy-done.8, bf16[256,1152]{1,0:T(8,128)(2,1)S(1)} %copy-done, bf16[2152,1152]{1,0:T(8,128)(2,1)} %bitcast.17, bf16[2152,1152]{1,0:T(8,128)(2,1)} %bitcast.18), custom_call_target="tpu_custom_call" | custom-call | flops 2538602496 | bytes 11534336 | tf_op jit(solution)/shard_map/pallas_call | solution.py:163
  12.0 3.8 %collective-permute-start = (bf16[128,1152]{1,0:T(8,128)(2,1)S(1)}, bf16[128,1152]{1,0:T(8,128)(2,1)S(1)}, u32[]{:S(2)}, u32[]{:S(2)}) collective-permute-start(bf16[128,1152]{1,0:T(8,128)(2,1)S(1)} %get-tuple-element.34), channel_id=1, source_target_pairs={{0,1},{2,3},{1,0},{3,2},{4,5},{6,7},{5,4},{7,6},{8,9},{10,11},{9,8... | collective-permute-start | bytes 884744 | tf_op jit(solution)/shard_map/ppermute | solution.py:34
  15.8 0.1 collective-permute-start.1
  15.9 5.6 %collective-permute-done.recv_ref = bf16[128,1152]{1,0:T(8,128)(2,1)S(1)} collective-permute-done((bf16[128,1152]{1,0:T(8,128)(2,1)S(1)}, bf16[128,1152]{1,0:T(8,128)(2,1)S(1)}, u32[]{:S(2)}, u32[]{:S(2)}) %collective-permute-start) | collective-permute-done | bytes 294944 | tf_op jit(solution)/shard_map/ppermute | solution.py:34
  21.5 0.2 shard_map.89
  21.7 0.0 copy-start.9
  21.7 6.4 %collective-permute-start.3 = (bf16[128,1152]{1,0:T(8,128)(2,1)S(1)}, bf16[128,1152]{1,0:T(8,128)(2,1)S(1)}, u32[]{:S(2)}, u32[]{:S(2)}) collective-permute-start(bf16[128,1152]{1,0:T(8,128)(2,1)S(1)} %get-tuple-element.36.refs_0_), channel_id=1, source_target_pairs={{0,112},{2,114},{1,113},{3,115},{4,116},{6,118},{5,117},{7,119},{8... | collective-permute-start | bytes 884744 | tf_op jit(solution)/shard_map/ppermute | solution.py:34
  28.2 0.0 collective-permute-start.2
  28.2 0.0 collective-permute-done.1.recv_ref
  28.2 0.2 shard_map.90.refs_0_
  28.4 3.5 %collective-permute-start.8 = (bf16[128,1152]{1,0:T(8,128)(2,1)S(1)}, bf16[128,1152]{1,0:T(8,128)(2,1)S(1)}, u32[]{:S(2)}, u32[]{:S(2)}) collective-permute-start(bf16[128,1152]{1,0:T(8,128)(2,1)S(1)} %shard_map.90.refs_0_), channel_id=1, source_target_pairs={{0,8},{2,10},{1,9},{3,11},{4,12},{6,14},{5,13},{7,15},{8,0},{10,2}... | collective-permute-start | bytes 884744 | tf_op jit(solution)/shard_map/ppermute | solution.py:34
  31.8 0.8 collective-permute-start.7
  32.6 0.7 collective-permute-start.6
  33.3 0.0 collective-permute-done.3.refs_2_
  33.3 1.7 %collective-permute-done.2.refs_1_ = bf16[128,1152]{1,0:T(8,128)(2,1)S(1)} collective-permute-done((bf16[128,1152]{1,0:T(8,128)(2,1)S(1)}, bf16[128,1152]{1,0:T(8,128)(2,1)S(1)}, u32[]{:S(2)}, u32[]{:S(2)}) %collective-permute-start.2) | collective-permute-done | bytes 294944 | tf_op jit(solution)/shard_map/ppermute | solution.py:34
  35.0 1.3 %collective-permute-done.8.refs_3_ = bf16[128,1152]{1,0:T(8,128)(2,1)S(1)} collective-permute-done((bf16[128,1152]{1,0:T(8,128)(2,1)S(1)}, bf16[128,1152]{1,0:T(8,128)(2,1)S(1)}, u32[]{:S(2)}, u32[]{:S(2)}) %collective-permute-start.8) | collective-permute-done | bytes 294944 | tf_op jit(solution)/shard_map/ppermute | solution.py:34
  36.2 3.6 %collective-permute-done.7.refs_2_ = bf16[128,1152]{1,0:T(8,128)(2,1)S(1)} collective-permute-done((bf16[128,1152]{1,0:T(8,128)(2,1)S(1)}, bf16[128,1152]{1,0:T(8,128)(2,1)S(1)}, u32[]{:S(2)}, u32[]{:S(2)}) %collective-permute-start.7) | collective-permute-done | bytes 294944 | tf_op jit(solution)/shard_map/ppermute | solution.py:34
  39.8 0.0 collective-permute-done.6.refs_1_
  39.8 0.1 shard_map.91.refs_8_
  39.9 2.6 %collective-permute-start.10 = (bf16[512,1152]{1,0:T(8,128)(2,1)S(1)}, bf16[512,1152]{1,0:T(8,128)(2,1)S(1)}, u32[]{:S(2)}, u32[]{:S(2)}) collective-permute-start(bf16[512,1152]{1,0:T(8,128)(2,1)S(1)} %shard_map.91.refs_8_), channel_id=1, source_target_pairs={{0,3},{2,0},{1,2},{3,1},{4,7},{6,4},{5,6},{7,5},{8,11},{10,8},{9,1... | collective-permute-start | bytes 3538952 | tf_op jit(solution)/shard_map/ppermute | solution.py:34
  42.5 1.6 %collective-permute-start.4 = (bf16[128,1152]{1,0:T(8,128)(2,1)S(1)}, bf16[128,1152]{1,0:T(8,128)(2,1)}, u32[]{:S(2)}, u32[]{:S(2)}) collective-permute-start(bf16[128,1152]{1,0:T(8,128)(2,1)S(1)} %collective-permute-done.2.refs_1_), channel_id=1, source_target_pairs={{0,16},{2,18},{1,17},{3,19},{4,20},{6,22},{5,21},{7,23},{8,24},{10... | collective-permute-start | bytes 884744 | tf_op jit(solution)/shard_map/ppermute | solution.py:34
  44.1 3.9 %collective-permute-start.5 = (bf16[128,1152]{1,0:T(8,128)(2,1)S(1)}, bf16[128,1152]{1,0:T(8,128)(2,1)}, u32[]{:S(2)}, u32[]{:S(2)}) collective-permute-start(bf16[128,1152]{1,0:T(8,128)(2,1)S(1)} %collective-permute-done.3.refs_2_), channel_id=1, source_target_pairs={{0,112},{2,114},{1,113},{3,115},{4,116},{6,118},{5,117},{7,119},{8... | collective-permute-start | bytes 884744 | tf_op jit(solution)/shard_map/ppermute | solution.py:34
  48.1 4.5 %collective-permute-done.4.refs_3_ = bf16[128,1152]{1,0:T(8,128)(2,1)} collective-permute-done((bf16[128,1152]{1,0:T(8,128)(2,1)S(1)}, bf16[128,1152]{1,0:T(8,128)(2,1)}, u32[]{:S(2)}, u32[]{:S(2)}) %collective-permute-start.4) | collective-permute-done | bytes 294944 | tf_op jit(solution)/shard_map/ppermute | solution.py:34
  52.6 0.0 collective-permute-done.5.refs_4_
  52.6 2.7 %collective-permute-start.12 = (bf16[128,1152]{1,0:T(8,128)(2,1)}, bf16[128,1152]{1,0:T(8,128)(2,1)S(1)}, u32[]{:S(2)}, u32[]{:S(2)}) collective-permute-start(bf16[128,1152]{1,0:T(8,128)(2,1)} %collective-permute-done.5.refs_4_), channel_id=1, source_target_pairs={{0,112},{2,114},{1,113},{3,115},{4,116},{6,118},{5,117},{7,119},{8... | collective-permute-start | bytes 884744 | tf_op jit(solution)/shard_map/ppermute | solution.py:34
  55.2 4.7 %collective-permute-done.11.refs_5_ = bf16[128,1152]{1,0:T(8,128)(2,1)S(1)} collective-permute-done((bf16[128,1152]{1,0:T(8,128)(2,1)}, bf16[128,1152]{1,0:T(8,128)(2,1)S(1)}, u32[]{:S(2)}, u32[]{:S(2)}) %collective-permute-start.11) | collective-permute-done | bytes 294944 | tf_op jit(solution)/shard_map/ppermute | solution.py:34
  60.0 1.1 slice.6
  61.1 0.0 copy-start.15
  61.1 0.0 copy-start.10
  61.2 3.3 %collective-permute-start.15 = (bf16[256,1152]{1,0:T(8,128)(2,1)S(1)}, bf16[256,1152]{1,0:T(8,128)(2,1)S(1)}, u32[]{:S(2)}, u32[]{:S(2)}) collective-permute-start(bf16[256,1152]{1,0:T(8,128)(2,1)S(1)} %slice.7), channel_id=1, source_target_pairs={{0,3},{2,0},{1,2},{3,1},{4,7},{6,4},{5,6},{7,5},{8,11},{10,8},{9,1... | collective-permute-start | bytes 1769480 | tf_op jit(solution)/shard_map/ppermute | solution.py:34
  64.5 3.3 %collective-permute-start.13 = (bf16[128,1152]{1,0:T(8,128)(2,1)S(1)}, bf16[128,1152]{1,0:T(8,128)(2,1)S(1)}, u32[]{:S(2)}, u32[]{:S(2)}) collective-permute-start(bf16[128,1152]{1,0:T(8,128)(2,1)S(1)} %broadcast_select_fusion), channel_id=1, source_target_pairs={{0,16},{2,18},{1,17},{3,19},{4,20},{6,22},{5,21},{7,23},{8,24},{10... | collective-permute-start | bytes 884744 | tf_op jit(solution)/shard_map/ppermute | solution.py:34
  67.8 0.5 shard_map.86
  68.3 3.2 %collective-permute-done.13.refs_7_ = bf16[128,1152]{1,0:T(8,128)(2,1)S(1)} collective-permute-done((bf16[128,1152]{1,0:T(8,128)(2,1)S(1)}, bf16[128,1152]{1,0:T(8,128)(2,1)S(1)}, u32[]{:S(2)}, u32[]{:S(2)}) %collective-permute-start.13) | collective-permute-done | bytes 294944 | tf_op jit(solution)/shard_map/ppermute | solution.py:34
  71.5 3.2 %collective-permute-done.14.refs_11_ = bf16[256,1152]{1,0:T(8,128)(2,1)S(1)} collective-permute-done((bf16[256,1152]{1,0:T(8,128)(2,1)S(1)}, bf16[256,1152]{1,0:T(8,128)(2,1)S(1)}, u32[]{:S(2)}, u32[]{:S(2)}) %collective-permute-start.14) | collective-permute-done | bytes 589856 | tf_op jit(solution)/shard_map/ppermute | solution.py:34
  74.7 13.5 %shard_map.92 = bf16[256,1280]{1,0:T(8,128)(2,1)} custom-call(s32[6]{0:T(128)S(1)} %stack.27.pos_ref, f32[128,128]{1,0:T(8,128)S(1)} %get-tuple-element.28.chosen_ref, f32[128,128]{1,0:T(8,128)S(1)} %get-tuple-element.29.place_ref, bf16[128,1152]{1,0:T(8,128)(2,1)S(1)} %copy-done.10, bf16[128,1152]{1,0:T(8,128)(2,1)S(1)} %copy-done.14, ...), custom_call_target="tpu_custom_call" | custom-call | flops 7247757312 | bytes 1048576 | tf_op jit(solution)/shard_map/pallas_call | solution.py:64
  88.2 5.4 %all-to-all-start = ((bf16[8,32,1280]{2,1,0:T(8,128)(2,1)}), bf16[8,32,1280]{2,1,0:T(8,128)(2,1)S(1)}, u32[]{:S(2)}, u32[]{:S(2)}) async-start(bf16[8,32,1280]{2,1,0:T(8,128)(2,1)} %bitcast.11), calls=%async_computation | async-start | bytes 1310720 | tf_op jit(solution)/shard_map/all_to_all | solution.py:422
  93.7 1.0 shard_map.93
  94.7 12.7 %all-to-all-done = bf16[8,32,1280]{2,1,0:T(8,128)(2,1)S(1)} async-done(((bf16[8,32,1280]{2,1,0:T(8,128)(2,1)}), bf16[8,32,1280]{2,1,0:T(8,128)(2,1)S(1)}, u32[]{:S(2)}, u32[]{:S(2)}) %all-to-all-start) | async-done | bytes 655392 | tf_op jit(solution)/shard_map/all_to_all | solution.py:422
  107.4 0.2 shard_map.94
  107.7 0.6 copy-done.4
  108.3 7.9 %collective-permute-start.16 = (f32[40,576]{1,0:T(8,128)S(1)}, f32[40,576]{1,0:T(8,128)S(1)}, u32[]{:S(2)}, u32[]{:S(2)}) collective-permute-start(f32[40,576]{1,0:T(8,128)S(1)} %get-tuple-element.51), channel_id=1, source_target_pairs={{0,128},{2,130},{1,129},{3,131},{4,132},{6,134},{5,133},{7,135},{8... | collective-permute-start | bytes 276488 | tf_op jit(solution)/shard_map/ppermute | solution.py:34
  116.2 0.9 collective-permute-done.16.recv_ref
  117.2 0.6 copy-done.16
  117.8 2.7 %shard_map.95 = (f32[1,128]{1,0:T(1,128)}, f32[128,576]{1,0:T(8,128)}) custom-call(s32[6]{0:T(128)} %copy-done.7, f32[40,576]{1,0:T(8,128)} %copy-done.4, f32[40,576]{1,0:T(8,128)} %copy-done.16, f32[128,128]{1,0:T(8,128)} %copy-done.2), custom_call_target="tpu_custom_call" | custom-call | flops 16777216 | bytes 1048576 | tf_op jit(solution)/shard_map/pallas_call | solution.py:334
  120.5 1.8 %copy.9 = f32[128,576]{0,1:T(8,128)} copy(f32[128,576]{1,0:T(8,128)} %get-tuple-element.55) | data formatting | bytes 589824
  (37 shorter events, 0.2 us)
Async XLA Ops:
  0.6 4.0 %copy-start = (bf16[256,1152]{1,0:T(8,128)(2,1)S(1)}, bf16[256,1152]{1,0:T(8,128)(2,1)}, u32[]{:S(2)}) copy-start(bf16[256,1152]{1,0:T(8,128)(2,1)} %x_hbm) | copy-start | bytes 1769476
  0.7 92.9 %copy-start.7 = (s32[6]{0:T(128)}, s32[6]{0:T(128)S(1)}, u32[]{:S(2)}) copy-start(s32[6]{0:T(128)S(1)} %stack.27.pos_ref) | copy-start | bytes 76
  0.7 1.1 copy-start.1
  1.9 2.8 %copy-start.8 = (f32[1,1152]{1,0:T(1,128)S(1)}, f32[1,1152]{1,0:T(1,128)}, u32[]{:S(2)}) copy-start(f32[1,1152]{1,0:T(1,128)} %gain_hbm.1) | copy-start | bytes 13828
  12.0 9.5 %collective-permute-start = (bf16[128,1152]{1,0:T(8,128)(2,1)S(1)}, bf16[128,1152]{1,0:T(8,128)(2,1)S(1)}, u32[]{:S(2)}, u32[]{:S(2)}) collective-permute-start(bf16[128,1152]{1,0:T(8,128)(2,1)S(1)} %get-tuple-element.34), channel_id=1, source_target_pairs={{0,1},{2,3},{1,0},{3,2},{4,5},{6,7},{5,4},{7,6},{8,9},{10,11},{9,8... | collective-permute-start | bytes 884744 | tf_op jit(solution)/shard_map/ppermute | solution.py:34
  15.8 12.3 %collective-permute-start.1 = (bf16[128,1152]{1,0:T(8,128)(2,1)S(1)}, bf16[128,1152]{1,0:T(8,128)(2,1)S(1)}, u32[]{:S(2)}, u32[]{:S(2)}) collective-permute-start(bf16[128,1152]{1,0:T(8,128)(2,1)S(1)} %get-tuple-element.38), channel_id=1, source_target_pairs={{0,1},{2,3},{1,0},{3,2},{4,5},{6,7},{5,4},{7,6},{8,9},{10,11},{9,8... | collective-permute-start | bytes 884744 | tf_op jit(solution)/shard_map/ppermute | solution.py:34
  21.7 10.1 %copy-start.5 = (f32[128,128]{1,0:T(8,128)}, f32[128,128]{1,0:T(8,128)S(1)}, u32[]{:S(2)}) copy-start(f32[128,128]{1,0:T(8,128)S(1)} %get-tuple-element.47.n_ref) | copy-start | bytes 196612
  21.7 18.2 %copy-start.9 = (bf16[128,1152]{1,0:T(8,128)(2,1)}, bf16[128,1152]{1,0:T(8,128)(2,1)S(1)}, u32[]{:S(2)}) copy-start(bf16[128,1152]{1,0:T(8,128)(2,1)S(1)} %get-tuple-element.36.refs_0_) | copy-start | bytes 884740
  21.7 11.5 %collective-permute-start.3 = (bf16[128,1152]{1,0:T(8,128)(2,1)S(1)}, bf16[128,1152]{1,0:T(8,128)(2,1)S(1)}, u32[]{:S(2)}, u32[]{:S(2)}) collective-permute-start(bf16[128,1152]{1,0:T(8,128)(2,1)S(1)} %get-tuple-element.36.refs_0_), channel_id=1, source_target_pairs={{0,112},{2,114},{1,113},{3,115},{4,116},{6,118},{5,117},{7,119},{8... | collective-permute-start | bytes 884744 | tf_op jit(solution)/shard_map/ppermute | solution.py:34
  28.2 6.8 %collective-permute-start.2 = (bf16[128,1152]{1,0:T(8,128)(2,1)S(1)}, bf16[128,1152]{1,0:T(8,128)(2,1)S(1)}, u32[]{:S(2)}, u32[]{:S(2)}) collective-permute-start(bf16[128,1152]{1,0:T(8,128)(2,1)S(1)} %get-tuple-element.36.refs_0_), channel_id=1, source_target_pairs={{0,16},{2,18},{1,17},{3,19},{4,20},{6,22},{5,21},{7,23},{8,24},{10... | collective-permute-start | bytes 884744 | tf_op jit(solution)/shard_map/ppermute | solution.py:34
  28.4 7.9 %collective-permute-start.8 = (bf16[128,1152]{1,0:T(8,128)(2,1)S(1)}, bf16[128,1152]{1,0:T(8,128)(2,1)S(1)}, u32[]{:S(2)}, u32[]{:S(2)}) collective-permute-start(bf16[128,1152]{1,0:T(8,128)(2,1)S(1)} %shard_map.90.refs_0_), channel_id=1, source_target_pairs={{0,8},{2,10},{1,9},{3,11},{4,12},{6,14},{5,13},{7,15},{8,0},{10,2}... | collective-permute-start | bytes 884744 | tf_op jit(solution)/shard_map/ppermute | solution.py:34
  31.8 8.0 %collective-permute-start.7 = (bf16[128,1152]{1,0:T(8,128)(2,1)S(1)}, bf16[128,1152]{1,0:T(8,128)(2,1)S(1)}, u32[]{:S(2)}, u32[]{:S(2)}) collective-permute-start(bf16[128,1152]{1,0:T(8,128)(2,1)S(1)} %shard_map.90.refs_0_), channel_id=1, source_target_pairs={{0,12},{2,14},{1,13},{3,15},{4,0},{6,2},{5,1},{7,3},{8,4},{10,6},{... | collective-permute-start | bytes 884744 | tf_op jit(solution)/shard_map/ppermute | solution.py:34
  32.6 7.2 %collective-permute-start.6 = (bf16[128,1152]{1,0:T(8,128)(2,1)S(1)}, bf16[128,1152]{1,0:T(8,128)(2,1)S(1)}, u32[]{:S(2)}, u32[]{:S(2)}) collective-permute-start(bf16[128,1152]{1,0:T(8,128)(2,1)S(1)} %shard_map.90.refs_0_), channel_id=1, source_target_pairs={{0,4},{2,6},{1,5},{3,7},{4,8},{6,10},{5,9},{7,11},{8,12},{10,14},{... | collective-permute-start | bytes 884744 | tf_op jit(solution)/shard_map/ppermute | solution.py:34
  33.3 19.3 %copy-start.11 = (bf16[128,1152]{1,0:T(8,128)(2,1)}, bf16[128,1152]{1,0:T(8,128)(2,1)S(1)}, u32[]{:S(2)}) copy-start(bf16[128,1152]{1,0:T(8,128)(2,1)S(1)} %collective-permute-done.3.refs_2_) | copy-start | bytes 884740
  35.0 13.1 %copy-start.13 = (bf16[128,1152]{1,0:T(8,128)(2,1)}, bf16[128,1152]{1,0:T(8,128)(2,1)S(1)}, u32[]{:S(2)}) copy-start(bf16[128,1152]{1,0:T(8,128)(2,1)S(1)} %collective-permute-done.2.refs_1_) | copy-start | bytes 884740
  39.9 20.0 %collective-permute-start.10 = (bf16[512,1152]{1,0:T(8,128)(2,1)S(1)}, bf16[512,1152]{1,0:T(8,128)(2,1)S(1)}, u32[]{:S(2)}, u32[]{:S(2)}) collective-permute-start(bf16[512,1152]{1,0:T(8,128)(2,1)S(1)} %shard_map.91.refs_8_), channel_id=1, source_target_pairs={{0,3},{2,0},{1,2},{3,1},{4,7},{6,4},{5,6},{7,5},{8,11},{10,8},{9,1... | collective-permute-start | bytes 3538952 | tf_op jit(solution)/shard_map/ppermute | solution.py:34
  42.5 17.5 %collective-permute-start.9 = (bf16[512,1152]{1,0:T(8,128)(2,1)S(1)}, bf16[512,1152]{1,0:T(8,128)(2,1)}, u32[]{:S(2)}, u32[]{:S(2)}) collective-permute-start(bf16[512,1152]{1,0:T(8,128)(2,1)S(1)} %shard_map.91.refs_8_), channel_id=1, source_target_pairs={{0,2},{2,1},{1,3},{3,0},{4,6},{6,5},{5,7},{7,4},{8,10},{10,9},{9,1... | collective-permute-start | bytes 3538952 | tf_op jit(solution)/shard_map/ppermute | solution.py:34
  42.5 10.1 %collective-permute-start.4 = (bf16[128,1152]{1,0:T(8,128)(2,1)S(1)}, bf16[128,1152]{1,0:T(8,128)(2,1)}, u32[]{:S(2)}, u32[]{:S(2)}) collective-permute-start(bf16[128,1152]{1,0:T(8,128)(2,1)S(1)} %collective-permute-done.2.refs_1_), channel_id=1, source_target_pairs={{0,16},{2,18},{1,17},{3,19},{4,20},{6,22},{5,21},{7,23},{8,24},{10... | collective-permute-start | bytes 884744 | tf_op jit(solution)/shard_map/ppermute | solution.py:34
  44.1 8.5 %collective-permute-start.5 = (bf16[128,1152]{1,0:T(8,128)(2,1)S(1)}, bf16[128,1152]{1,0:T(8,128)(2,1)}, u32[]{:S(2)}, u32[]{:S(2)}) collective-permute-start(bf16[128,1152]{1,0:T(8,128)(2,1)S(1)} %collective-permute-done.3.refs_2_), channel_id=1, source_target_pairs={{0,112},{2,114},{1,113},{3,115},{4,116},{6,118},{5,117},{7,119},{8... | collective-permute-start | bytes 884744 | tf_op jit(solution)/shard_map/ppermute | solution.py:34
  52.6 7.4 %collective-permute-start.11 = (bf16[128,1152]{1,0:T(8,128)(2,1)}, bf16[128,1152]{1,0:T(8,128)(2,1)S(1)}, u32[]{:S(2)}, u32[]{:S(2)}) collective-permute-start(bf16[128,1152]{1,0:T(8,128)(2,1)} %collective-permute-done.4.refs_3_), channel_id=1, source_target_pairs={{0,16},{2,18},{1,17},{3,19},{4,20},{6,22},{5,21},{7,23},{8,24},{10... | collective-permute-start | bytes 884744 | tf_op jit(solution)/shard_map/ppermute | solution.py:34
  52.6 7.4 %collective-permute-start.12 = (bf16[128,1152]{1,0:T(8,128)(2,1)}, bf16[128,1152]{1,0:T(8,128)(2,1)S(1)}, u32[]{:S(2)}, u32[]{:S(2)}) collective-permute-start(bf16[128,1152]{1,0:T(8,128)(2,1)} %collective-permute-done.5.refs_4_), channel_id=1, source_target_pairs={{0,112},{2,114},{1,113},{3,115},{4,116},{6,118},{5,117},{7,119},{8... | collective-permute-start | bytes 884744 | tf_op jit(solution)/shard_map/ppermute | solution.py:34
  61.1 6.7 %copy-start.15 = (s32[2048]{0:T(1024)S(1)}, s32[2048]{0:T(1024)}, u32[]{:S(2)}) copy-start(s32[2048]{0:T(1024)} %param.13) | copy-start | bytes 24580
  61.1 13.6 %copy-start.10 = (bf16[128,1152]{1,0:T(8,128)(2,1)S(1)}, bf16[128,1152]{1,0:T(8,128)(2,1)}, u32[]{:S(2)}) copy-start(bf16[128,1152]{1,0:T(8,128)(2,1)} %copy-done.9) | copy-start | bytes 884740
  61.1 13.6 %copy-start.12 = (bf16[128,1152]{1,0:T(8,128)(2,1)S(1)}, bf16[128,1152]{1,0:T(8,128)(2,1)}, u32[]{:S(2)}) copy-start(bf16[128,1152]{1,0:T(8,128)(2,1)} %copy-done.11) | copy-start | bytes 884740
  61.1 13.6 %copy-start.14 = (bf16[128,1152]{1,0:T(8,128)(2,1)S(1)}, bf16[128,1152]{1,0:T(8,128)(2,1)}, u32[]{:S(2)}) copy-start(bf16[128,1152]{1,0:T(8,128)(2,1)} %copy-done.13) | copy-start | bytes 884740
  61.2 10.3 %collective-permute-start.15 = (bf16[256,1152]{1,0:T(8,128)(2,1)S(1)}, bf16[256,1152]{1,0:T(8,128)(2,1)S(1)}, u32[]{:S(2)}, u32[]{:S(2)}) collective-permute-start(bf16[256,1152]{1,0:T(8,128)(2,1)S(1)} %slice.7), channel_id=1, source_target_pairs={{0,3},{2,0},{1,2},{3,1},{4,7},{6,4},{5,6},{7,5},{8,11},{10,8},{9,1... | collective-permute-start | bytes 1769480 | tf_op jit(solution)/shard_map/ppermute | solution.py:34
  64.5 10.2 %collective-permute-start.14 = (bf16[256,1152]{1,0:T(8,128)(2,1)S(1)}, bf16[256,1152]{1,0:T(8,128)(2,1)S(1)}, u32[]{:S(2)}, u32[]{:S(2)}) collective-permute-start(bf16[256,1152]{1,0:T(8,128)(2,1)S(1)} %slice.6), channel_id=1, source_target_pairs={{0,2},{2,1},{1,3},{3,0},{4,6},{6,5},{5,7},{7,4},{8,10},{10,9},{9,1... | collective-permute-start | bytes 1769480 | tf_op jit(solution)/shard_map/ppermute | solution.py:34
  64.5 6.9 %collective-permute-start.13 = (bf16[128,1152]{1,0:T(8,128)(2,1)S(1)}, bf16[128,1152]{1,0:T(8,128)(2,1)S(1)}, u32[]{:S(2)}, u32[]{:S(2)}) collective-permute-start(bf16[128,1152]{1,0:T(8,128)(2,1)S(1)} %broadcast_select_fusion), channel_id=1, source_target_pairs={{0,16},{2,18},{1,17},{3,19},{4,20},{6,22},{5,21},{7,23},{8,24},{10... | collective-permute-start | bytes 884744 | tf_op jit(solution)/shard_map/ppermute | solution.py:34
  68.3 20.0 %copy-start.2 = (f32[128,128]{1,0:T(8,128)}, f32[128,128]{1,0:T(8,128)S(1)}, u32[]{:S(2)}) copy-start(f32[128,128]{1,0:T(8,128)S(1)} %get-tuple-element.29.place_ref) | copy-start | bytes 196612
  88.2 5.4 %copy-start.6 = (f32[128,128]{1,0:T(8,128)S(1)}, f32[128,128]{1,0:T(8,128)}, u32[]{:S(2)}) copy-start(f32[128,128]{1,0:T(8,128)} %copy-done.5) | copy-start | bytes 196612
  88.2 5.5 %copy-start.3 = (f32[128,128]{1,0:T(8,128)S(1)}, f32[128,128]{1,0:T(8,128)}, u32[]{:S(2)}) copy-start(f32[128,128]{1,0:T(8,128)} %copy-done.2) | copy-start | bytes 196612
  88.2 19.2 %all-to-all-start = ((bf16[8,32,1280]{2,1,0:T(8,128)(2,1)}), bf16[8,32,1280]{2,1,0:T(8,128)(2,1)S(1)}, u32[]{:S(2)}, u32[]{:S(2)}) async-start(bf16[8,32,1280]{2,1,0:T(8,128)(2,1)} %bitcast.11), calls=%async_computation | async-start | bytes 1310720 | tf_op jit(solution)/shard_map/all_to_all | solution.py:422
  107.7 0.6 copy-start.4
  108.3 8.8 %collective-permute-start.16 = (f32[40,576]{1,0:T(8,128)S(1)}, f32[40,576]{1,0:T(8,128)S(1)}, u32[]{:S(2)}, u32[]{:S(2)}) collective-permute-start(f32[40,576]{1,0:T(8,128)S(1)} %get-tuple-element.51), channel_id=1, source_target_pairs={{0,128},{2,130},{1,129},{3,131},{4,132},{6,134},{5,133},{7,135},{8... | collective-permute-start | bytes 276488 | tf_op jit(solution)/shard_map/ppermute | solution.py:34
  117.2 0.6 copy-start.16

commit v3 on v2

--- a/solution.py
+++ b/solution.py
@@ -12,6 +12,7 @@
 LN2 = 0.6931471805599453
 NZ, NX, NY = 8, 4, 4
 ROWS = 128
+BLOCK = 256
 CAP = 32
 AXES = ("grp", "z", "x", "ylo", "yhi")
 ZOFF = (0, -1, 1, -2, 2, -3, 3, 4)
@@ -97,45 +98,39 @@
     other_ref[...] = other.astype(jnp.bfloat16)
 
 
-def text_kernel(
-    pos_ref, text_hbm, head_hbm, own_ref, other_ref, text_ref, head_ref, acc_ref, sems
+def head_kernel(
+    pos_ref, x_hbm, gain_hbm, text_hbm, head_hbm, up_hbm, down_hbm,
+    own_ref, other_ref, own_text_ref, other_text_ref,
+    x_ref, gain_ref, text_ref, head_ref, up_ref, down_ref,
+    normed_ref, hidden_ref, acc_ref, sems,
 ):
+    sources = [x_hbm, gain_hbm, text_hbm, head_hbm, up_hbm, down_hbm]
+    targets = [x_ref, gain_ref, text_ref, head_ref, up_ref, down_ref]
     copies = [
-        pltpu.make_async_copy(text_hbm, text_ref, sems.at[0]),
-        pltpu.make_async_copy(head_hbm, head_ref, sems.at[1]),
+        pltpu.make_async_copy(source, target, sems.at[k])
+        for k, (source, target) in enumerate(zip(sources, targets))
     ]
     for c in copies:
         c.start()
-    for c in copies:
-        c.wait()
-    depth = head_ref.shape[0]
     m = pos_ref[0]
-    text = text_ref[...]
-    part = jnp.where(m == 0, text[:, :depth], text[:, depth:])
-    acc_ref[...] = jnp.dot(part, head_ref[...], preferred_element_type=jnp.float32)
-    split_rows(acc_ref, m, own_ref, other_ref)
-
-
-def mlp_kernel(
-    pos_ref, gain_hbm, x_hbm, up_hbm, down_hbm, own_ref, other_ref,
-    gain_ref, x_ref, up_ref, down_ref, normed_ref, hidden_ref, acc_ref, sems,
-):
-    copies = [
-        pltpu.make_async_copy(source, target, sems.at[k])
-        for k, (source, target) in enumerate(
-            [(x_hbm, x_ref), (up_hbm, up_ref), (down_hbm, down_ref), (gain_hbm, gain_ref)]
-        )
-    ]
-    for c in copies:
-        c.start()
+    rows = own_ref.shape[0]
     copies[0].wait()
+    copies[1].wait()
     x = x_ref[...].astype(jnp.float32)
     mean = jnp.mean(x, axis=1, keepdims=True)
     gap = x - mean
     var = jnp.mean(gap * gap, axis=1, keepdims=True)
+    normed_ref[...] = (gap * lax.rsqrt(var + EPS) * gain_ref[...]).astype(jnp.bfloat16)
+
+    copies[2].wait()
     copies[3].wait()
-    normed_ref[...] = (gap * lax.rsqrt(var + EPS) * gain_ref[...]).astype(jnp.bfloat16)
-    copies[1].wait()
+    depth = head_ref.shape[0]
+    text = text_ref[...]
+    part = jnp.where(m == 0, text[:, :depth], text[:, depth:])
+    acc_ref[...] = jnp.dot(part, head_ref[...], preferred_element_type=jnp.float32)
+    split_rows(acc_ref, m, own_text_ref, other_text_ref)
+
+    copies[4].wait()
     total, block = up_ref.shape[0], 512
     for start in range(0, total, block):
         stop = min(start + block, total)
@@ -146,30 +141,38 @@
             preferred_element_type=jnp.float32,
         )
         hidden_ref[:, start:stop] = jax.nn.gelu(acc, approximate=True).astype(jnp.bfloat16)
-    copies[2].wait()
+    copies[5].wait()
     block = 384
     for start in range(0, acc_ref.shape[1], block):
         acc_ref[:, start : start + block] = jnp.dot(
             hidden_ref[...], down_ref[:, start : start + block], preferred_element_type=jnp.float32
         )
-    split_rows(acc_ref, pos_ref[0], own_ref, other_ref)
-    rows = own_ref.shape[0]
-    x = x_ref[pl.ds(pl.multiple_of(pos_ref[0] * rows, rows), rows), :]
+    split_rows(acc_ref, m, own_ref, other_ref)
+    x = x_ref[pl.ds(pl.multiple_of(m * rows, rows), rows), :]
     own_ref[...] = own_ref[...] + x.astype(jnp.float32)
 
 
-def from_hbm(kernel, pos, arrays, rows, width, scratch, flops):
+def heads(pos, x, gain, text, head, up, down):
+    arrays = [x, gain, text, head, up, down]
+    rows, width, hidden = x.shape[0], x.shape[1], up.shape[0]
+    half, bf16 = rows // 2, jnp.bfloat16
     vmem, hbm = pl.BlockSpec(memory_space=pltpu.VMEM), pl.BlockSpec(memory_space=pl.ANY)
     return pl.pallas_call(
-        kernel,
+        head_kernel,
         in_specs=[pl.BlockSpec(memory_space=pltpu.SMEM)] + [hbm] * len(arrays),
-        out_specs=[vmem, vmem],
-        out_shape=[shape((rows, width)), shape((rows, width), jnp.bfloat16)],
+        out_specs=[vmem] * 4,
+        out_shape=[shape((half, width)), shape((half, width), bf16)] * 2,
         scratch_shapes=[pltpu.VMEM(a.shape, a.dtype) for a in arrays]
-        + scratch
-        + [pltpu.VMEM((2 * rows, width), jnp.float32), pltpu.SemaphoreType.DMA((len(arrays),))],
+        + [
+            pltpu.VMEM((rows, width), bf16),
+            pltpu.VMEM((rows, hidden), bf16),
+            pltpu.VMEM((rows, width), jnp.float32),
+            pltpu.SemaphoreType.DMA((len(arrays),)),
+        ],
         compiler_params=pltpu.CompilerParams(vmem_limit_bytes=52 * 1024 * 1024),
-        cost_estimate=pl.CostEstimate(flops=flops, bytes_accessed=11 << 20, transcendentals=0),
+        cost_estimate=pl.CostEstimate(
+            flops=4 * rows * width * hidden, bytes_accessed=12 << 20, transcendentals=rows * hidden
+        ),
     )(pos, *arrays)
 
 
@@ -233,12 +236,35 @@
     return lax.rem(z + (offset + NZ), NZ)
 
 
-def pair_kernel(pos_ref, chosen_ref, place_ref, *refs):
+def group_loss(images, pieces, own):
+    img = [r[...] for r in images]
+    img = img[0] if len(img) == 1 else jnp.concatenate(img, axis=0)
+    total = jnp.zeros((8, img.shape[0]), jnp.float32)
+    for k, (ref, start) in enumerate(pieces):
+        total = total + tile_loss(ref[start : start + BLOCK, :], img, own and k == 0)
+    return jnp.sum(total, axis=0, keepdims=True)
+
+
+def text_pieces(refs):
+    return [(ref, start) for ref in refs for start in range(0, ref.shape[0], BLOCK)]
+
+
+def early_kernel(*refs):
+    images, texts, out_ref = refs[: NZ - 1], refs[NZ - 1 : -1], refs[-1]
+    pieces = text_pieces(texts)
+    for first in range(0, NZ - 1, 2):
+        group = images[first : first + 2]
+        total = group_loss(group, pieces, first == 0)
+        for k in range(len(group)):
+            out_ref[first + k : first + k + 1, :] = total[:, k * ROWS : (k + 1) * ROWS]
+    out_ref[NZ - 1 :, :] = jnp.zeros((1, ROWS), jnp.float32)
+
+
+def pair_kernel(pos_ref, chosen_ref, place_ref, early_ref, *refs):
     images, texts, load_ref = refs[:NZ], refs[NZ:-1], refs[-1]
     z, x, y, xy = pos_ref[1], pos_ref[2], pos_ref[3], pos_ref[4]
     planes = NX * NY
-    block = 256
-    pieces = [(ref, s) for ref in texts for s in range(0, ref.shape[0], block)]
+    pieces = text_pieces(texts)
 
     picks = [own_pick(place_ref[pl.ds(image_row(z, o) * planes + xy, 1), :]) for o in ZOFF]
     packed = jnp.concatenate(
@@ -256,8 +282,8 @@
 
     lines = [text_row(dx, dy) for dx in POFF for dy in POFF]
     total = jnp.zeros(packed.shape, jnp.float32)
-    for k, (ref, s) in enumerate(pieces):
-        text = ref[s : s + block, :]
+    for k, (ref, start) in enumerate(pieces):
+        text = ref[start : start + BLOCK, :]
         mask = jnp.concatenate(lines[2 * k : 2 * k + 2], axis=1)
         t = lax.dot_general(
             packed, text, (((1,), (1,)), ((), ())), preferred_element_type=jnp.float32
@@ -278,14 +304,13 @@
         rows = pl.ds(pl.multiple_of(image_row(z, o) * CAP, CAP), CAP)
         load_ref[rows, :width] = total[k * CAP : (k + 1) * CAP, :]
 
-    for number in range(NZ // 2):
-        img = jnp.concatenate([images[2 * number][...], images[2 * number + 1][...]], axis=0)
-        total = jnp.zeros((8, img.shape[0]), jnp.float32)
-        for k, (ref, s) in enumerate(pieces):
-            total = total + tile_loss(ref[s : s + block, :], img, number == 0 and k == 0)
-        total = jnp.sum(total, axis=0, keepdims=True)
+    near, far = text_pieces(texts[:3]), text_pieces(texts[3:])
+    late = group_loss(images[NZ - 1 :], near, False)
+    for first in range(0, NZ, 2):
+        total = group_loss(images[first : first + 2], far, False)
         for k in range(2):
             loss = total[:, k * ROWS : (k + 1) * ROWS]
+            loss = loss + (late if first + k == NZ - 1 else early_ref[first + k : first + k + 1, :])
             parts = []
             for _ in range(3):
                 part = loss.astype(jnp.bfloat16).astype(jnp.float32)
@@ -293,7 +318,7 @@
                 parts.append(part)
             parts.append(jnp.zeros((CAP - 3, ROWS), jnp.float32))
             beside = jnp.concatenate(parts, axis=0).astype(jnp.bfloat16)
-            row = image_row(z, ZOFF[2 * number + k])
+            row = image_row(z, ZOFF[first + k])
             load_ref[pl.ds(pl.multiple_of(row * CAP, CAP), CAP), width:] = beside
 
 
@@ -314,32 +339,15 @@
     msg_ref[CAP:, :] = jnp.broadcast_to(line, (8, cut))
 
 
-def spread_kernel(pos_ref, keep_ref, recv_ref, place_ref, learn_ref, out_hbm, out_ref, sem):
+def spread_kernel(pos_ref, keep_ref, recv_ref, place_ref, learn_ref, out_ref):
     learner = pos_ref[5] == 1
     half = jnp.where(learner, keep_ref[:CAP, :], recv_ref[:CAP, :])
     pick = own_pick(place_ref[pl.ds(pos_ref[1] * (NX * NY) + pos_ref[4], 1), :])
     out_ref[...] = lax.dot_general(
-        pick, half, (((0,), (0,)), ((), ())), precision=EXACT, preferred_element_type=jnp.float32
-    )
-    copy = pltpu.make_async_copy(out_ref, out_hbm, sem)
-    copy.start()
+        half, pick, (((0,), (0,)), ((), ())), precision=EXACT, preferred_element_type=jnp.float32
+    )
     own, other = keep_ref[CAP : CAP + 1, :ROWS], recv_ref[CAP : CAP + 1, :ROWS]
     learn_ref[...] = jnp.where(learner, own - other, other - own)
-    copy.wait()
-
-
-def spread(pos, keep, recv, place_of):
-    vmem, hbm = pl.BlockSpec(memory_space=pltpu.VMEM), pl.BlockSpec(memory_space=pl.ANY)
-    cut = keep.shape[1]
-    return pl.pallas_call(
-        spread_kernel,
-        in_specs=[pl.BlockSpec(memory_space=pltpu.SMEM)] + [vmem] * 3,
-        out_specs=[vmem, hbm],
-        out_shape=[shape((1, ROWS)), shape((ROWS, cut))],
-        scratch_shapes=[pltpu.VMEM((ROWS, cut), jnp.float32), pltpu.SemaphoreType.DMA(())],
-        compiler_params=pltpu.CompilerParams(vmem_limit_bytes=56 * 1024 * 1024),
-        cost_estimate=pl.CostEstimate(flops=1 << 24, bytes_accessed=1 << 20, transcendentals=0),
-    )(pos, keep, recv, place_of)
 
 
 def shards(image_features, text_features, norm_gain, up_weight, down_weight, text_head, sub_index):
@@ -357,22 +365,17 @@
     pos = jnp.stack([p.astype(jnp.int32) for p in pos])
     cells = rows * width
 
-    own_text, other_text = from_hbm(
-        text_kernel, pos, [text_features, text_head[0]], rows, width, [], 2 * cells * width
-    )
+    own_img, other_img, own_text, other_text = heads(
+        pos,
+        image_features,
+        norm_gain,
+        text_features,
+        text_head[0],
+        up_weight[0].T,
+        down_weight[0],
+    )
+    recv_img = over_mp(other_img)
     recv_text = over_mp(other_text)
-    features, own_text = lax.optimization_barrier((image_features, own_text))
-    hidden = up_weight.shape[2]
-    own_img, other_img = from_hbm(
-        mlp_kernel,
-        pos,
-        [norm_gain, features, up_weight[0].T, down_weight[0]],
-        rows,
-        width,
-        [pltpu.VMEM((2 * rows, width), bf16), pltpu.VMEM((2 * rows, hidden), bf16)],
-        8 * cells * hidden,
-    )
-    recv_img = over_mp(other_img)
     chosen, place_of = call(
         index_kernel, [], [sub_index.reshape(1, -1)], [shape((blocks, rows))] * 2, 100 << 20
     )
@@ -395,9 +398,9 @@
         ahead.append(over_z(ahead[-1], (-1, -1)))
 
     z_step()
-    line[0], back[1], ahead[1] = lax.optimization_barrier((line[0], back[1], ahead[1]))
+    z_step()
+    line[0], back[2], ahead[2] = lax.optimization_barrier((line[0], back[2], ahead[2]))
     (joined,) = call(join_kernel, [], line, [shape((4 * rows, width), bf16)], cells)
-    z_step()
     text_back, text_ahead = over_plane(joined, 1, 1), over_plane(joined, -1, 1)
     z_step()
     text_back, text_ahead, back[3], ahead[3] = lax.optimization_barrier(
@@ -409,15 +412,22 @@
     texts = [joined, text_back, text_ahead, far_top, far_low]
     images = [z_img, back[1], ahead[1], back[2], ahead[2], back[3], ahead[3], last]
 
-    n_pairs, n_text = (NZ * rows, NX * NY * rows)
+    all_img, n_text = NZ * rows, NX * NY * rows
+    (early,) = call(
+        early_kernel,
+        [],
+        images[:-1] + texts[:3],
+        [shape((NZ, rows))],
+        all_img * width * n_text,
+        transcendentals=all_img * n_text // 2,
+    )
     (load,) = call(
         pair_kernel,
         [pos],
-        [chosen, place_of] + images + texts,
+        [chosen, place_of, early] + images + texts,
         [shape((NZ * CAP, width + rows), bf16)],
-        (2 * n_pairs + 4 * NZ * CAP) * width * n_text,
-        mib=16,
-        transcendentals=(n_pairs + NZ * CAP) * n_text,
+        (all_img + 4 * NZ * CAP) * width * n_text,
+        transcendentals=all_img * n_text // 2,
     )
     load = lax.all_to_all(load, "z", 0, 0, tiled=True)
     unit_sub, n_sub = call(
@@ -430,8 +440,14 @@
     keep, msg = call(
         finish_kernel, [], [load, unit_sub, n_sub], [shape((CAP + 8, cut))] * 2, 10 * cells
     )
-    learn, image_grad = spread(pos, keep, swap_cores(msg), place_of)
-    return (learn.reshape(rows), image_grad)
+    learn, image_grad = call(
+        spread_kernel,
+        [pos],
+        [keep, swap_cores(msg), place_of],
+        [shape((1, rows)), shape((cut, rows))],
+        200 * cells,
+    )
+    return (learn.reshape(rows), image_grad.T)
 
 
 def solution(mesh):

time: 123 us -> 116 us (0.943)
  starting transfers between devices: 46 us -> 42.7 us
  local copies, waits for them, and re-layouts: 5.56 us -> 2.6 us
    pallas_call x3 -> x1, Pallas kernels: 12.8 us -> 8 us  [heads(): pl.pallas_call(head_kernel, in_specs=[pl.BlockSpec(memory_space=pltpu.SME...]
    pallas_call x7 -> x9, Pallas kernels: 15.6 us -> 20.4 us  [call(): pl.pallas_call(kernel, in_specs=[pl.BlockSpec(memory_space=pltpu.SMEM)] *...]
    unnamed x35 -> x24, local copies, waits for them, and re-layouts: 4.32 us -> 1.36 us
    all_to_all x1, starting transfers between devices: 5.43 us -> 3.67 us  [shards(): load = lax.all_to_all(load, 'z', 0, 0, tiled=True)]
    ppermute x17, starting transfers between devices: 40.6 us -> 39.1 us  [permute(): return lax.ppermute(v, AXES, perm)]
  transfers between devices with their start and end apart: 18 -> 18, of which waited for: 10 -> 10; matrix products, arithmetic and copies ran while one was open for 0% -> 0% of each run, Pallas kernels for 1% -> 7%
where the time goes in v3:
time: 116 us
  starting transfers between devices  42.7 us (37%)
  waiting for transfers between devices  41.2 us (36%)
  Pallas kernels  28.4 us (24%)
  local copies, waits for them, and re-layouts  2.6 us (2%)
    ppermute x17, starting transfers between devices, permute(): return lax.ppermute(v, AXES, perm)  39.1 us
    ppermute x17, waiting for transfers between devices, permute(): return lax.ppermute(v, AXES, perm)  29 us
    pallas_call x9, Pallas kernels, call(): pl.pallas_call(kernel, in_specs=[pl.BlockSpec(memory_space=pltpu.SMEM)] *...  20.4 us
    all_to_all x1, waiting for transfers between devices, shards(): load = lax.all_to_all(load, 'z', 0, 0, tiled=True)  12.2 us
    pallas_call x1, Pallas kernels, heads(): pl.pallas_call(head_kernel, in_specs=[pl.BlockSpec(memory_space=pltpu.SME...  8 us
    all_to_all x1, starting transfers between devices, shards(): load = lax.all_to_all(load, 'z', 0, 0, tiled=True)  3.67 us
  transfers between devices with their start and end apart: 18, of which 10 were waited for; matrix products, arithmetic and copies ran while one was open for 0% of the time, Pallas kernels for 7%

profile of v3, /device:TPU:1, one launch (start us, length us, event | category | flops | bytes accessed | tf_op | source)
XLA Modules:
  0.0 115.8 jit_solution(4489833356093446638)
XLA Ops:
  0.6 0.1 stack.27.pos_ref
  0.7 0.7 copy-done.4
  1.4 8.0 %shard_map.87 = (f32[128,1152]{1,0:T(8,128)S(1)}, bf16[128,1152]{1,0:T(8,128)(2,1)S(1)}, f32[128,1152]{1,0:T(8,128)S(1)}, bf16[128,1152]{1,0:T(8,128)(2,1)S(1)}) custom-call(s32[6]{0:T(128)S(1)} %stack.27.pos_ref, bf16[256,1152]{1,0:T(8,128)(2,1)} %x_hbm.1, f32[1,1152]{1,0:T(1,128)S(1)} %copy-done.4, bf16[256,1152]{1,0:T(8,128)(2,1)} %text_hbm.1, ...), custom_call_target="tpu_custom_call" | custom-call | flops 2538602496 | bytes 12582912 | tf_op jit(solution)/shard_map/pallas_call | solution.py:160
  9.4 3.8 %collective-permute-start = (bf16[128,1152]{1,0:T(8,128)(2,1)S(1)}, bf16[128,1152]{1,0:T(8,128)(2,1)S(1)}, u32[]{:S(2)}, u32[]{:S(2)}) collective-permute-start(bf16[128,1152]{1,0:T(8,128)(2,1)S(1)} %get-tuple-element.30), channel_id=1, source_target_pairs={{0,1},{2,3},{1,0},{3,2},{4,5},{6,7},{5,4},{7,6},{8,9},{10,11},{9,8... | collective-permute-start | bytes 884744 | tf_op jit(solution)/shard_map/ppermute | solution.py:35
  13.2 5.7 %collective-permute-done.recv_ref = bf16[128,1152]{1,0:T(8,128)(2,1)S(1)} collective-permute-done((bf16[128,1152]{1,0:T(8,128)(2,1)S(1)}, bf16[128,1152]{1,0:T(8,128)(2,1)S(1)}, u32[]{:S(2)}, u32[]{:S(2)}) %collective-permute-start) | collective-permute-done | bytes 294944 | tf_op jit(solution)/shard_map/ppermute | solution.py:35
  18.9 0.2 shard_map.88
  19.1 0.6 copy-done.2
  19.7 6.4 %collective-permute-start.2 = (bf16[128,1152]{1,0:T(8,128)(2,1)S(1)}, bf16[128,1152]{1,0:T(8,128)(2,1)S(1)}, u32[]{:S(2)}, u32[]{:S(2)}) collective-permute-start(bf16[128,1152]{1,0:T(8,128)(2,1)S(1)} %get-tuple-element.32.refs_0_), channel_id=1, source_target_pairs={{0,112},{2,114},{1,113},{3,115},{4,116},{6,118},{5,117},{7,119},{8... | collective-permute-start | bytes 884744 | tf_op jit(solution)/shard_map/ppermute | solution.py:35
  26.1 0.0 collective-permute-start.1
  26.1 2.9 %collective-permute-start.3 = (bf16[128,1152]{1,0:T(8,128)(2,1)S(1)}, bf16[128,1152]{1,0:T(8,128)(2,1)S(1)}, u32[]{:S(2)}, u32[]{:S(2)}) collective-permute-start(bf16[128,1152]{1,0:T(8,128)(2,1)S(1)} %get-tuple-element.34), channel_id=1, source_target_pairs={{0,1},{2,3},{1,0},{3,2},{4,5},{6,7},{5,4},{7,6},{8,9},{10,11},{9,8... | collective-permute-start | bytes 884744 | tf_op jit(solution)/shard_map/ppermute | solution.py:35
  29.0 1.8 %collective-permute-done.2.refs_2_ = bf16[128,1152]{1,0:T(8,128)(2,1)S(1)} collective-permute-done((bf16[128,1152]{1,0:T(8,128)(2,1)S(1)}, bf16[128,1152]{1,0:T(8,128)(2,1)S(1)}, u32[]{:S(2)}, u32[]{:S(2)}) %collective-permute-start.2) | collective-permute-done | bytes 294944 | tf_op jit(solution)/shard_map/ppermute | solution.py:35
  30.9 3.4 %collective-permute-start.5 = (bf16[128,1152]{1,0:T(8,128)(2,1)S(1)}, bf16[128,1152]{1,0:T(8,128)(2,1)}, u32[]{:S(2)}, u32[]{:S(2)}) collective-permute-start(bf16[128,1152]{1,0:T(8,128)(2,1)S(1)} %collective-permute-done.2.refs_2_), channel_id=1, source_target_pairs={{0,112},{2,114},{1,113},{3,115},{4,116},{6,118},{5,117},{7,119},{8... | collective-permute-start | bytes 884744 | tf_op jit(solution)/shard_map/ppermute | solution.py:35
  34.3 0.0 collective-permute-done.3.recv_ref
  34.3 0.2 shard_map.89.refs_0_
  34.5 3.0 %collective-permute-start.8 = (bf16[128,1152]{1,0:T(8,128)(2,1)S(1)}, bf16[128,1152]{1,0:T(8,128)(2,1)S(1)}, u32[]{:S(2)}, u32[]{:S(2)}) collective-permute-start(bf16[128,1152]{1,0:T(8,128)(2,1)S(1)} %shard_map.89.refs_0_), channel_id=1, source_target_pairs={{0,8},{2,10},{1,9},{3,11},{4,12},{6,14},{5,13},{7,15},{8,0},{10,2}... | collective-permute-start | bytes 884744 | tf_op jit(solution)/shard_map/ppermute | solution.py:35
  37.5 0.8 collective-permute-start.7
  38.3 0.7 collective-permute-start.6
  39.0 0.0 collective-permute-done.5.refs_4_
  39.0 2.2 %collective-permute-done.4.refs_3_ = bf16[128,1152]{1,0:T(8,128)(2,1)} collective-permute-done((bf16[128,1152]{1,0:T(8,128)(2,1)S(1)}, bf16[128,1152]{1,0:T(8,128)(2,1)}, u32[]{:S(2)}, u32[]{:S(2)}) %collective-permute-start.4) | collective-permute-done | bytes 294944 | tf_op jit(solution)/shard_map/ppermute | solution.py:35
  41.2 0.5 collective-permute-done.8.refs_3_
  41.7 3.8 %collective-permute-done.7.refs_2_ = bf16[128,1152]{1,0:T(8,128)(2,1)S(1)} collective-permute-done((bf16[128,1152]{1,0:T(8,128)(2,1)S(1)}, bf16[128,1152]{1,0:T(8,128)(2,1)S(1)}, u32[]{:S(2)}, u32[]{:S(2)}) %collective-permute-start.7) | collective-permute-done | bytes 294944 | tf_op jit(solution)/shard_map/ppermute | solution.py:35
  45.5 0.1 shard_map.90.refs_7_.refs_8_
  45.6 2.7 %collective-permute-start.10 = (bf16[512,1152]{1,0:T(8,128)(2,1)S(1)}, bf16[512,1152]{1,0:T(8,128)(2,1)S(1)}, u32[]{:S(2)}, u32[]{:S(2)}) collective-permute-start(bf16[512,1152]{1,0:T(8,128)(2,1)S(1)} %shard_map.90.refs_7_.refs_8_), channel_id=1, source_target_pairs={{0,3},{2,0},{1,2},{3,1},{4,7},{6,4},{5,6},{7,5},{8,11},{10,8},{9,1... | collective-permute-start | bytes 3538952 | tf_op jit(solution)/shard_map/ppermute | solution.py:35
  48.4 0.0 collective-permute-start.9
  48.4 0.0 collective-permute-start.11
  48.4 2.7 %collective-permute-start.12 = (bf16[128,1152]{1,0:T(8,128)(2,1)}, bf16[128,1152]{1,0:T(8,128)(2,1)S(1)}, u32[]{:S(2)}, u32[]{:S(2)}) collective-permute-start(bf16[128,1152]{1,0:T(8,128)(2,1)} %collective-permute-done.5.refs_4_), channel_id=1, source_target_pairs={{0,112},{2,114},{1,113},{3,115},{4,116},{6,118},{5,117},{7,119},{8... | collective-permute-start | bytes 884744 | tf_op jit(solution)/shard_map/ppermute | solution.py:35
  51.0 4.3 %collective-permute-done.11.refs_5_ = bf16[128,1152]{1,0:T(8,128)(2,1)S(1)} collective-permute-done((bf16[128,1152]{1,0:T(8,128)(2,1)}, bf16[128,1152]{1,0:T(8,128)(2,1)S(1)}, u32[]{:S(2)}, u32[]{:S(2)}) %collective-permute-start.11) | collective-permute-done | bytes 294944 | tf_op jit(solution)/shard_map/ppermute | solution.py:35
  55.4 0.0 collective-permute-done.12.refs_6_
  55.4 6.1 %collective-permute-done.10.refs_9_.refs_10_ = bf16[512,1152]{1,0:T(8,128)(2,1)S(1)} collective-permute-done((bf16[512,1152]{1,0:T(8,128)(2,1)S(1)}, bf16[512,1152]{1,0:T(8,128)(2,1)S(1)}, u32[]{:S(2)}, u32[]{:S(2)}) %collective-permute-start.10) | collective-permute-done | bytes 1179680 | tf_op jit(solution)/shard_map/ppermute | solution.py:35
  61.5 3.5 %collective-permute-done.9.refs_8_.refs_9_ = bf16[512,1152]{1,0:T(8,128)(2,1)} collective-permute-done((bf16[512,1152]{1,0:T(8,128)(2,1)S(1)}, bf16[512,1152]{1,0:T(8,128)(2,1)}, u32[]{:S(2)}, u32[]{:S(2)}) %collective-permute-start.9) | collective-permute-done | bytes 1179680 | tf_op jit(solution)/shard_map/ppermute | solution.py:35
  65.0 1.1 slice.6
  66.1 0.0 copy-start.11
  66.2 0.0 copy-start.6
  66.2 0.1 collective-permute-start.15
  66.3 1.5 %collective-permute-start.14 = (bf16[256,1152]{1,0:T(8,128)(2,1)S(1)}, bf16[256,1152]{1,0:T(8,128)(2,1)S(1)}, u32[]{:S(2)}, u32[]{:S(2)}) collective-permute-start(bf16[256,1152]{1,0:T(8,128)(2,1)S(1)} %slice.6), channel_id=1, source_target_pairs={{0,2},{2,1},{1,3},{3,0},{4,6},{6,5},{5,7},{7,4},{8,10},{10,9},{9,1... | collective-permute-start | bytes 1769480 | tf_op jit(solution)/shard_map/ppermute | solution.py:35
  67.8 3.0 %collective-permute-start.13 = (bf16[128,1152]{1,0:T(8,128)(2,1)S(1)}, bf16[128,1152]{1,0:T(8,128)(2,1)S(1)}, u32[]{:S(2)}, u32[]{:S(2)}) collective-permute-start(bf16[128,1152]{1,0:T(8,128)(2,1)S(1)} %broadcast_select_fusion), channel_id=1, source_target_pairs={{0,16},{2,18},{1,17},{3,19},{4,20},{6,22},{5,21},{7,23},{8,24},{10... | collective-permute-start | bytes 884744 | tf_op jit(solution)/shard_map/ppermute | solution.py:35
  70.8 0.5 shard_map.86
  71.3 0.0 copy-start
  71.3 6.3 %shard_map.91.early_ref = f32[8,128]{1,0:T(8,128)S(1)} custom-call(bf16[128,1152]{1,0:T(8,128)(2,1)S(1)} %copy-done.6, bf16[128,1152]{1,0:T(8,128)(2,1)S(1)} %copy-done.10, bf16[128,1152]{1,0:T(8,128)(2,1)S(1)} %copy-done.8, bf16[128,1152]{1,0:T(8,128)(2,1)} %collective-permute-done.4.refs_3_, bf16[128,1152]{1,0:T(8,128)(2,1)} %collective-permute-done.5.refs_4_, ...), custom_call_target="tpu_custom_call" | custom-call | flops 2415919104 | bytes 1048576 | tf_op jit(solution)/shard_map/pallas_call | solution.py:65
  77.6 0.0 collective-permute-done.15.refs_12_
  77.6 10.3 %shard_map.92 = bf16[256,1280]{1,0:T(8,128)(2,1)} custom-call(s32[6]{0:T(128)S(1)} %stack.27.pos_ref, f32[128,128]{1,0:T(8,128)S(1)} %get-tuple-element.26.chosen_ref, f32[128,128]{1,0:T(8,128)S(1)} %get-tuple-element.27.place_ref, f32[8,128]{1,0:T(8,128)S(1)} %shard_map.91.early_ref, bf16[128,1152]{1,0:T(8,128)(2,1)S(1)} %copy-done.6, ...), custom_call_target="tpu_custom_call" | custom-call | flops 4831838208 | bytes 1048576 | tf_op jit(solution)/shard_map/pallas_call | solution.py:65
  87.9 3.7 %all-to-all-start = ((bf16[8,32,1280]{2,1,0:T(8,128)(2,1)}), bf16[8,32,1280]{2,1,0:T(8,128)(2,1)S(1)}, u32[]{:S(2)}, u32[]{:S(2)}) async-start(bf16[8,32,1280]{2,1,0:T(8,128)(2,1)} %bitcast.11), calls=%async_computation | async-start | bytes 1310720 | tf_op jit(solution)/shard_map/all_to_all | solution.py:432
  91.6 1.0 shard_map.93
  92.6 12.2 %all-to-all-done = bf16[8,32,1280]{2,1,0:T(8,128)(2,1)S(1)} async-done(((bf16[8,32,1280]{2,1,0:T(8,128)(2,1)}), bf16[8,32,1280]{2,1,0:T(8,128)(2,1)S(1)}, u32[]{:S(2)}, u32[]{:S(2)}) %all-to-all-start) | async-done | bytes 655392 | tf_op jit(solution)/shard_map/all_to_all | solution.py:432
  104.7 0.2 shard_map.94
  105.0 8.2 %collective-permute-start.16 = (f32[40,576]{1,0:T(8,128)S(1)}, f32[40,576]{1,0:T(8,128)S(1)}, u32[]{:S(2)}, u32[]{:S(2)}) collective-permute-start(f32[40,576]{1,0:T(8,128)S(1)} %get-tuple-element.47), channel_id=1, source_target_pairs={{0,128},{2,130},{1,129},{3,131},{4,132},{6,134},{5,133},{7,135},{8... | collective-permute-start | bytes 276488 | tf_op jit(solution)/shard_map/ppermute | solution.py:35
  113.1 0.9 collective-permute-done.16.recv_ref
  114.1 1.7 %shard_map.95 = (f32[1,128]{1,0:T(1,128)}, f32[576,128]{1,0:T(8,128)}) custom-call(s32[6]{0:T(128)S(1)} %stack.27.pos_ref, f32[40,576]{1,0:T(8,128)S(1)} %get-tuple-element.46.keep_ref, f32[40,576]{1,0:T(8,128)S(1)} %collective-permute-done.16.recv_ref, f32[128,128]{1,0:T(8,128)S(1)} %copy-done.1), custom_call_target="tpu_custom_call" | custom-call | flops 29491200 | bytes 1048576 | tf_op jit(solution)/shard_map/pallas_call | solution.py:65
  (26 shorter events, 0.1 us)
Async XLA Ops:
  0.7 0.7 copy-start.4
  9.4 9.5 %collective-permute-start = (bf16[128,1152]{1,0:T(8,128)(2,1)S(1)}, bf16[128,1152]{1,0:T(8,128)(2,1)S(1)}, u32[]{:S(2)}, u32[]{:S(2)}) collective-permute-start(bf16[128,1152]{1,0:T(8,128)(2,1)S(1)} %get-tuple-element.30), channel_id=1, source_target_pairs={{0,1},{2,3},{1,0},{3,2},{4,5},{6,7},{5,4},{7,6},{8,9},{10,11},{9,8... | collective-permute-start | bytes 884744 | tf_op jit(solution)/shard_map/ppermute | solution.py:35
  19.1 0.6 copy-start.2
  19.7 25.9 %copy-start.5 = (bf16[128,1152]{1,0:T(8,128)(2,1)}, bf16[128,1152]{1,0:T(8,128)(2,1)S(1)}, u32[]{:S(2)}) copy-start(bf16[128,1152]{1,0:T(8,128)(2,1)S(1)} %get-tuple-element.32.refs_0_) | copy-start | bytes 884740
  19.7 11.1 %collective-permute-start.2 = (bf16[128,1152]{1,0:T(8,128)(2,1)S(1)}, bf16[128,1152]{1,0:T(8,128)(2,1)S(1)}, u32[]{:S(2)}, u32[]{:S(2)}) collective-permute-start(bf16[128,1152]{1,0:T(8,128)(2,1)S(1)} %get-tuple-element.32.refs_0_), channel_id=1, source_target_pairs={{0,112},{2,114},{1,113},{3,115},{4,116},{6,118},{5,117},{7,119},{8... | collective-permute-start | bytes 884744 | tf_op jit(solution)/shard_map/ppermute | solution.py:35
  26.1 8.2 %collective-permute-start.1 = (bf16[128,1152]{1,0:T(8,128)(2,1)S(1)}, bf16[128,1152]{1,0:T(8,128)(2,1)S(1)}, u32[]{:S(2)}, u32[]{:S(2)}) collective-permute-start(bf16[128,1152]{1,0:T(8,128)(2,1)S(1)} %get-tuple-element.32.refs_0_), channel_id=1, source_target_pairs={{0,16},{2,18},{1,17},{3,19},{4,20},{6,22},{5,21},{7,23},{8,24},{10... | collective-permute-start | bytes 884744 | tf_op jit(solution)/shard_map/ppermute | solution.py:35
  26.1 8.2 %collective-permute-start.3 = (bf16[128,1152]{1,0:T(8,128)(2,1)S(1)}, bf16[128,1152]{1,0:T(8,128)(2,1)S(1)}, u32[]{:S(2)}, u32[]{:S(2)}) collective-permute-start(bf16[128,1152]{1,0:T(8,128)(2,1)S(1)} %get-tuple-element.34), channel_id=1, source_target_pairs={{0,1},{2,3},{1,0},{3,2},{4,5},{6,7},{5,4},{7,6},{8,9},{10,11},{9,8... | collective-permute-start | bytes 884744 | tf_op jit(solution)/shard_map/ppermute | solution.py:35
  30.9 14.7 %copy-start.7 = (bf16[128,1152]{1,0:T(8,128)(2,1)}, bf16[128,1152]{1,0:T(8,128)(2,1)S(1)}, u32[]{:S(2)}) copy-start(bf16[128,1152]{1,0:T(8,128)(2,1)S(1)} %collective-permute-done.2.refs_2_) | copy-start | bytes 884740
  30.9 8.1 %collective-permute-start.5 = (bf16[128,1152]{1,0:T(8,128)(2,1)S(1)}, bf16[128,1152]{1,0:T(8,128)(2,1)}, u32[]{:S(2)}, u32[]{:S(2)}) collective-permute-start(bf16[128,1152]{1,0:T(8,128)(2,1)S(1)} %collective-permute-done.2.refs_2_), channel_id=1, source_target_pairs={{0,112},{2,114},{1,113},{3,115},{4,116},{6,118},{5,117},{7,119},{8... | collective-permute-start | bytes 884744 | tf_op jit(solution)/shard_map/ppermute | solution.py:35
  34.3 11.3 %copy-start.9 = (bf16[128,1152]{1,0:T(8,128)(2,1)}, bf16[128,1152]{1,0:T(8,128)(2,1)S(1)}, u32[]{:S(2)}) copy-start(bf16[128,1152]{1,0:T(8,128)(2,1)S(1)} %collective-permute-done.1.refs_1_) | copy-start | bytes 884740
  34.3 6.9 %collective-permute-start.4 = (bf16[128,1152]{1,0:T(8,128)(2,1)S(1)}, bf16[128,1152]{1,0:T(8,128)(2,1)}, u32[]{:S(2)}, u32[]{:S(2)}) collective-permute-start(bf16[128,1152]{1,0:T(8,128)(2,1)S(1)} %collective-permute-done.1.refs_1_), channel_id=1, source_target_pairs={{0,16},{2,18},{1,17},{3,19},{4,20},{6,22},{5,21},{7,23},{8,24},{10... | collective-permute-start | bytes 884744 | tf_op jit(solution)/shard_map/ppermute | solution.py:35
  34.5 7.2 %collective-permute-start.8 = (bf16[128,1152]{1,0:T(8,128)(2,1)S(1)}, bf16[128,1152]{1,0:T(8,128)(2,1)S(1)}, u32[]{:S(2)}, u32[]{:S(2)}) collective-permute-start(bf16[128,1152]{1,0:T(8,128)(2,1)S(1)} %shard_map.89.refs_0_), channel_id=1, source_target_pairs={{0,8},{2,10},{1,9},{3,11},{4,12},{6,14},{5,13},{7,15},{8,0},{10,2}... | collective-permute-start | bytes 884744 | tf_op jit(solution)/shard_map/ppermute | solution.py:35
  37.5 8.0 %collective-permute-start.7 = (bf16[128,1152]{1,0:T(8,128)(2,1)S(1)}, bf16[128,1152]{1,0:T(8,128)(2,1)S(1)}, u32[]{:S(2)}, u32[]{:S(2)}) collective-permute-start(bf16[128,1152]{1,0:T(8,128)(2,1)S(1)} %shard_map.89.refs_0_), channel_id=1, source_target_pairs={{0,12},{2,14},{1,13},{3,15},{4,0},{6,2},{5,1},{7,3},{8,4},{10,6},{... | collective-permute-start | bytes 884744 | tf_op jit(solution)/shard_map/ppermute | solution.py:35
  38.3 7.2 %collective-permute-start.6 = (bf16[128,1152]{1,0:T(8,128)(2,1)S(1)}, bf16[128,1152]{1,0:T(8,128)(2,1)S(1)}, u32[]{:S(2)}, u32[]{:S(2)}) collective-permute-start(bf16[128,1152]{1,0:T(8,128)(2,1)S(1)} %shard_map.89.refs_0_), channel_id=1, source_target_pairs={{0,4},{2,6},{1,5},{3,7},{4,8},{6,10},{5,9},{7,11},{8,12},{10,14},{... | collective-permute-start | bytes 884744 | tf_op jit(solution)/shard_map/ppermute | solution.py:35
  45.6 15.9 %collective-permute-start.10 = (bf16[512,1152]{1,0:T(8,128)(2,1)S(1)}, bf16[512,1152]{1,0:T(8,128)(2,1)S(1)}, u32[]{:S(2)}, u32[]{:S(2)}) collective-permute-start(bf16[512,1152]{1,0:T(8,128)(2,1)S(1)} %shard_map.90.refs_7_.refs_8_), channel_id=1, source_target_pairs={{0,3},{2,0},{1,2},{3,1},{4,7},{6,4},{5,6},{7,5},{8,11},{10,8},{9,1... | collective-permute-start | bytes 3538952 | tf_op jit(solution)/shard_map/ppermute | solution.py:35
  48.4 16.7 %collective-permute-start.9 = (bf16[512,1152]{1,0:T(8,128)(2,1)S(1)}, bf16[512,1152]{1,0:T(8,128)(2,1)}, u32[]{:S(2)}, u32[]{:S(2)}) collective-permute-start(bf16[512,1152]{1,0:T(8,128)(2,1)S(1)} %shard_map.90.refs_7_.refs_8_), channel_id=1, source_target_pairs={{0,2},{2,1},{1,3},{3,0},{4,6},{6,5},{5,7},{7,4},{8,10},{10,9},{9,1... | collective-permute-start | bytes 3538952 | tf_op jit(solution)/shard_map/ppermute | solution.py:35
  48.4 7.0 %collective-permute-start.11 = (bf16[128,1152]{1,0:T(8,128)(2,1)}, bf16[128,1152]{1,0:T(8,128)(2,1)S(1)}, u32[]{:S(2)}, u32[]{:S(2)}) collective-permute-start(bf16[128,1152]{1,0:T(8,128)(2,1)} %collective-permute-done.4.refs_3_), channel_id=1, source_target_pairs={{0,16},{2,18},{1,17},{3,19},{4,20},{6,22},{5,21},{7,23},{8,24},{10... | collective-permute-start | bytes 884744 | tf_op jit(solution)/shard_map/ppermute | solution.py:35
  48.4 7.0 %collective-permute-start.12 = (bf16[128,1152]{1,0:T(8,128)(2,1)}, bf16[128,1152]{1,0:T(8,128)(2,1)S(1)}, u32[]{:S(2)}, u32[]{:S(2)}) collective-permute-start(bf16[128,1152]{1,0:T(8,128)(2,1)} %collective-permute-done.5.refs_4_), channel_id=1, source_target_pairs={{0,112},{2,114},{1,113},{3,115},{4,116},{6,118},{5,117},{7,119},{8... | collective-permute-start | bytes 884744 | tf_op jit(solution)/shard_map/ppermute | solution.py:35
  66.1 4.6 %copy-start.11 = (s32[2048]{0:T(1024)S(1)}, s32[2048]{0:T(1024)}, u32[]{:S(2)}) copy-start(s32[2048]{0:T(1024)} %param.13) | copy-start | bytes 24580
  66.2 5.1 %copy-start.6 = (bf16[128,1152]{1,0:T(8,128)(2,1)S(1)}, bf16[128,1152]{1,0:T(8,128)(2,1)}, u32[]{:S(2)}) copy-start(bf16[128,1152]{1,0:T(8,128)(2,1)} %copy-done.5) | copy-start | bytes 884740
  66.2 5.1 %copy-start.8 = (bf16[128,1152]{1,0:T(8,128)(2,1)S(1)}, bf16[128,1152]{1,0:T(8,128)(2,1)}, u32[]{:S(2)}) copy-start(bf16[128,1152]{1,0:T(8,128)(2,1)} %copy-done.7) | copy-start | bytes 884740
  66.2 5.1 %copy-start.10 = (bf16[128,1152]{1,0:T(8,128)(2,1)S(1)}, bf16[128,1152]{1,0:T(8,128)(2,1)}, u32[]{:S(2)}) copy-start(bf16[128,1152]{1,0:T(8,128)(2,1)} %copy-done.9) | copy-start | bytes 884740
  66.2 11.3 %collective-permute-start.15 = (bf16[256,1152]{1,0:T(8,128)(2,1)S(1)}, bf16[256,1152]{1,0:T(8,128)(2,1)S(1)}, u32[]{:S(2)}, u32[]{:S(2)}) collective-permute-start(bf16[256,1152]{1,0:T(8,128)(2,1)S(1)} %slice.7), channel_id=1, source_target_pairs={{0,3},{2,0},{1,2},{3,1},{4,7},{6,4},{5,6},{7,5},{8,11},{10,8},{9,1... | collective-permute-start | bytes 1769480 | tf_op jit(solution)/shard_map/ppermute | solution.py:35
  66.3 11.3 %collective-permute-start.14 = (bf16[256,1152]{1,0:T(8,128)(2,1)S(1)}, bf16[256,1152]{1,0:T(8,128)(2,1)S(1)}, u32[]{:S(2)}, u32[]{:S(2)}) collective-permute-start(bf16[256,1152]{1,0:T(8,128)(2,1)S(1)} %slice.6), channel_id=1, source_target_pairs={{0,2},{2,1},{1,3},{3,0},{4,6},{6,5},{5,7},{7,4},{8,10},{10,9},{9,1... | collective-permute-start | bytes 1769480 | tf_op jit(solution)/shard_map/ppermute | solution.py:35
  67.8 9.7 %collective-permute-start.13 = (bf16[128,1152]{1,0:T(8,128)(2,1)S(1)}, bf16[128,1152]{1,0:T(8,128)(2,1)S(1)}, u32[]{:S(2)}, u32[]{:S(2)}) collective-permute-start(bf16[128,1152]{1,0:T(8,128)(2,1)S(1)} %broadcast_select_fusion), channel_id=1, source_target_pairs={{0,16},{2,18},{1,17},{3,19},{4,20},{6,22},{5,21},{7,23},{8,24},{10... | collective-permute-start | bytes 884744 | tf_op jit(solution)/shard_map/ppermute | solution.py:35
  71.3 6.3 %copy-start = (f32[128,128]{1,0:T(8,128)}, f32[128,128]{1,0:T(8,128)S(1)}, u32[]{:S(2)}) copy-start(f32[128,128]{1,0:T(8,128)S(1)} %get-tuple-element.27.place_ref) | copy-start | bytes 196612
  87.9 3.7 %copy-start.1 = (f32[128,128]{1,0:T(8,128)S(1)}, f32[128,128]{1,0:T(8,128)}, u32[]{:S(2)}) copy-start(f32[128,128]{1,0:T(8,128)} %copy-done) | copy-start | bytes 196612
  87.9 3.7 %copy-start.3 = (f32[128,128]{1,0:T(8,128)S(1)}, f32[128,128]{1,0:T(8,128)}, u32[]{:S(2)}) copy-start(f32[128,128]{1,0:T(8,128)} %copy-done.2) | copy-start | bytes 196612
  87.9 16.9 %all-to-all-start = ((bf16[8,32,1280]{2,1,0:T(8,128)(2,1)}), bf16[8,32,1280]{2,1,0:T(8,128)(2,1)S(1)}, u32[]{:S(2)}, u32[]{:S(2)}) async-start(bf16[8,32,1280]{2,1,0:T(8,128)(2,1)} %bitcast.11), calls=%async_computation | async-start | bytes 1310720 | tf_op jit(solution)/shard_map/all_to_all | solution.py:432
  105.0 9.1 %collective-permute-start.16 = (f32[40,576]{1,0:T(8,128)S(1)}, f32[40,576]{1,0:T(8,128)S(1)}, u32[]{:S(2)}, u32[]{:S(2)}) collective-permute-start(f32[40,576]{1,0:T(8,128)S(1)} %get-tuple-element.47), channel_id=1, source_target_pairs={{0,128},{2,130},{1,129},{3,131},{4,132},{6,134},{5,133},{7,135},{8... | collective-permute-start | bytes 276488 | tf_op jit(solution)/shard_map/ppermute | solution.py:35

commit v4 on v3

--- a/solution.py
+++ b/solution.py
@@ -98,19 +98,36 @@
     other_ref[...] = other.astype(jnp.bfloat16)
 
 
-def head_kernel(
-    pos_ref, x_hbm, gain_hbm, text_hbm, head_hbm, up_hbm, down_hbm,
-    own_ref, other_ref, own_text_ref, other_text_ref,
-    x_ref, gain_ref, text_ref, head_ref, up_ref, down_ref,
-    normed_ref, hidden_ref, acc_ref, sems,
+def text_kernel(
+    pos_ref, text_hbm, head_hbm, own_ref, other_ref, text_ref, head_ref, acc_ref, sems
 ):
-    sources = [x_hbm, gain_hbm, text_hbm, head_hbm, up_hbm, down_hbm]
-    targets = [x_ref, gain_ref, text_ref, head_ref, up_ref, down_ref]
+    copies = [
+        pltpu.make_async_copy(text_hbm, text_ref, sems.at[0]),
+        pltpu.make_async_copy(head_hbm, head_ref, sems.at[1]),
+    ]
+    for c in copies:
+        c.start()
+    for c in copies:
+        c.wait()
+    depth = head_ref.shape[0]
+    m = pos_ref[0]
+    text = text_ref[...]
+    part = jnp.where(m == 0, text[:, :depth], text[:, depth:])
+    acc_ref[...] = jnp.dot(part, head_ref[...], preferred_element_type=jnp.float32)
+    split_rows(acc_ref, m, own_ref, other_ref)
+
+
+def mlp_kernel(
+    pos_ref, x_hbm, gain_hbm, up_hbm, down_hbm, own_ref, other_ref,
+    x_ref, gain_ref, up_ref, down_ref, normed_ref, hidden_ref, acc_ref, sems,
+):
     copies = [
         pltpu.make_async_copy(source, target, sems.at[k])
-        for k, (source, target) in enumerate(zip(sources, targets))
+        for k, (source, target) in enumerate(
+            [(x_hbm, x_ref), (gain_hbm, gain_ref), (up_hbm, up_ref), (down_hbm, down_ref)]
+        )
     ]
-    for c in copies:
+    for c in copies[:3]:
         c.start()
     m = pos_ref[0]
     rows = own_ref.shape[0]
@@ -121,16 +138,8 @@
     gap = x - mean
     var = jnp.mean(gap * gap, axis=1, keepdims=True)
     normed_ref[...] = (gap * lax.rsqrt(var + EPS) * gain_ref[...]).astype(jnp.bfloat16)
-
     copies[2].wait()
-    copies[3].wait()
-    depth = head_ref.shape[0]
-    text = text_ref[...]
-    part = jnp.where(m == 0, text[:, :depth], text[:, depth:])
-    acc_ref[...] = jnp.dot(part, head_ref[...], preferred_element_type=jnp.float32)
-    split_rows(acc_ref, m, own_text_ref, other_text_ref)
-
-    copies[4].wait()
+    copies[3].start()
     total, block = up_ref.shape[0], 512
     for start in range(0, total, block):
         stop = min(start + block, total)
@@ -141,7 +150,7 @@
             preferred_element_type=jnp.float32,
         )
         hidden_ref[:, start:stop] = jax.nn.gelu(acc, approximate=True).astype(jnp.bfloat16)
-    copies[5].wait()
+    copies[3].wait()
     block = 384
     for start in range(0, acc_ref.shape[1], block):
         acc_ref[:, start : start + block] = jnp.dot(
@@ -152,27 +161,18 @@
     own_ref[...] = own_ref[...] + x.astype(jnp.float32)
 
 
-def heads(pos, x, gain, text, head, up, down):
-    arrays = [x, gain, text, head, up, down]
-    rows, width, hidden = x.shape[0], x.shape[1], up.shape[0]
-    half, bf16 = rows // 2, jnp.bfloat16
+def from_hbm(kernel, pos, arrays, rows, width, scratch, flops):
     vmem, hbm = pl.BlockSpec(memory_space=pltpu.VMEM), pl.BlockSpec(memory_space=pl.ANY)
     return pl.pallas_call(
-        head_kernel,
+        kernel,
         in_specs=[pl.BlockSpec(memory_space=pltpu.SMEM)] + [hbm] * len(arrays),
-        out_specs=[vmem] * 4,
-        out_shape=[shape((half, width)), shape((half, width), bf16)] * 2,
+        out_specs=[vmem, vmem],
+        out_shape=[shape((rows, width)), shape((rows, width), jnp.bfloat16)],
         scratch_shapes=[pltpu.VMEM(a.shape, a.dtype) for a in arrays]
-        + [
-            pltpu.VMEM((rows, width), bf16),
-            pltpu.VMEM((rows, hidden), bf16),
-            pltpu.VMEM((rows, width), jnp.float32),
-            pltpu.SemaphoreType.DMA((len(arrays),)),
-        ],
+        + scratch
+        + [pltpu.VMEM((2 * rows, width), jnp.float32), pltpu.SemaphoreType.DMA((len(arrays),))],
         compiler_params=pltpu.CompilerParams(vmem_limit_bytes=52 * 1024 * 1024),
-        cost_estimate=pl.CostEstimate(
-            flops=4 * rows * width * hidden, bytes_accessed=12 << 20, transcendentals=rows * hidden
-        ),
+        cost_estimate=pl.CostEstimate(flops=flops, bytes_accessed=11 << 20, transcendentals=0),
     )(pos, *arrays)
 
 
@@ -365,17 +365,23 @@
     pos = jnp.stack([p.astype(jnp.int32) for p in pos])
     cells = rows * width
 
-    own_img, other_img, own_text, other_text = heads(
+    own_text, other_text = from_hbm(
+        text_kernel, pos, [text_features, text_head[0]], rows, width, [], 2 * cells * width
+    )
+    recv_text = over_mp(other_text)
+    features, own_text = lax.optimization_barrier((image_features, own_text))
+    hidden = up_weight.shape[2]
+    own_img, other_img = from_hbm(
+        mlp_kernel,
         pos,
-        image_features,
-        norm_gain,
-        text_features,
-        text_head[0],
-        up_weight[0].T,
-        down_weight[0],
-    )
+        [features, norm_gain, up_weight[0].T, down_weight[0]],
+        rows,
+        width,
+        [pltpu.VMEM((2 * rows, width), bf16), pltpu.VMEM((2 * rows, hidden), bf16)],
+        8 * cells * hidden,
+    )
+    other_img, recv_text = lax.optimization_barrier((other_img, recv_text))
     recv_img = over_mp(other_img)
-    recv_text = over_mp(other_text)
     chosen, place_of = call(
         index_kernel, [], [sub_index.reshape(1, -1)], [shape((blocks, rows))] * 2, 100 << 20
     )
@@ -386,26 +392,21 @@
         [shape((rows, width), bf16), shape((rows, width)), shape((rows, rows))],
         20 * cells,
     )
-    own_text, z_img = lax.optimization_barrier((own_text, z_img))
     (z_txt,) = call(
         text_unit_kernel, [], [own_text, recv_text], [shape((rows, width), bf16)], 20 * cells
     )
     line = [z_txt] + [over_plane(z_txt, shift, 0) for shift in (1, -1, 2)]
+    z_img, *line = lax.optimization_barrier((z_img, *line))
     back, ahead = [z_img], [z_img]
 
     def z_step():
         back.append(over_z(back[-1], (1, 1)))
         ahead.append(over_z(ahead[-1], (-1, -1)))
 
-    z_step()
-    z_step()
-    line[0], back[2], ahead[2] = lax.optimization_barrier((line[0], back[2], ahead[2]))
     (joined,) = call(join_kernel, [], line, [shape((4 * rows, width), bf16)], cells)
     text_back, text_ahead = over_plane(joined, 1, 1), over_plane(joined, -1, 1)
-    z_step()
-    text_back, text_ahead, back[3], ahead[3] = lax.optimization_barrier(
-        (text_back, text_ahead, back[3], ahead[3])
-    )
+    for _ in range(3):
+        z_step()
     last = over_z(jnp.where(g_idx == 0, back[3], ahead[3]), (1, -1))
     far_top = over_plane(text_back[: 2 * rows], 1, 1)
     far_low = over_plane(text_ahead[2 * rows :], -1, 1)

time: 116 us -> 117 us (level)
  starting transfers between devices: 42.7 us -> 32.3 us
  waiting for transfers between devices: 41.2 us -> 48.2 us
  Pallas kernels: 28.4 us -> 30.9 us
  local copies, waits for them, and re-layouts: 2.6 us -> 3.89 us
    ppermute x17, starting transfers between devices: 39.1 us -> 28.6 us  [permute(): return lax.ppermute(v, AXES, perm)]
    all_to_all x1, waiting for transfers between devices: 12.2 us -> 17.1 us  [shards(): load = lax.all_to_all(load, 'z', 0, 0, tiled=True)]
    pallas_call x1 -> x2, Pallas kernels: 8 us -> 10.5 us  [from_hbm(): pl.pallas_call(kernel, in_specs=[pl.BlockSpec(memory_space=pltpu.SMEM)] +...]
    ppermute x17, waiting for transfers between devices: 29 us -> 31.1 us  [permute(): return lax.ppermute(v, AXES, perm)]
    unnamed x24 -> x28, local copies, waits for them, and re-layouts: 1.36 us -> 2.64 us
  transfers between devices with their start and end apart: 18 -> 18, of which waited for: 10 -> 11; matrix products, arithmetic and copies ran while one was open for 0% -> 1% of each run, Pallas kernels for 7% -> 14%
where the time goes in v4:
time: 117 us; the launch traced here: 116 us
  waiting for transfers between devices  48.2 us (41%)
  starting transfers between devices  32.3 us (28%)
  Pallas kernels  30.9 us (26%)
  local copies, waits for them, and re-layouts  3.89 us (3%)
    ppermute x17, waiting for transfers between devices, permute(): return lax.ppermute(v, AXES, perm)  31.1 us
    ppermute x17, starting transfers between devices, permute(): return lax.ppermute(v, AXES, perm)  28.6 us
    pallas_call x9, Pallas kernels, call(): pl.pallas_call(kernel, in_specs=[pl.BlockSpec(memory_space=pltpu.SMEM)] *...  20.3 us
    all_to_all x1, waiting for transfers between devices, shards(): load = lax.all_to_all(load, 'z', 0, 0, tiled=True)  17.1 us
    pallas_call x2, Pallas kernels, from_hbm(): pl.pallas_call(kernel, in_specs=[pl.BlockSpec(memory_space=pltpu.SMEM)] +...  10.5 us
    all_to_all x1, starting transfers between devices, shards(): load = lax.all_to_all(load, 'z', 0, 0, tiled=True)  3.67 us
    unnamed x28, local copies, waits for them, and re-layouts  2.64 us
  transfers between devices with their start and end apart: 18, of which 11 were waited for; matrix products, arithmetic and copies ran while one was open for 1% of the time, Pallas kernels for 14%

profile of v4, /device:TPU:1, one launch (start us, length us, event | category | flops | bytes accessed | tf_op | source)
XLA Modules:
  0.0 116.1 jit_solution(14957442513727224129)
XLA Ops:
  0.7 0.1 stack.27.pos_ref
  0.7 1.1 copy-done.1
  1.9 2.8 %shard_map.87 = (f32[128,1152]{1,0:T(8,128)S(1)}, bf16[128,1152]{1,0:T(8,128)(2,1)S(1)}) custom-call(s32[6]{0:T(128)S(1)} %stack.27.pos_ref, bf16[256,1152]{1,0:T(8,128)(2,1)S(1)} %copy-done.1, bf16[576,1152]{1,0:T(8,128)(2,1)} %bitcast.20), custom_call_target="tpu_custom_call" | custom-call | flops 339738624 | bytes 11534336 | tf_op jit(solution)/shard_map/pallas_call | solution.py:166
  4.7 3.8 %collective-permute-start = (bf16[128,1152]{1,0:T(8,128)(2,1)S(1)}, bf16[128,1152]{1,0:T(8,128)(2,1)S(1)}, u32[]{:S(2)}, u32[]{:S(2)}) collective-permute-start(bf16[128,1152]{1,0:T(8,128)(2,1)S(1)} %get-tuple-element.32), channel_id=1, source_target_pairs={{0,1},{2,3},{1,0},{3,2},{4,5},{6,7},{5,4},{7,6},{8,9},{10,11},{9,8... | collective-permute-start | bytes 884744 | tf_op jit(solution)/shard_map/ppermute | solution.py:35
  8.5 7.7 %shard_map.88 = (f32[128,1152]{1,0:T(8,128)S(1)}, bf16[128,1152]{1,0:T(8,128)(2,1)S(1)}) custom-call(s32[6]{0:T(128)S(1)} %stack.27.pos_ref, bf16[256,1152]{1,0:T(8,128)(2,1)S(1)} %copy-done, f32[1,1152]{1,0:T(1,128)S(1)} %copy-done.6, bf16[2152,1152]{1,0:T(8,128)(2,1)} %bitcast.18, bf16[2152,1152]{1,0:T(8,128)(2,1)} %bitcast.19), custom_call_target="tpu_custom_call" | custom-call | flops 2538602496 | bytes 11534336 | tf_op jit(solution)/shard_map/pallas_call | solution.py:166
  16.2 0.0 collective-permute-done.recv_ref
  16.2 1.6 %collective-permute-start.1 = (bf16[128,1152]{1,0:T(8,128)(2,1)S(1)}, bf16[128,1152]{1,0:T(8,128)(2,1)S(1)}, u32[]{:S(2)}, u32[]{:S(2)}) collective-permute-start(bf16[128,1152]{1,0:T(8,128)(2,1)S(1)} %get-tuple-element.33), channel_id=1, source_target_pairs={{0,1},{2,3},{1,0},{3,2},{4,5},{6,7},{5,4},{7,6},{8,9},{10,11},{9,8... | collective-permute-start | bytes 884744 | tf_op jit(solution)/shard_map/ppermute | solution.py:35
  17.9 0.2 shard_map.90.refs_0_
  18.0 1.5 %collective-permute-start.4 = (bf16[128,1152]{1,0:T(8,128)(2,1)S(1)}, bf16[128,1152]{1,0:T(8,128)(2,1)S(1)}, u32[]{:S(2)}, u32[]{:S(2)}) collective-permute-start(bf16[128,1152]{1,0:T(8,128)(2,1)S(1)} %shard_map.90.refs_0_), channel_id=1, source_target_pairs={{0,8},{2,10},{1,9},{3,11},{4,12},{6,14},{5,13},{7,15},{8,0},{10,2}... | collective-permute-start | bytes 884744 | tf_op jit(solution)/shard_map/ppermute | solution.py:35
  19.6 1.3 %collective-permute-start.3 = (bf16[128,1152]{1,0:T(8,128)(2,1)S(1)}, bf16[128,1152]{1,0:T(8,128)(2,1)S(1)}, u32[]{:S(2)}, u32[]{:S(2)}) collective-permute-start(bf16[128,1152]{1,0:T(8,128)(2,1)S(1)} %shard_map.90.refs_0_), channel_id=1, source_target_pairs={{0,12},{2,14},{1,13},{3,15},{4,0},{6,2},{5,1},{7,3},{8,4},{10,6},{... | collective-permute-start | bytes 884744 | tf_op jit(solution)/shard_map/ppermute | solution.py:35
  20.9 0.1 collective-permute-start.2
  21.0 4.4 %collective-permute-done.1.recv_ref = bf16[128,1152]{1,0:T(8,128)(2,1)S(1)} collective-permute-done((bf16[128,1152]{1,0:T(8,128)(2,1)S(1)}, bf16[128,1152]{1,0:T(8,128)(2,1)S(1)}, u32[]{:S(2)}, u32[]{:S(2)}) %collective-permute-start.1) | collective-permute-done | bytes 294944 | tf_op jit(solution)/shard_map/ppermute | solution.py:35
  25.4 0.2 shard_map.89
  25.6 0.0 copy-start.7
  25.6 4.2 %collective-permute-done.4.refs_3_ = bf16[128,1152]{1,0:T(8,128)(2,1)S(1)} collective-permute-done((bf16[128,1152]{1,0:T(8,128)(2,1)S(1)}, bf16[128,1152]{1,0:T(8,128)(2,1)S(1)}, u32[]{:S(2)}, u32[]{:S(2)}) %collective-permute-start.4) | collective-permute-done | bytes 294944 | tf_op jit(solution)/shard_map/ppermute | solution.py:35
  29.8 2.1 %collective-permute-done.3.refs_2_ = bf16[128,1152]{1,0:T(8,128)(2,1)S(1)} collective-permute-done((bf16[128,1152]{1,0:T(8,128)(2,1)S(1)}, bf16[128,1152]{1,0:T(8,128)(2,1)S(1)}, u32[]{:S(2)}, u32[]{:S(2)}) %collective-permute-start.3) | collective-permute-done | bytes 294944 | tf_op jit(solution)/shard_map/ppermute | solution.py:35
  31.9 1.0 collective-permute-done.2.refs_1_
  32.9 0.1 shard_map.91.refs_7_.refs_8_
  33.0 2.6 %collective-permute-start.12 = (bf16[512,1152]{1,0:T(8,128)(2,1)S(1)}, bf16[512,1152]{1,0:T(8,128)(2,1)S(1)}, u32[]{:S(2)}, u32[]{:S(2)}) collective-permute-start(bf16[512,1152]{1,0:T(8,128)(2,1)S(1)} %shard_map.91.refs_7_.refs_8_), channel_id=1, source_target_pairs={{0,3},{2,0},{1,2},{3,1},{4,7},{6,4},{5,6},{7,5},{8,11},{10,8},{9,1... | collective-permute-start | bytes 3538952 | tf_op jit(solution)/shard_map/ppermute | solution.py:35
  35.5 5.6 %collective-permute-start.6 = (bf16[128,1152]{1,0:T(8,128)(2,1)S(1)}, bf16[128,1152]{1,0:T(8,128)(2,1)S(1)}, u32[]{:S(2)}, u32[]{:S(2)}) collective-permute-start(bf16[128,1152]{1,0:T(8,128)(2,1)S(1)} %get-tuple-element.37.refs_0_), channel_id=1, source_target_pairs={{0,112},{2,114},{1,113},{3,115},{4,116},{6,118},{5,117},{7,119},{8... | collective-permute-start | bytes 884744 | tf_op jit(solution)/shard_map/ppermute | solution.py:35
  41.1 0.0 collective-permute-start.5
  41.1 6.0 %collective-permute-done.6.refs_2_ = bf16[128,1152]{1,0:T(8,128)(2,1)S(1)} collective-permute-done((bf16[128,1152]{1,0:T(8,128)(2,1)S(1)}, bf16[128,1152]{1,0:T(8,128)(2,1)S(1)}, u32[]{:S(2)}, u32[]{:S(2)}) %collective-permute-start.6) | collective-permute-done | bytes 294944 | tf_op jit(solution)/shard_map/ppermute | solution.py:35
  47.1 3.5 %collective-permute-start.8 = (bf16[128,1152]{1,0:T(8,128)(2,1)S(1)}, bf16[128,1152]{1,0:T(8,128)(2,1)}, u32[]{:S(2)}, u32[]{:S(2)}) collective-permute-start(bf16[128,1152]{1,0:T(8,128)(2,1)S(1)} %collective-permute-done.6.refs_2_), channel_id=1, source_target_pairs={{0,112},{2,114},{1,113},{3,115},{4,116},{6,118},{5,117},{7,119},{8... | collective-permute-start | bytes 884744 | tf_op jit(solution)/shard_map/ppermute | solution.py:35
  50.6 0.7 copy-done.9
  51.3 0.0 collective-permute-done.5.refs_1_
  51.4 0.7 copy-done.11
  52.1 5.4 %collective-permute-done.8.refs_4_ = bf16[128,1152]{1,0:T(8,128)(2,1)} collective-permute-done((bf16[128,1152]{1,0:T(8,128)(2,1)S(1)}, bf16[128,1152]{1,0:T(8,128)(2,1)}, u32[]{:S(2)}, u32[]{:S(2)}) %collective-permute-start.8) | collective-permute-done | bytes 294944 | tf_op jit(solution)/shard_map/ppermute | solution.py:35
  57.5 3.4 %collective-permute-start.10 = (bf16[128,1152]{1,0:T(8,128)(2,1)}, bf16[128,1152]{1,0:T(8,128)(2,1)S(1)}, u32[]{:S(2)}, u32[]{:S(2)}) collective-permute-start(bf16[128,1152]{1,0:T(8,128)(2,1)} %collective-permute-done.8.refs_4_), channel_id=1, source_target_pairs={{0,112},{2,114},{1,113},{3,115},{4,116},{6,118},{5,117},{7,119},{8... | collective-permute-start | bytes 884744 | tf_op jit(solution)/shard_map/ppermute | solution.py:35
  60.8 0.6 collective-permute-done.7.refs_3_
  61.5 0.0 copy-start.13
  61.5 0.0 copy-start.8
  61.6 1.0 collective-permute-start.15
  62.6 1.1 slice.8
  63.7 0.6 collective-permute-start.14
  64.3 2.8 %collective-permute-done.10.refs_6_ = bf16[128,1152]{1,0:T(8,128)(2,1)S(1)} collective-permute-done((bf16[128,1152]{1,0:T(8,128)(2,1)}, bf16[128,1152]{1,0:T(8,128)(2,1)S(1)}, u32[]{:S(2)}, u32[]{:S(2)}) %collective-permute-start.10) | collective-permute-done | bytes 294944 | tf_op jit(solution)/shard_map/ppermute | solution.py:35
  67.2 3.7 %collective-permute-done.9.refs_5_ = bf16[128,1152]{1,0:T(8,128)(2,1)S(1)} collective-permute-done((bf16[128,1152]{1,0:T(8,128)(2,1)}, bf16[128,1152]{1,0:T(8,128)(2,1)S(1)}, u32[]{:S(2)}, u32[]{:S(2)}) %collective-permute-start.9) | collective-permute-done | bytes 294944 | tf_op jit(solution)/shard_map/ppermute | solution.py:35
  70.9 0.3 collective-permute-start.13
  71.2 0.5 shard_map.86
  71.7 0.0 copy-start.2
  71.7 6.3 %shard_map.92.early_ref = f32[8,128]{1,0:T(8,128)S(1)} custom-call(bf16[128,1152]{1,0:T(8,128)(2,1)S(1)} %copy-done.8, bf16[128,1152]{1,0:T(8,128)(2,1)S(1)} %copy-done.12, bf16[128,1152]{1,0:T(8,128)(2,1)S(1)} %copy-done.10, bf16[128,1152]{1,0:T(8,128)(2,1)} %collective-permute-done.7.refs_3_, bf16[128,1152]{1,0:T(8,128)(2,1)} %collective-permute-done.8.refs_4_, ...), custom_call_target="tpu_custom_call" | custom-call | flops 2415919104 | bytes 1048576 | tf_op jit(solution)/shard_map/pallas_call | solution.py:65
  78.0 10.2 %shard_map.93 = bf16[256,1280]{1,0:T(8,128)(2,1)} custom-call(s32[6]{0:T(128)S(1)} %stack.27.pos_ref, f32[128,128]{1,0:T(8,128)S(1)} %get-tuple-element.26.chosen_ref, f32[128,128]{1,0:T(8,128)S(1)} %get-tuple-element.27.place_ref, f32[8,128]{1,0:T(8,128)S(1)} %shard_map.92.early_ref, bf16[128,1152]{1,0:T(8,128)(2,1)S(1)} %copy-done.8, ...), custom_call_target="tpu_custom_call" | custom-call | flops 4831838208 | bytes 1048576 | tf_op jit(solution)/shard_map/pallas_call | solution.py:65
  88.3 3.7 %all-to-all-start = ((bf16[8,32,1280]{2,1,0:T(8,128)(2,1)}), bf16[8,32,1280]{2,1,0:T(8,128)(2,1)S(1)}, u32[]{:S(2)}, u32[]{:S(2)}) async-start(bf16[8,32,1280]{2,1,0:T(8,128)(2,1)} %bitcast.11), calls=%async_computation | async-start | bytes 1310720 | tf_op jit(solution)/shard_map/all_to_all | solution.py:433
  92.0 1.0 shard_map.94
  93.0 17.1 %all-to-all-done = bf16[8,32,1280]{2,1,0:T(8,128)(2,1)S(1)} async-done(((bf16[8,32,1280]{2,1,0:T(8,128)(2,1)}), bf16[8,32,1280]{2,1,0:T(8,128)(2,1)S(1)}, u32[]{:S(2)}, u32[]{:S(2)}) %all-to-all-start) | async-done | bytes 655392 | tf_op jit(solution)/shard_map/all_to_all | solution.py:433
  110.0 0.2 shard_map.95
  110.3 3.2 %collective-permute-start.16 = (f32[40,576]{1,0:T(8,128)S(1)}, f32[40,576]{1,0:T(8,128)S(1)}, u32[]{:S(2)}, u32[]{:S(2)}) collective-permute-start(f32[40,576]{1,0:T(8,128)S(1)} %get-tuple-element.47), channel_id=1, source_target_pairs={{0,128},{2,130},{1,129},{3,131},{4,132},{6,134},{5,133},{7,135},{8... | collective-permute-start | bytes 276488 | tf_op jit(solution)/shard_map/ppermute | solution.py:35
  113.5 0.9 collective-permute-done.16.recv_ref
  114.4 1.7 %shard_map.96 = (f32[1,128]{1,0:T(1,128)}, f32[576,128]{1,0:T(8,128)}) custom-call(s32[6]{0:T(128)S(1)} %stack.27.pos_ref, f32[40,576]{1,0:T(8,128)S(1)} %get-tuple-element.46.keep_ref, f32[40,576]{1,0:T(8,128)S(1)} %collective-permute-done.16.recv_ref, f32[128,128]{1,0:T(8,128)S(1)} %copy-done.3), custom_call_target="tpu_custom_call" | custom-call | flops 29491200 | bytes 1048576 | tf_op jit(solution)/shard_map/pallas_call | solution.py:65
  (31 shorter events, 0.1 us)
Async XLA Ops:
  0.6 7.9 %copy-start = (bf16[256,1152]{1,0:T(8,128)(2,1)S(1)}, bf16[256,1152]{1,0:T(8,128)(2,1)}, u32[]{:S(2)}) copy-start(bf16[256,1152]{1,0:T(8,128)(2,1)} %x_hbm) | copy-start | bytes 1769476
  0.7 1.1 copy-start.1
  1.9 6.6 %copy-start.6 = (f32[1,1152]{1,0:T(1,128)S(1)}, f32[1,1152]{1,0:T(1,128)}, u32[]{:S(2)}) copy-start(f32[1,1152]{1,0:T(1,128)} %gain_hbm.1) | copy-start | bytes 13828
  4.7 11.6 %collective-permute-start = (bf16[128,1152]{1,0:T(8,128)(2,1)S(1)}, bf16[128,1152]{1,0:T(8,128)(2,1)S(1)}, u32[]{:S(2)}, u32[]{:S(2)}) collective-permute-start(bf16[128,1152]{1,0:T(8,128)(2,1)S(1)} %get-tuple-element.32), channel_id=1, source_target_pairs={{0,1},{2,3},{1,0},{3,2},{4,5},{6,7},{5,4},{7,6},{8,9},{10,11},{9,8... | collective-permute-start | bytes 884744 | tf_op jit(solution)/shard_map/ppermute | solution.py:35
  16.2 9.1 %collective-permute-start.1 = (bf16[128,1152]{1,0:T(8,128)(2,1)S(1)}, bf16[128,1152]{1,0:T(8,128)(2,1)S(1)}, u32[]{:S(2)}, u32[]{:S(2)}) collective-permute-start(bf16[128,1152]{1,0:T(8,128)(2,1)S(1)} %get-tuple-element.33), channel_id=1, source_target_pairs={{0,1},{2,3},{1,0},{3,2},{4,5},{6,7},{5,4},{7,6},{8,9},{10,11},{9,8... | collective-permute-start | bytes 884744 | tf_op jit(solution)/shard_map/ppermute | solution.py:35
  18.0 11.8 %collective-permute-start.4 = (bf16[128,1152]{1,0:T(8,128)(2,1)S(1)}, bf16[128,1152]{1,0:T(8,128)(2,1)S(1)}, u32[]{:S(2)}, u32[]{:S(2)}) collective-permute-start(bf16[128,1152]{1,0:T(8,128)(2,1)S(1)} %shard_map.90.refs_0_), channel_id=1, source_target_pairs={{0,8},{2,10},{1,9},{3,11},{4,12},{6,14},{5,13},{7,15},{8,0},{10,2}... | collective-permute-start | bytes 884744 | tf_op jit(solution)/shard_map/ppermute | solution.py:35
  19.6 12.3 %collective-permute-start.3 = (bf16[128,1152]{1,0:T(8,128)(2,1)S(1)}, bf16[128,1152]{1,0:T(8,128)(2,1)S(1)}, u32[]{:S(2)}, u32[]{:S(2)}) collective-permute-start(bf16[128,1152]{1,0:T(8,128)(2,1)S(1)} %shard_map.90.refs_0_), channel_id=1, source_target_pairs={{0,12},{2,14},{1,13},{3,15},{4,0},{6,2},{5,1},{7,3},{8,4},{10,6},{... | collective-permute-start | bytes 884744 | tf_op jit(solution)/shard_map/ppermute | solution.py:35
  20.9 12.0 %collective-permute-start.2 = (bf16[128,1152]{1,0:T(8,128)(2,1)S(1)}, bf16[128,1152]{1,0:T(8,128)(2,1)S(1)}, u32[]{:S(2)}, u32[]{:S(2)}) collective-permute-start(bf16[128,1152]{1,0:T(8,128)(2,1)S(1)} %shard_map.90.refs_0_), channel_id=1, source_target_pairs={{0,4},{2,6},{1,5},{3,7},{4,8},{6,10},{5,9},{7,11},{8,12},{10,14},{... | collective-permute-start | bytes 884744 | tf_op jit(solution)/shard_map/ppermute | solution.py:35
  25.6 35.3 %copy-start.4 = (f32[128,128]{1,0:T(8,128)}, f32[128,128]{1,0:T(8,128)S(1)}, u32[]{:S(2)}) copy-start(f32[128,128]{1,0:T(8,128)S(1)} %get-tuple-element.43.n_ref) | copy-start | bytes 196612
  25.6 35.9 %copy-start.7 = (bf16[128,1152]{1,0:T(8,128)(2,1)}, bf16[128,1152]{1,0:T(8,128)(2,1)S(1)}, u32[]{:S(2)}) copy-start(bf16[128,1152]{1,0:T(8,128)(2,1)S(1)} %get-tuple-element.37.refs_0_) | copy-start | bytes 884740
  33.0 28.5 %collective-permute-start.12 = (bf16[512,1152]{1,0:T(8,128)(2,1)S(1)}, bf16[512,1152]{1,0:T(8,128)(2,1)S(1)}, u32[]{:S(2)}, u32[]{:S(2)}) collective-permute-start(bf16[512,1152]{1,0:T(8,128)(2,1)S(1)} %shard_map.91.refs_7_.refs_8_), channel_id=1, source_target_pairs={{0,3},{2,0},{1,2},{3,1},{4,7},{6,4},{5,6},{7,5},{8,11},{10,8},{9,1... | collective-permute-start | bytes 3538952 | tf_op jit(solution)/shard_map/ppermute | solution.py:35
  35.5 27.0 %collective-permute-start.11 = (bf16[512,1152]{1,0:T(8,128)(2,1)S(1)}, bf16[512,1152]{1,0:T(8,128)(2,1)}, u32[]{:S(2)}, u32[]{:S(2)}) collective-permute-start(bf16[512,1152]{1,0:T(8,128)(2,1)S(1)} %shard_map.91.refs_7_.refs_8_), channel_id=1, source_target_pairs={{0,2},{2,1},{1,3},{3,0},{4,6},{6,5},{5,7},{7,4},{8,10},{10,9},{9,1... | collective-permute-start | bytes 3538952 | tf_op jit(solution)/shard_map/ppermute | solution.py:35
  35.5 11.6 %collective-permute-start.6 = (bf16[128,1152]{1,0:T(8,128)(2,1)S(1)}, bf16[128,1152]{1,0:T(8,128)(2,1)S(1)}, u32[]{:S(2)}, u32[]{:S(2)}) collective-permute-start(bf16[128,1152]{1,0:T(8,128)(2,1)S(1)} %get-tuple-element.37.refs_0_), channel_id=1, source_target_pairs={{0,112},{2,114},{1,113},{3,115},{4,116},{6,118},{5,117},{7,119},{8... | collective-permute-start | bytes 884744 | tf_op jit(solution)/shard_map/ppermute | solution.py:35
  41.1 10.2 %collective-permute-start.5 = (bf16[128,1152]{1,0:T(8,128)(2,1)S(1)}, bf16[128,1152]{1,0:T(8,128)(2,1)S(1)}, u32[]{:S(2)}, u32[]{:S(2)}) collective-permute-start(bf16[128,1152]{1,0:T(8,128)(2,1)S(1)} %get-tuple-element.37.refs_0_), channel_id=1, source_target_pairs={{0,16},{2,18},{1,17},{3,19},{4,20},{6,22},{5,21},{7,23},{8,24},{10... | collective-permute-start | bytes 884744 | tf_op jit(solution)/shard_map/ppermute | solution.py:35
  47.1 10.3 %collective-permute-start.8 = (bf16[128,1152]{1,0:T(8,128)(2,1)S(1)}, bf16[128,1152]{1,0:T(8,128)(2,1)}, u32[]{:S(2)}, u32[]{:S(2)}) collective-permute-start(bf16[128,1152]{1,0:T(8,128)(2,1)S(1)} %collective-permute-done.6.refs_2_), channel_id=1, source_target_pairs={{0,112},{2,114},{1,113},{3,115},{4,116},{6,118},{5,117},{7,119},{8... | collective-permute-start | bytes 884744 | tf_op jit(solution)/shard_map/ppermute | solution.py:35
  50.6 0.7 copy-start.9
  51.3 10.1 %collective-permute-start.7 = (bf16[128,1152]{1,0:T(8,128)(2,1)S(1)}, bf16[128,1152]{1,0:T(8,128)(2,1)}, u32[]{:S(2)}, u32[]{:S(2)}) collective-permute-start(bf16[128,1152]{1,0:T(8,128)(2,1)S(1)} %collective-permute-done.5.refs_1_), channel_id=1, source_target_pairs={{0,16},{2,18},{1,17},{3,19},{4,20},{6,22},{5,21},{7,23},{8,24},{10... | collective-permute-start | bytes 884744 | tf_op jit(solution)/shard_map/ppermute | solution.py:35
  51.3 0.8 copy-start.11
  57.5 9.7 %collective-permute-start.10 = (bf16[128,1152]{1,0:T(8,128)(2,1)}, bf16[128,1152]{1,0:T(8,128)(2,1)S(1)}, u32[]{:S(2)}, u32[]{:S(2)}) collective-permute-start(bf16[128,1152]{1,0:T(8,128)(2,1)} %collective-permute-done.8.refs_4_), channel_id=1, source_target_pairs={{0,112},{2,114},{1,113},{3,115},{4,116},{6,118},{5,117},{7,119},{8... | collective-permute-start | bytes 884744 | tf_op jit(solution)/shard_map/ppermute | solution.py:35
  61.5 9.4 %collective-permute-start.9 = (bf16[128,1152]{1,0:T(8,128)(2,1)}, bf16[128,1152]{1,0:T(8,128)(2,1)S(1)}, u32[]{:S(2)}, u32[]{:S(2)}) collective-permute-start(bf16[128,1152]{1,0:T(8,128)(2,1)} %collective-permute-done.7.refs_3_), channel_id=1, source_target_pairs={{0,16},{2,18},{1,17},{3,19},{4,20},{6,22},{5,21},{7,23},{8,24},{10... | collective-permute-start | bytes 884744 | tf_op jit(solution)/shard_map/ppermute | solution.py:35
  61.5 9.7 %copy-start.13 = (s32[2048]{0:T(1024)S(1)}, s32[2048]{0:T(1024)}, u32[]{:S(2)}) copy-start(s32[2048]{0:T(1024)} %param.13) | copy-start | bytes 24580
  61.5 10.1 %copy-start.8 = (bf16[128,1152]{1,0:T(8,128)(2,1)S(1)}, bf16[128,1152]{1,0:T(8,128)(2,1)}, u32[]{:S(2)}) copy-start(bf16[128,1152]{1,0:T(8,128)(2,1)} %copy-done.7) | copy-start | bytes 884740
  61.6 10.1 %copy-start.10 = (bf16[128,1152]{1,0:T(8,128)(2,1)S(1)}, bf16[128,1152]{1,0:T(8,128)(2,1)}, u32[]{:S(2)}) copy-start(bf16[128,1152]{1,0:T(8,128)(2,1)} %copy-done.9) | copy-start | bytes 884740
  61.6 10.1 %copy-start.12 = (bf16[128,1152]{1,0:T(8,128)(2,1)S(1)}, bf16[128,1152]{1,0:T(8,128)(2,1)}, u32[]{:S(2)}) copy-start(bf16[128,1152]{1,0:T(8,128)(2,1)} %copy-done.11) | copy-start | bytes 884740
  61.6 16.4 %collective-permute-start.15 = (bf16[256,1152]{1,0:T(8,128)(2,1)S(1)}, bf16[256,1152]{1,0:T(8,128)(2,1)S(1)}, u32[]{:S(2)}, u32[]{:S(2)}) collective-permute-start(bf16[256,1152]{1,0:T(8,128)(2,1)S(1)} %slice.9), channel_id=1, source_target_pairs={{0,3},{2,0},{1,2},{3,1},{4,7},{6,4},{5,6},{7,5},{8,11},{10,8},{9,1... | collective-permute-start | bytes 1769480 | tf_op jit(solution)/shard_map/ppermute | solution.py:35
  63.7 14.3 %collective-permute-start.14 = (bf16[256,1152]{1,0:T(8,128)(2,1)S(1)}, bf16[256,1152]{1,0:T(8,128)(2,1)S(1)}, u32[]{:S(2)}, u32[]{:S(2)}) collective-permute-start(bf16[256,1152]{1,0:T(8,128)(2,1)S(1)} %slice.8), channel_id=1, source_target_pairs={{0,2},{2,1},{1,3},{3,0},{4,6},{6,5},{5,7},{7,4},{8,10},{10,9},{9,1... | collective-permute-start | bytes 1769480 | tf_op jit(solution)/shard_map/ppermute | solution.py:35
  70.9 7.1 %collective-permute-start.13 = (bf16[128,1152]{1,0:T(8,128)(2,1)S(1)}, bf16[128,1152]{1,0:T(8,128)(2,1)S(1)}, u32[]{:S(2)}, u32[]{:S(2)}) collective-permute-start(bf16[128,1152]{1,0:T(8,128)(2,1)S(1)} %broadcast_select_fusion), channel_id=1, source_target_pairs={{0,16},{2,18},{1,17},{3,19},{4,20},{6,22},{5,21},{7,23},{8,24},{10... | collective-permute-start | bytes 884744 | tf_op jit(solution)/shard_map/ppermute | solution.py:35
  71.7 6.3 %copy-start.2 = (f32[128,128]{1,0:T(8,128)}, f32[128,128]{1,0:T(8,128)S(1)}, u32[]{:S(2)}) copy-start(f32[128,128]{1,0:T(8,128)S(1)} %get-tuple-element.27.place_ref) | copy-start | bytes 196612
  88.3 3.7 %copy-start.3 = (f32[128,128]{1,0:T(8,128)S(1)}, f32[128,128]{1,0:T(8,128)}, u32[]{:S(2)}) copy-start(f32[128,128]{1,0:T(8,128)} %copy-done.2) | copy-start | bytes 196612
  88.3 3.7 %copy-start.5 = (f32[128,128]{1,0:T(8,128)S(1)}, f32[128,128]{1,0:T(8,128)}, u32[]{:S(2)}) copy-start(f32[128,128]{1,0:T(8,128)} %copy-done.4) | copy-start | bytes 196612
  88.3 21.8 %all-to-all-start = ((bf16[8,32,1280]{2,1,0:T(8,128)(2,1)}), bf16[8,32,1280]{2,1,0:T(8,128)(2,1)S(1)}, u32[]{:S(2)}, u32[]{:S(2)}) async-start(bf16[8,32,1280]{2,1,0:T(8,128)(2,1)} %bitcast.11), calls=%async_computation | async-start | bytes 1310720 | tf_op jit(solution)/shard_map/all_to_all | solution.py:433
  110.3 4.1 %collective-permute-start.16 = (f32[40,576]{1,0:T(8,128)S(1)}, f32[40,576]{1,0:T(8,128)S(1)}, u32[]{:S(2)}, u32[]{:S(2)}) collective-permute-start(f32[40,576]{1,0:T(8,128)S(1)} %get-tuple-element.47), channel_id=1, source_target_pairs={{0,128},{2,130},{1,129},{3,131},{4,132},{6,134},{5,133},{7,135},{8... | collective-permute-start | bytes 276488 | tf_op jit(solution)/shard_map/ppermute | solution.py:35

commit v5 on v4

--- a/solution.py
+++ b/solution.py
@@ -12,7 +12,6 @@
 LN2 = 0.6931471805599453
 NZ, NX, NY = 8, 4, 4
 ROWS = 128
-BLOCK = 256
 CAP = 32
 AXES = ("grp", "z", "x", "ylo", "yhi")
 ZOFF = (0, -1, 1, -2, 2, -3, 3, 4)
@@ -236,25 +235,20 @@
     return lax.rem(z + (offset + NZ), NZ)
 
 
-def group_loss(images, pieces, own):
+def group_loss(images, texts, own):
     img = [r[...] for r in images]
     img = img[0] if len(img) == 1 else jnp.concatenate(img, axis=0)
     total = jnp.zeros((8, img.shape[0]), jnp.float32)
-    for k, (ref, start) in enumerate(pieces):
-        total = total + tile_loss(ref[start : start + BLOCK, :], img, own and k == 0)
+    for k, ref in enumerate(texts):
+        total = total + tile_loss(ref[...], img, own and k == 0)
     return jnp.sum(total, axis=0, keepdims=True)
-
-
-def text_pieces(refs):
-    return [(ref, start) for ref in refs for start in range(0, ref.shape[0], BLOCK)]
 
 
 def early_kernel(*refs):
     images, texts, out_ref = refs[: NZ - 1], refs[NZ - 1 : -1], refs[-1]
-    pieces = text_pieces(texts)
     for first in range(0, NZ - 1, 2):
         group = images[first : first + 2]
-        total = group_loss(group, pieces, first == 0)
+        total = group_loss(group, texts, first == 0)
         for k in range(len(group)):
             out_ref[first + k : first + k + 1, :] = total[:, k * ROWS : (k + 1) * ROWS]
     out_ref[NZ - 1 :, :] = jnp.zeros((1, ROWS), jnp.float32)
@@ -264,7 +258,6 @@
     images, texts, load_ref = refs[:NZ], refs[NZ:-1], refs[-1]
     z, x, y, xy = pos_ref[1], pos_ref[2], pos_ref[3], pos_ref[4]
     planes = NX * NY
-    pieces = text_pieces(texts)
 
     picks = [own_pick(place_ref[pl.ds(image_row(z, o) * planes + xy, 1), :]) for o in ZOFF]
     packed = jnp.concatenate(
@@ -282,9 +275,11 @@
 
     lines = [text_row(dx, dy) for dx in POFF for dy in POFF]
     total = jnp.zeros(packed.shape, jnp.float32)
-    for k, (ref, start) in enumerate(pieces):
-        text = ref[start : start + BLOCK, :]
-        mask = jnp.concatenate(lines[2 * k : 2 * k + 2], axis=1)
+    for k, ref in enumerate(texts):
+        text = ref[...]
+        count = text.shape[0] // ROWS
+        mask = jnp.concatenate(lines[:count], axis=1)
+        lines = lines[count:]
         t = lax.dot_general(
             packed, text, (((1,), (1,)), ((), ())), preferred_element_type=jnp.float32
         )
@@ -304,7 +299,7 @@
         rows = pl.ds(pl.multiple_of(image_row(z, o) * CAP, CAP), CAP)
         load_ref[rows, :width] = total[k * CAP : (k + 1) * CAP, :]
 
-    near, far = text_pieces(texts[:3]), text_pieces(texts[3:])
+    near, far = texts[:3], texts[3:]
     late = group_loss(images[NZ - 1 :], near, False)
     for first in range(0, NZ, 2):
         total = group_loss(images[first : first + 2], far, False)
@@ -396,17 +391,19 @@
         text_unit_kernel, [], [own_text, recv_text], [shape((rows, width), bf16)], 20 * cells
     )
     line = [z_txt] + [over_plane(z_txt, shift, 0) for shift in (1, -1, 2)]
-    z_img, *line = lax.optimization_barrier((z_img, *line))
+    z_img, line[3] = lax.optimization_barrier((z_img, line[3]))
     back, ahead = [z_img], [z_img]
 
     def z_step():
         back.append(over_z(back[-1], (1, 1)))
         ahead.append(over_z(ahead[-1], (-1, -1)))
 
+    z_step()
+    line[0], back[1], ahead[1] = lax.optimization_barrier((line[0], back[1], ahead[1]))
     (joined,) = call(join_kernel, [], line, [shape((4 * rows, width), bf16)], cells)
     text_back, text_ahead = over_plane(joined, 1, 1), over_plane(joined, -1, 1)
-    for _ in range(3):
-        z_step()
+    z_step()
+    z_step()
     last = over_z(jnp.where(g_idx == 0, back[3], ahead[3]), (1, -1))
     far_top = over_plane(text_back[: 2 * rows], 1, 1)
     far_low = over_plane(text_ahead[2 * rows :], -1, 1)

time: 117 us -> 114 us (0.974)
  waiting for transfers between devices: 48.2 us -> 44.4 us
  starting transfers between devices: 32.3 us -> 35 us
    ppermute x17, waiting for transfers between devices: 31.1 us -> 27.6 us  [permute(): return lax.ppermute(v, AXES, perm)]
    ppermute x17, starting transfers between devices: 28.6 us -> 31.3 us  [permute(): return lax.ppermute(v, AXES, perm)]
  transfers between devices with their start and end apart: 18 -> 18, of which waited for: 11 -> 9; matrix products, arithmetic and copies ran while one was open for 1% -> 1% of each run, Pallas kernels for 14% -> 14%
where the time goes in v5:
time: 114 us; the launch traced here: 113 us
  waiting for transfers between devices  44.4 us (39%)
  starting transfers between devices  35 us (31%)
  Pallas kernels  29.8 us (26%)
  local copies, waits for them, and re-layouts  3.03 us (3%)
    ppermute x17, starting transfers between devices, permute(): return lax.ppermute(v, AXES, perm)  31.3 us
    ppermute x17, waiting for transfers between devices, permute(): return lax.ppermute(v, AXES, perm)  27.6 us
    pallas_call x9, Pallas kernels, call(): pl.pallas_call(kernel, in_specs=[pl.BlockSpec(memory_space=pltpu.SMEM)] *...  19.3 us
    all_to_all x1, waiting for transfers between devices, shards(): load = lax.all_to_all(load, 'z', 0, 0, tiled=True)  16.8 us
    pallas_call x2, Pallas kernels, from_hbm(): pl.pallas_call(kernel, in_specs=[pl.BlockSpec(memory_space=pltpu.SMEM)] +...  10.5 us
    all_to_all x1, starting transfers between devices, shards(): load = lax.all_to_all(load, 'z', 0, 0, tiled=True)  3.67 us
  transfers between devices with their start and end apart: 18, of which 9 were waited for; matrix products, arithmetic and copies ran while one was open for 1% of the time, Pallas kernels for 14%

profile of v5, /device:TPU:1, one launch (start us, length us, event | category | flops | bytes accessed | tf_op | source)
XLA Modules:
  0.0 113.2 jit_solution(10410516967981964470)
XLA Ops:
  0.7 0.1 stack.27.pos_ref
  0.7 1.1 copy-done.1
  1.9 2.8 %shard_map.87 = (f32[128,1152]{1,0:T(8,128)S(1)}, bf16[128,1152]{1,0:T(8,128)(2,1)S(1)}) custom-call(s32[6]{0:T(128)S(1)} %stack.27.pos_ref, bf16[256,1152]{1,0:T(8,128)(2,1)S(1)} %copy-done.1, bf16[576,1152]{1,0:T(8,128)(2,1)} %bitcast.20), custom_call_target="tpu_custom_call" | custom-call | flops 339738624 | bytes 11534336 | tf_op jit(solution)/shard_map/pallas_call | solution.py:165
  4.7 3.8 %collective-permute-start = (bf16[128,1152]{1,0:T(8,128)(2,1)S(1)}, bf16[128,1152]{1,0:T(8,128)(2,1)S(1)}, u32[]{:S(2)}, u32[]{:S(2)}) collective-permute-start(bf16[128,1152]{1,0:T(8,128)(2,1)S(1)} %get-tuple-element.32), channel_id=1, source_target_pairs={{0,1},{2,3},{1,0},{3,2},{4,5},{6,7},{5,4},{7,6},{8,9},{10,11},{9,8... | collective-permute-start | bytes 884744 | tf_op jit(solution)/shard_map/ppermute | solution.py:34
  8.5 7.7 %shard_map.88 = (f32[128,1152]{1,0:T(8,128)S(1)}, bf16[128,1152]{1,0:T(8,128)(2,1)S(1)}) custom-call(s32[6]{0:T(128)S(1)} %stack.27.pos_ref, bf16[256,1152]{1,0:T(8,128)(2,1)S(1)} %copy-done, f32[1,1152]{1,0:T(1,128)S(1)} %copy-done.6, bf16[2152,1152]{1,0:T(8,128)(2,1)} %bitcast.18, bf16[2152,1152]{1,0:T(8,128)(2,1)} %bitcast.19), custom_call_target="tpu_custom_call" | custom-call | flops 2538602496 | bytes 11534336 | tf_op jit(solution)/shard_map/pallas_call | solution.py:165
  16.2 1.6 %collective-permute-start.1 = (bf16[128,1152]{1,0:T(8,128)(2,1)S(1)}, bf16[128,1152]{1,0:T(8,128)(2,1)S(1)}, u32[]{:S(2)}, u32[]{:S(2)}) collective-permute-start(bf16[128,1152]{1,0:T(8,128)(2,1)S(1)} %get-tuple-element.33), channel_id=1, source_target_pairs={{0,1},{2,3},{1,0},{3,2},{4,5},{6,7},{5,4},{7,6},{8,9},{10,11},{9,8... | collective-permute-start | bytes 884744 | tf_op jit(solution)/shard_map/ppermute | solution.py:34
  17.9 0.2 shard_map.90.refs_0_
  18.0 1.5 %collective-permute-start.2 = (bf16[128,1152]{1,0:T(8,128)(2,1)S(1)}, bf16[128,1152]{1,0:T(8,128)(2,1)S(1)}, u32[]{:S(2)}, u32[]{:S(2)}) collective-permute-start(bf16[128,1152]{1,0:T(8,128)(2,1)S(1)} %shard_map.90.refs_0_), channel_id=1, source_target_pairs={{0,8},{2,10},{1,9},{3,11},{4,12},{6,14},{5,13},{7,15},{8,0},{10,2}... | collective-permute-start | bytes 884744 | tf_op jit(solution)/shard_map/ppermute | solution.py:34
  19.6 5.8 %collective-permute-done.1.recv_ref = bf16[128,1152]{1,0:T(8,128)(2,1)S(1)} collective-permute-done((bf16[128,1152]{1,0:T(8,128)(2,1)S(1)}, bf16[128,1152]{1,0:T(8,128)(2,1)S(1)}, u32[]{:S(2)}, u32[]{:S(2)}) %collective-permute-start.1) | collective-permute-done | bytes 294944 | tf_op jit(solution)/shard_map/ppermute | solution.py:34
  25.4 0.2 shard_map.89
  25.6 0.6 copy-done.4
  26.2 3.5 %collective-permute-done.2.refs_3_ = bf16[128,1152]{1,0:T(8,128)(2,1)S(1)} collective-permute-done((bf16[128,1152]{1,0:T(8,128)(2,1)S(1)}, bf16[128,1152]{1,0:T(8,128)(2,1)S(1)}, u32[]{:S(2)}, u32[]{:S(2)}) %collective-permute-start.2) | collective-permute-done | bytes 294944 | tf_op jit(solution)/shard_map/ppermute | solution.py:34
  29.7 5.6 %collective-permute-start.4 = (bf16[128,1152]{1,0:T(8,128)(2,1)S(1)}, bf16[128,1152]{1,0:T(8,128)(2,1)S(1)}, u32[]{:S(2)}, u32[]{:S(2)}) collective-permute-start(bf16[128,1152]{1,0:T(8,128)(2,1)S(1)} %get-tuple-element.37.refs_0_), channel_id=1, source_target_pairs={{0,112},{2,114},{1,113},{3,115},{4,116},{6,118},{5,117},{7,119},{8... | collective-permute-start | bytes 884744 | tf_op jit(solution)/shard_map/ppermute | solution.py:34
  35.3 0.0 collective-permute-start.3
  35.3 1.3 %collective-permute-start.10 = (bf16[128,1152]{1,0:T(8,128)(2,1)S(1)}, bf16[128,1152]{1,0:T(8,128)(2,1)S(1)}, u32[]{:S(2)}, u32[]{:S(2)}) collective-permute-start(bf16[128,1152]{1,0:T(8,128)(2,1)S(1)} %shard_map.90.refs_0_), channel_id=1, source_target_pairs={{0,12},{2,14},{1,13},{3,15},{4,0},{6,2},{5,1},{7,3},{8,4},{10,6},{... | collective-permute-start | bytes 884744 | tf_op jit(solution)/shard_map/ppermute | solution.py:34
  36.7 0.1 collective-permute-start.9
  36.8 5.1 %collective-permute-done.4.refs_2_ = bf16[128,1152]{1,0:T(8,128)(2,1)S(1)} collective-permute-done((bf16[128,1152]{1,0:T(8,128)(2,1)S(1)}, bf16[128,1152]{1,0:T(8,128)(2,1)S(1)}, u32[]{:S(2)}, u32[]{:S(2)}) %collective-permute-start.4) | collective-permute-done | bytes 294944 | tf_op jit(solution)/shard_map/ppermute | solution.py:34
  41.9 3.2 %collective-permute-done.3.refs_1_ = bf16[128,1152]{1,0:T(8,128)(2,1)S(1)} collective-permute-done((bf16[128,1152]{1,0:T(8,128)(2,1)S(1)}, bf16[128,1152]{1,0:T(8,128)(2,1)S(1)}, u32[]{:S(2)}, u32[]{:S(2)}) %collective-permute-start.3) | collective-permute-done | bytes 294944 | tf_op jit(solution)/shard_map/ppermute | solution.py:34
  45.1 0.1 shard_map.91.refs_7_.refs_8_
  45.2 2.6 %collective-permute-start.12 = (bf16[512,1152]{1,0:T(8,128)(2,1)S(1)}, bf16[512,1152]{1,0:T(8,128)(2,1)S(1)}, u32[]{:S(2)}, u32[]{:S(2)}) collective-permute-start(bf16[512,1152]{1,0:T(8,128)(2,1)S(1)} %shard_map.91.refs_7_.refs_8_), channel_id=1, source_target_pairs={{0,3},{2,0},{1,2},{3,1},{4,7},{6,4},{5,6},{7,5},{8,11},{10,8},{9,1... | collective-permute-start | bytes 3538952 | tf_op jit(solution)/shard_map/ppermute | solution.py:34
  47.7 0.0 collective-permute-start.11
  47.8 0.0 collective-permute-start.5
  47.8 2.7 %collective-permute-start.6 = (bf16[128,1152]{1,0:T(8,128)(2,1)S(1)}, bf16[128,1152]{1,0:T(8,128)(2,1)}, u32[]{:S(2)}, u32[]{:S(2)}) collective-permute-start(bf16[128,1152]{1,0:T(8,128)(2,1)S(1)} %collective-permute-done.4.refs_2_), channel_id=1, source_target_pairs={{0,112},{2,114},{1,113},{3,115},{4,116},{6,118},{5,117},{7,119},{8... | collective-permute-start | bytes 884744 | tf_op jit(solution)/shard_map/ppermute | solution.py:34
  50.4 6.4 %collective-permute-done.5.refs_3_ = bf16[128,1152]{1,0:T(8,128)(2,1)} collective-permute-done((bf16[128,1152]{1,0:T(8,128)(2,1)S(1)}, bf16[128,1152]{1,0:T(8,128)(2,1)}, u32[]{:S(2)}, u32[]{:S(2)}) %collective-permute-start.5) | collective-permute-done | bytes 294944 | tf_op jit(solution)/shard_map/ppermute | solution.py:34
  56.9 0.0 collective-permute-done.6.refs_4_
  56.9 2.7 %collective-permute-start.8 = (bf16[128,1152]{1,0:T(8,128)(2,1)}, bf16[128,1152]{1,0:T(8,128)(2,1)S(1)}, u32[]{:S(2)}, u32[]{:S(2)}) collective-permute-start(bf16[128,1152]{1,0:T(8,128)(2,1)} %collective-permute-done.6.refs_4_), channel_id=1, source_target_pairs={{0,112},{2,114},{1,113},{3,115},{4,116},{6,118},{5,117},{7,119},{8... | collective-permute-start | bytes 884744 | tf_op jit(solution)/shard_map/ppermute | solution.py:34
  59.6 1.3 %collective-permute-done.12.refs_9_.refs_10_ = bf16[512,1152]{1,0:T(8,128)(2,1)S(1)} collective-permute-done((bf16[512,1152]{1,0:T(8,128)(2,1)S(1)}, bf16[512,1152]{1,0:T(8,128)(2,1)S(1)}, u32[]{:S(2)}, u32[]{:S(2)}) %collective-permute-start.12) | collective-permute-done | bytes 1179680 | tf_op jit(solution)/shard_map/ppermute | solution.py:34
  60.9 0.0 copy-start.13
  61.0 0.0 copy-start.8
  61.0 3.6 %collective-permute-start.15 = (bf16[256,1152]{1,0:T(8,128)(2,1)S(1)}, bf16[256,1152]{1,0:T(8,128)(2,1)S(1)}, u32[]{:S(2)}, u32[]{:S(2)}) collective-permute-start(bf16[256,1152]{1,0:T(8,128)(2,1)S(1)} %slice.9), channel_id=1, source_target_pairs={{0,3},{2,0},{1,2},{3,1},{4,7},{6,4},{5,6},{7,5},{8,11},{10,8},{9,1... | collective-permute-start | bytes 1769480 | tf_op jit(solution)/shard_map/ppermute | solution.py:34
  64.6 1.1 slice.8
  65.7 0.1 collective-permute-start.14
  65.8 0.0 collective-permute-done.7.refs_5_
  65.8 0.0 collective-permute-done.8.refs_6_
  65.9 2.2 %collective-permute-start.13 = (bf16[128,1152]{1,0:T(8,128)(2,1)S(1)}, bf16[128,1152]{1,0:T(8,128)(2,1)S(1)}, u32[]{:S(2)}, u32[]{:S(2)}) collective-permute-start(bf16[128,1152]{1,0:T(8,128)(2,1)S(1)} %broadcast_select_fusion), channel_id=1, source_target_pairs={{0,16},{2,18},{1,17},{3,19},{4,20},{6,22},{5,21},{7,23},{8,24},{10... | collective-permute-start | bytes 884744 | tf_op jit(solution)/shard_map/ppermute | solution.py:34
  68.1 0.5 shard_map.86
  68.6 0.0 copy-start.2
  68.6 6.2 %shard_map.92.early_ref = f32[8,128]{1,0:T(8,128)S(1)} custom-call(bf16[128,1152]{1,0:T(8,128)(2,1)S(1)} %copy-done.8, bf16[128,1152]{1,0:T(8,128)(2,1)S(1)} %copy-done.12, bf16[128,1152]{1,0:T(8,128)(2,1)S(1)} %copy-done.10, bf16[128,1152]{1,0:T(8,128)(2,1)} %collective-permute-done.5.refs_3_, bf16[128,1152]{1,0:T(8,128)(2,1)} %collective-permute-done.6.refs_4_, ...), custom_call_target="tpu_custom_call" | custom-call | flops 2415919104 | bytes 1048576 | tf_op jit(solution)/shard_map/pallas_call | solution.py:64
  74.7 0.0 collective-permute-done.13.refs_7_
  74.8 1.3 %collective-permute-done.14.refs_11_ = bf16[256,1152]{1,0:T(8,128)(2,1)S(1)} collective-permute-done((bf16[256,1152]{1,0:T(8,128)(2,1)S(1)}, bf16[256,1152]{1,0:T(8,128)(2,1)S(1)}, u32[]{:S(2)}, u32[]{:S(2)}) %collective-permute-start.14) | collective-permute-done | bytes 589856 | tf_op jit(solution)/shard_map/ppermute | solution.py:34
  76.0 9.3 %shard_map.93 = bf16[256,1280]{1,0:T(8,128)(2,1)} custom-call(s32[6]{0:T(128)S(1)} %stack.27.pos_ref, f32[128,128]{1,0:T(8,128)S(1)} %get-tuple-element.26.chosen_ref, f32[128,128]{1,0:T(8,128)S(1)} %get-tuple-element.27.place_ref, f32[8,128]{1,0:T(8,128)S(1)} %shard_map.92.early_ref, bf16[128,1152]{1,0:T(8,128)(2,1)S(1)} %copy-done.8, ...), custom_call_target="tpu_custom_call" | custom-call | flops 4831838208 | bytes 1048576 | tf_op jit(solution)/shard_map/pallas_call | solution.py:64
  85.3 3.7 %all-to-all-start = ((bf16[8,32,1280]{2,1,0:T(8,128)(2,1)}), bf16[8,32,1280]{2,1,0:T(8,128)(2,1)S(1)}, u32[]{:S(2)}, u32[]{:S(2)}) async-start(bf16[8,32,1280]{2,1,0:T(8,128)(2,1)} %bitcast.11), calls=%async_computation | async-start | bytes 1310720 | tf_op jit(solution)/shard_map/all_to_all | solution.py:430
  89.0 1.0 shard_map.94
  90.0 16.8 %all-to-all-done = bf16[8,32,1280]{2,1,0:T(8,128)(2,1)S(1)} async-done(((bf16[8,32,1280]{2,1,0:T(8,128)(2,1)}), bf16[8,32,1280]{2,1,0:T(8,128)(2,1)S(1)}, u32[]{:S(2)}, u32[]{:S(2)}) %all-to-all-start) | async-done | bytes 655392 | tf_op jit(solution)/shard_map/all_to_all | solution.py:430
  106.9 0.2 shard_map.95
  107.1 3.4 %collective-permute-start.16 = (f32[40,576]{1,0:T(8,128)S(1)}, f32[40,576]{1,0:T(8,128)S(1)}, u32[]{:S(2)}, u32[]{:S(2)}) collective-permute-start(f32[40,576]{1,0:T(8,128)S(1)} %get-tuple-element.47), channel_id=1, source_target_pairs={{0,128},{2,130},{1,129},{3,131},{4,132},{6,134},{5,133},{7,135},{8... | collective-permute-start | bytes 276488 | tf_op jit(solution)/shard_map/ppermute | solution.py:34
  110.5 0.9 collective-permute-done.16.recv_ref
  111.5 1.7 %shard_map.96 = (f32[1,128]{1,0:T(1,128)}, f32[576,128]{1,0:T(8,128)}) custom-call(s32[6]{0:T(128)S(1)} %stack.27.pos_ref, f32[40,576]{1,0:T(8,128)S(1)} %get-tuple-element.46.keep_ref, f32[40,576]{1,0:T(8,128)S(1)} %collective-permute-done.16.recv_ref, f32[128,128]{1,0:T(8,128)S(1)} %copy-done.3), custom_call_target="tpu_custom_call" | custom-call | flops 29491200 | bytes 1048576 | tf_op jit(solution)/shard_map/pallas_call | solution.py:64
  (31 shorter events, 0.1 us)
Async XLA Ops:
  0.6 7.9 %copy-start = (bf16[256,1152]{1,0:T(8,128)(2,1)S(1)}, bf16[256,1152]{1,0:T(8,128)(2,1)}, u32[]{:S(2)}) copy-start(bf16[256,1152]{1,0:T(8,128)(2,1)} %x_hbm) | copy-start | bytes 1769476
  0.7 1.1 copy-start.1
  1.9 6.6 %copy-start.6 = (f32[1,1152]{1,0:T(1,128)S(1)}, f32[1,1152]{1,0:T(1,128)}, u32[]{:S(2)}) copy-start(f32[1,1152]{1,0:T(1,128)} %gain_hbm.1) | copy-start | bytes 13828
  4.7 11.6 %collective-permute-start = (bf16[128,1152]{1,0:T(8,128)(2,1)S(1)}, bf16[128,1152]{1,0:T(8,128)(2,1)S(1)}, u32[]{:S(2)}, u32[]{:S(2)}) collective-permute-start(bf16[128,1152]{1,0:T(8,128)(2,1)S(1)} %get-tuple-element.32), channel_id=1, source_target_pairs={{0,1},{2,3},{1,0},{3,2},{4,5},{6,7},{5,4},{7,6},{8,9},{10,11},{9,8... | collective-permute-start | bytes 884744 | tf_op jit(solution)/shard_map/ppermute | solution.py:34
  16.2 9.1 %collective-permute-start.1 = (bf16[128,1152]{1,0:T(8,128)(2,1)S(1)}, bf16[128,1152]{1,0:T(8,128)(2,1)S(1)}, u32[]{:S(2)}, u32[]{:S(2)}) collective-permute-start(bf16[128,1152]{1,0:T(8,128)(2,1)S(1)} %get-tuple-element.33), channel_id=1, source_target_pairs={{0,1},{2,3},{1,0},{3,2},{4,5},{6,7},{5,4},{7,6},{8,9},{10,11},{9,8... | collective-permute-start | bytes 884744 | tf_op jit(solution)/shard_map/ppermute | solution.py:34
  18.0 11.7 %collective-permute-start.2 = (bf16[128,1152]{1,0:T(8,128)(2,1)S(1)}, bf16[128,1152]{1,0:T(8,128)(2,1)S(1)}, u32[]{:S(2)}, u32[]{:S(2)}) collective-permute-start(bf16[128,1152]{1,0:T(8,128)(2,1)S(1)} %shard_map.90.refs_0_), channel_id=1, source_target_pairs={{0,8},{2,10},{1,9},{3,11},{4,12},{6,14},{5,13},{7,15},{8,0},{10,2}... | collective-permute-start | bytes 884744 | tf_op jit(solution)/shard_map/ppermute | solution.py:34
  25.6 0.6 copy-start.4
  26.2 30.6 %copy-start.7 = (bf16[128,1152]{1,0:T(8,128)(2,1)}, bf16[128,1152]{1,0:T(8,128)(2,1)S(1)}, u32[]{:S(2)}) copy-start(bf16[128,1152]{1,0:T(8,128)(2,1)S(1)} %get-tuple-element.37.refs_0_) | copy-start | bytes 884740
  29.7 12.1 %collective-permute-start.4 = (bf16[128,1152]{1,0:T(8,128)(2,1)S(1)}, bf16[128,1152]{1,0:T(8,128)(2,1)S(1)}, u32[]{:S(2)}, u32[]{:S(2)}) collective-permute-start(bf16[128,1152]{1,0:T(8,128)(2,1)S(1)} %get-tuple-element.37.refs_0_), channel_id=1, source_target_pairs={{0,112},{2,114},{1,113},{3,115},{4,116},{6,118},{5,117},{7,119},{8... | collective-permute-start | bytes 884744 | tf_op jit(solution)/shard_map/ppermute | solution.py:34
  35.3 9.8 %collective-permute-start.3 = (bf16[128,1152]{1,0:T(8,128)(2,1)S(1)}, bf16[128,1152]{1,0:T(8,128)(2,1)S(1)}, u32[]{:S(2)}, u32[]{:S(2)}) collective-permute-start(bf16[128,1152]{1,0:T(8,128)(2,1)S(1)} %get-tuple-element.37.refs_0_), channel_id=1, source_target_pairs={{0,16},{2,18},{1,17},{3,19},{4,20},{6,22},{5,21},{7,23},{8,24},{10... | collective-permute-start | bytes 884744 | tf_op jit(solution)/shard_map/ppermute | solution.py:34
  35.3 9.8 %collective-permute-start.10 = (bf16[128,1152]{1,0:T(8,128)(2,1)S(1)}, bf16[128,1152]{1,0:T(8,128)(2,1)S(1)}, u32[]{:S(2)}, u32[]{:S(2)}) collective-permute-start(bf16[128,1152]{1,0:T(8,128)(2,1)S(1)} %shard_map.90.refs_0_), channel_id=1, source_target_pairs={{0,12},{2,14},{1,13},{3,15},{4,0},{6,2},{5,1},{7,3},{8,4},{10,6},{... | collective-permute-start | bytes 884744 | tf_op jit(solution)/shard_map/ppermute | solution.py:34
  36.7 8.4 %collective-permute-start.9 = (bf16[128,1152]{1,0:T(8,128)(2,1)S(1)}, bf16[128,1152]{1,0:T(8,128)(2,1)S(1)}, u32[]{:S(2)}, u32[]{:S(2)}) collective-permute-start(bf16[128,1152]{1,0:T(8,128)(2,1)S(1)} %shard_map.90.refs_0_), channel_id=1, source_target_pairs={{0,4},{2,6},{1,5},{3,7},{4,8},{6,10},{5,9},{7,11},{8,12},{10,14},{... | collective-permute-start | bytes 884744 | tf_op jit(solution)/shard_map/ppermute | solution.py:34
  41.9 15.0 %copy-start.9 = (bf16[128,1152]{1,0:T(8,128)(2,1)}, bf16[128,1152]{1,0:T(8,128)(2,1)S(1)}, u32[]{:S(2)}) copy-start(bf16[128,1152]{1,0:T(8,128)(2,1)S(1)} %collective-permute-done.4.refs_2_) | copy-start | bytes 884740
  45.1 5.3 %copy-start.11 = (bf16[128,1152]{1,0:T(8,128)(2,1)}, bf16[128,1152]{1,0:T(8,128)(2,1)S(1)}, u32[]{:S(2)}) copy-start(bf16[128,1152]{1,0:T(8,128)(2,1)S(1)} %collective-permute-done.3.refs_1_) | copy-start | bytes 884740
  45.2 15.7 %collective-permute-start.12 = (bf16[512,1152]{1,0:T(8,128)(2,1)S(1)}, bf16[512,1152]{1,0:T(8,128)(2,1)S(1)}, u32[]{:S(2)}, u32[]{:S(2)}) collective-permute-start(bf16[512,1152]{1,0:T(8,128)(2,1)S(1)} %shard_map.91.refs_7_.refs_8_), channel_id=1, source_target_pairs={{0,3},{2,0},{1,2},{3,1},{4,7},{6,4},{5,6},{7,5},{8,11},{10,8},{9,1... | collective-permute-start | bytes 3538952 | tf_op jit(solution)/shard_map/ppermute | solution.py:34
  47.7 16.8 %collective-permute-start.11 = (bf16[512,1152]{1,0:T(8,128)(2,1)S(1)}, bf16[512,1152]{1,0:T(8,128)(2,1)}, u32[]{:S(2)}, u32[]{:S(2)}) collective-permute-start(bf16[512,1152]{1,0:T(8,128)(2,1)S(1)} %shard_map.91.refs_7_.refs_8_), channel_id=1, source_target_pairs={{0,2},{2,1},{1,3},{3,0},{4,6},{6,5},{5,7},{7,4},{8,10},{10,9},{9,1... | collective-permute-start | bytes 3538952 | tf_op jit(solution)/shard_map/ppermute | solution.py:34
  47.8 9.1 %collective-permute-start.5 = (bf16[128,1152]{1,0:T(8,128)(2,1)S(1)}, bf16[128,1152]{1,0:T(8,128)(2,1)}, u32[]{:S(2)}, u32[]{:S(2)}) collective-permute-start(bf16[128,1152]{1,0:T(8,128)(2,1)S(1)} %collective-permute-done.3.refs_1_), channel_id=1, source_target_pairs={{0,16},{2,18},{1,17},{3,19},{4,20},{6,22},{5,21},{7,23},{8,24},{10... | collective-permute-start | bytes 884744 | tf_op jit(solution)/shard_map/ppermute | solution.py:34
  47.8 9.1 %collective-permute-start.6 = (bf16[128,1152]{1,0:T(8,128)(2,1)S(1)}, bf16[128,1152]{1,0:T(8,128)(2,1)}, u32[]{:S(2)}, u32[]{:S(2)}) collective-permute-start(bf16[128,1152]{1,0:T(8,128)(2,1)S(1)} %collective-permute-done.4.refs_2_), channel_id=1, source_target_pairs={{0,112},{2,114},{1,113},{3,115},{4,116},{6,118},{5,117},{7,119},{8... | collective-permute-start | bytes 884744 | tf_op jit(solution)/shard_map/ppermute | solution.py:34
  56.9 8.9 %collective-permute-start.7 = (bf16[128,1152]{1,0:T(8,128)(2,1)}, bf16[128,1152]{1,0:T(8,128)(2,1)S(1)}, u32[]{:S(2)}, u32[]{:S(2)}) collective-permute-start(bf16[128,1152]{1,0:T(8,128)(2,1)} %collective-permute-done.5.refs_3_), channel_id=1, source_target_pairs={{0,16},{2,18},{1,17},{3,19},{4,20},{6,22},{5,21},{7,23},{8,24},{10... | collective-permute-start | bytes 884744 | tf_op jit(solution)/shard_map/ppermute | solution.py:34
  56.9 8.9 %collective-permute-start.8 = (bf16[128,1152]{1,0:T(8,128)(2,1)}, bf16[128,1152]{1,0:T(8,128)(2,1)S(1)}, u32[]{:S(2)}, u32[]{:S(2)}) collective-permute-start(bf16[128,1152]{1,0:T(8,128)(2,1)} %collective-permute-done.6.refs_4_), channel_id=1, source_target_pairs={{0,112},{2,114},{1,113},{3,115},{4,116},{6,118},{5,117},{7,119},{8... | collective-permute-start | bytes 884744 | tf_op jit(solution)/shard_map/ppermute | solution.py:34
  60.9 7.1 %copy-start.13 = (s32[2048]{0:T(1024)S(1)}, s32[2048]{0:T(1024)}, u32[]{:S(2)}) copy-start(s32[2048]{0:T(1024)} %param.13) | copy-start | bytes 24580
  61.0 7.6 %copy-start.8 = (bf16[128,1152]{1,0:T(8,128)(2,1)S(1)}, bf16[128,1152]{1,0:T(8,128)(2,1)}, u32[]{:S(2)}) copy-start(bf16[128,1152]{1,0:T(8,128)(2,1)} %copy-done.7) | copy-start | bytes 884740
  61.0 7.6 %copy-start.10 = (bf16[128,1152]{1,0:T(8,128)(2,1)S(1)}, bf16[128,1152]{1,0:T(8,128)(2,1)}, u32[]{:S(2)}) copy-start(bf16[128,1152]{1,0:T(8,128)(2,1)} %copy-done.9) | copy-start | bytes 884740
  61.0 7.6 %copy-start.12 = (bf16[128,1152]{1,0:T(8,128)(2,1)S(1)}, bf16[128,1152]{1,0:T(8,128)(2,1)}, u32[]{:S(2)}) copy-start(bf16[128,1152]{1,0:T(8,128)(2,1)} %copy-done.11) | copy-start | bytes 884740
  61.0 13.8 %collective-permute-start.15 = (bf16[256,1152]{1,0:T(8,128)(2,1)S(1)}, bf16[256,1152]{1,0:T(8,128)(2,1)S(1)}, u32[]{:S(2)}, u32[]{:S(2)}) collective-permute-start(bf16[256,1152]{1,0:T(8,128)(2,1)S(1)} %slice.9), channel_id=1, source_target_pairs={{0,3},{2,0},{1,2},{3,1},{4,7},{6,4},{5,6},{7,5},{8,11},{10,8},{9,1... | collective-permute-start | bytes 1769480 | tf_op jit(solution)/shard_map/ppermute | solution.py:34
  65.7 10.3 %collective-permute-start.14 = (bf16[256,1152]{1,0:T(8,128)(2,1)S(1)}, bf16[256,1152]{1,0:T(8,128)(2,1)S(1)}, u32[]{:S(2)}, u32[]{:S(2)}) collective-permute-start(bf16[256,1152]{1,0:T(8,128)(2,1)S(1)} %slice.8), channel_id=1, source_target_pairs={{0,2},{2,1},{1,3},{3,0},{4,6},{6,5},{5,7},{7,4},{8,10},{10,9},{9,1... | collective-permute-start | bytes 1769480 | tf_op jit(solution)/shard_map/ppermute | solution.py:34
  65.9 8.9 %collective-permute-start.13 = (bf16[128,1152]{1,0:T(8,128)(2,1)S(1)}, bf16[128,1152]{1,0:T(8,128)(2,1)S(1)}, u32[]{:S(2)}, u32[]{:S(2)}) collective-permute-start(bf16[128,1152]{1,0:T(8,128)(2,1)S(1)} %broadcast_select_fusion), channel_id=1, source_target_pairs={{0,16},{2,18},{1,17},{3,19},{4,20},{6,22},{5,21},{7,23},{8,24},{10... | collective-permute-start | bytes 884744 | tf_op jit(solution)/shard_map/ppermute | solution.py:34
  68.6 7.4 %copy-start.2 = (f32[128,128]{1,0:T(8,128)}, f32[128,128]{1,0:T(8,128)S(1)}, u32[]{:S(2)}) copy-start(f32[128,128]{1,0:T(8,128)S(1)} %get-tuple-element.27.place_ref) | copy-start | bytes 196612
  85.3 3.7 %copy-start.3 = (f32[128,128]{1,0:T(8,128)S(1)}, f32[128,128]{1,0:T(8,128)}, u32[]{:S(2)}) copy-start(f32[128,128]{1,0:T(8,128)} %copy-done.2) | copy-start | bytes 196612
  85.3 3.7 %copy-start.5 = (f32[128,128]{1,0:T(8,128)S(1)}, f32[128,128]{1,0:T(8,128)}, u32[]{:S(2)}) copy-start(f32[128,128]{1,0:T(8,128)} %copy-done.4) | copy-start | bytes 196612
  85.3 21.5 %all-to-all-start = ((bf16[8,32,1280]{2,1,0:T(8,128)(2,1)}), bf16[8,32,1280]{2,1,0:T(8,128)(2,1)S(1)}, u32[]{:S(2)}, u32[]{:S(2)}) async-start(bf16[8,32,1280]{2,1,0:T(8,128)(2,1)} %bitcast.11), calls=%async_computation | async-start | bytes 1310720 | tf_op jit(solution)/shard_map/all_to_all | solution.py:430
  107.1 4.4 %collective-permute-start.16 = (f32[40,576]{1,0:T(8,128)S(1)}, f32[40,576]{1,0:T(8,128)S(1)}, u32[]{:S(2)}, u32[]{:S(2)}) collective-permute-start(f32[40,576]{1,0:T(8,128)S(1)} %get-tuple-element.47), channel_id=1, source_target_pairs={{0,128},{2,130},{1,129},{3,131},{4,132},{6,134},{5,133},{7,135},{8... | collective-permute-start | bytes 276488 | tf_op jit(solution)/shard_map/ppermute | solution.py:34

commit v6 on v5

--- a/solution.py
+++ b/solution.py
@@ -217,40 +217,51 @@
     return e[0]
 
 
-def tile_loss(text, img, own):
-    rows, width = text.shape[0], img.shape[0]
-    t = lax.dot_general(text, img, (((1,), (1,)), ((), ())), preferred_element_type=jnp.float32)
-    t = t * (SCALE * LOG2E) + (BIAS * LOG2E)
+def tile_dot(text, img):
+    return lax.dot_general(text, img, (((1,), (1,)), ((), ())), preferred_element_type=jnp.float32)
+
+
+def tile_loss(d, own):
+    rows, width = d.shape
+    d = d + BIAS / SCALE
     if own:
         row = lax.broadcasted_iota(jnp.int32, (ROWS, width), 0)
         col = lax.broadcasted_iota(jnp.int32, (ROWS, width), 1)
-        t = jnp.concatenate([jnp.where(col == row, -t[:ROWS], t[:ROWS]), t[ROWS:]], axis=0)
-    t = t.reshape(rows // 8, 8, width)
-    high = jnp.sum(jnp.maximum(t, 0.0), axis=0)
-    low = jnp.log1p(fold_terms(jnp.exp2(-jnp.abs(t))))
-    return high * LN2 + low
+        d = jnp.concatenate([jnp.where(col == row, -d[:ROWS], d[:ROWS]), d[ROWS:]], axis=0)
+    d = d.reshape(rows // 8, 8, width)
+    high = jnp.sum(jnp.maximum(d, 0.0), axis=0)
+    low = jnp.log1p(fold_terms(jnp.exp2(jnp.abs(d) * (-SCALE * LOG2E))))
+    return high * SCALE + low
+
+
+def losses_of(tasks):
+    totals = [jnp.zeros((8, sum(r.shape[0] for r in g)), jnp.float32) for g, _, _ in tasks]
+    waiting = None
+    for number, (group, texts, own) in enumerate(tasks):
+        img = [r[...] for r in group]
+        img = img[0] if len(img) == 1 else jnp.concatenate(img, axis=0)
+        for k, ref in enumerate(texts):
+            d = tile_dot(ref[...], img)
+            if waiting is not None:
+                before, tile, diagonal = waiting
+                totals[before] = totals[before] + tile_loss(tile, diagonal)
+            waiting = (number, d, own and k == 0)
+    before, tile, diagonal = waiting
+    totals[before] = totals[before] + tile_loss(tile, diagonal)
+    return [jnp.sum(t, axis=0, keepdims=True) for t in totals]
 
 
 def image_row(z, offset):
     return lax.rem(z + (offset + NZ), NZ)
 
 
-def group_loss(images, texts, own):
-    img = [r[...] for r in images]
-    img = img[0] if len(img) == 1 else jnp.concatenate(img, axis=0)
-    total = jnp.zeros((8, img.shape[0]), jnp.float32)
-    for k, ref in enumerate(texts):
-        total = total + tile_loss(ref[...], img, own and k == 0)
-    return jnp.sum(total, axis=0, keepdims=True)
-
-
 def early_kernel(*refs):
     images, texts, out_ref = refs[: NZ - 1], refs[NZ - 1 : -1], refs[-1]
-    for first in range(0, NZ - 1, 2):
-        group = images[first : first + 2]
-        total = group_loss(group, texts, first == 0)
-        for k in range(len(group)):
-            out_ref[first + k : first + k + 1, :] = total[:, k * ROWS : (k + 1) * ROWS]
+    tasks = [(images[k : k + 2], texts, k == 0) for k in range(0, NZ - 1, 2)]
+    for number, total in enumerate(losses_of(tasks)):
+        for k in range(total.shape[1] // ROWS):
+            row = 2 * number + k
+            out_ref[row : row + 1, :] = total[:, k * ROWS : (k + 1) * ROWS]
     out_ref[NZ - 1 :, :] = jnp.zeros((1, ROWS), jnp.float32)
 
 
@@ -275,23 +286,23 @@
 
     lines = [text_row(dx, dy) for dx in POFF for dy in POFF]
     total = jnp.zeros(packed.shape, jnp.float32)
+    ahead = tile_dot(packed, texts[0][...])
     for k, ref in enumerate(texts):
         text = ref[...]
+        t = ahead * SCALE + BIAS
+        if k + 1 < len(texts):
+            ahead = tile_dot(packed, texts[k + 1][...])
         count = text.shape[0] // ROWS
         mask = jnp.concatenate(lines[:count], axis=1)
         lines = lines[count:]
-        t = lax.dot_general(
-            packed, text, (((1,), (1,)), ((), ())), preferred_element_type=jnp.float32
-        )
-        t = t * SCALE + BIAS
         sign = jnp.ones(t.shape, jnp.float32)
         if k == 0:
             own = jnp.concatenate([1.0 - 2.0 * picks[0], sign[:CAP, ROWS:]], axis=1)
             sign = jnp.concatenate([own, sign[CAP:]], axis=0)
-        t = sign * t
+            t = sign * t
         e = jnp.exp(-jnp.abs(t))
         s = jnp.where(t >= 0, 1.0, e) / (1.0 + e)
-        slope = (sign * s * mask).astype(jnp.bfloat16)
+        slope = (s * (sign * mask) if k == 0 else s * mask).astype(jnp.bfloat16)
         total = total + jnp.dot(slope, text, preferred_element_type=jnp.float32)
     total = total.astype(jnp.bfloat16)
     width = total.shape[1]
@@ -300,9 +311,9 @@
         load_ref[rows, :width] = total[k * CAP : (k + 1) * CAP, :]
 
     near, far = texts[:3], texts[3:]
-    late = group_loss(images[NZ - 1 :], near, False)
-    for first in range(0, NZ, 2):
-        total = group_loss(images[first : first + 2], far, False)
+    tasks = [(images[k : k + 2], far, False) for k in range(0, NZ, 2)]
+    *totals, late = losses_of(tasks + [(images[NZ - 1 :], near, False)])
+    for first, total in zip(range(0, NZ, 2), totals):
         for k in range(2):
             loss = total[:, k * ROWS : (k + 1) * ROWS]
             loss = loss + (late if first + k == NZ - 1 else early_ref[first + k : first + k + 1, :])
@@ -380,6 +391,7 @@
     chosen, place_of = call(
         index_kernel, [], [sub_index.reshape(1, -1)], [shape((blocks, rows))] * 2, 100 << 20
     )
+    own_img, place_of, chosen = lax.optimization_barrier((own_img, place_of, chosen))
     z_img, unit, n_img = call(
         image_unit_kernel,
         [],
@@ -391,7 +403,7 @@
         text_unit_kernel, [], [own_text, recv_text], [shape((rows, width), bf16)], 20 * cells
     )
     line = [z_txt] + [over_plane(z_txt, shift, 0) for shift in (1, -1, 2)]
-    z_img, line[3] = lax.optimization_barrier((z_img, line[3]))
+    z_img, line[1], line[2] = lax.optimization_barrier((z_img, line[1], line[2]))
     back, ahead = [z_img], [z_img]
 
     def z_step():

time: 114 us -> 113 us (level)
  waiting for transfers between devices: 44.4 us -> 46.4 us
  starting transfers between devices: 35 us -> 33.5 us
    all_to_all x1, waiting for transfers between devices: 16.8 us -> 19.7 us  [shards(): load = lax.all_to_all(load, 'z', 0, 0, tiled=True)]
    ppermute x17, starting transfers between devices: 31.3 us -> 29.8 us  [permute(): return lax.ppermute(v, AXES, perm)]
    pallas_call x9, Pallas kernels: 19.3 us -> 18.1 us  [call(): pl.pallas_call(kernel, in_specs=[pl.BlockSpec(memory_space=pltpu.SMEM)] *...]
  transfers between devices with their start and end apart: 18 -> 18, of which waited for: 9 -> 11; matrix products, arithmetic and copies ran while one was open for 1% -> 1% of each run, Pallas kernels for 14% -> 14%
where the time goes in v6:
time: 113 us
  waiting for transfers between devices  46.4 us (41%)
  starting transfers between devices  33.5 us (30%)
  Pallas kernels  28.7 us (25%)
  local copies, waits for them, and re-layouts  3.05 us (3%)
    ppermute x17, starting transfers between devices, permute(): return lax.ppermute(v, AXES, perm)  29.8 us
    ppermute x17, waiting for transfers between devices, permute(): return lax.ppermute(v, AXES, perm)  26.8 us
    all_to_all x1, waiting for transfers between devices, shards(): load = lax.all_to_all(load, 'z', 0, 0, tiled=True)  19.7 us
    pallas_call x9, Pallas kernels, call(): pl.pallas_call(kernel, in_specs=[pl.BlockSpec(memory_space=pltpu.SMEM)] *...  18.1 us
    pallas_call x2, Pallas kernels, from_hbm(): pl.pallas_call(kernel, in_specs=[pl.BlockSpec(memory_space=pltpu.SMEM)] +...  10.5 us
    all_to_all x1, starting transfers between devices, shards(): load = lax.all_to_all(load, 'z', 0, 0, tiled=True)  3.67 us
  transfers between devices with their start and end apart: 18, of which 11 were waited for; matrix products, arithmetic and copies ran while one was open for 1% of the time, Pallas kernels for 14%

profile of v6, /device:TPU:1, one launch (start us, length us, event | category | flops | bytes accessed | tf_op | source)
XLA Modules:
  0.0 112.6 jit_solution(7392342285471868363)
XLA Ops:
  0.7 0.1 stack.27.pos_ref
  0.7 1.1 %copy-done.1 = bf16[256,1152]{1,0:T(8,128)(2,1)S(1)} copy-done((bf16[256,1152]{1,0:T(8,128)(2,1)S(1)}, bf16[256,1152]{1,0:T(8,128)(2,1)}, u32[]{:S(2)}) %copy-start.1) | copy-done | bytes 589848
  1.9 2.8 %shard_map.86 = (f32[128,1152]{1,0:T(8,128)S(1)}, bf16[128,1152]{1,0:T(8,128)(2,1)S(1)}) custom-call(s32[6]{0:T(128)S(1)} %stack.27.pos_ref, bf16[256,1152]{1,0:T(8,128)(2,1)S(1)} %copy-done.1, bf16[576,1152]{1,0:T(8,128)(2,1)} %bitcast.20), custom_call_target="tpu_custom_call" | custom-call | flops 339738624 | bytes 11534336 | tf_op jit(solution)/shard_map/pallas_call | solution.py:165
  4.7 3.8 %collective-permute-start = (bf16[128,1152]{1,0:T(8,128)(2,1)S(1)}, bf16[128,1152]{1,0:T(8,128)(2,1)S(1)}, u32[]{:S(2)}, u32[]{:S(2)}) collective-permute-start(bf16[128,1152]{1,0:T(8,128)(2,1)S(1)} %get-tuple-element.39), channel_id=1, source_target_pairs={{0,1},{2,3},{1,0},{3,2},{4,5},{6,7},{5,4},{7,6},{8,9},{10,11},{9,8... | collective-permute-start | bytes 884744 | tf_op jit(solution)/shard_map/ppermute | solution.py:34
  8.5 7.7 %shard_map.87 = (f32[128,1152]{1,0:T(8,128)S(1)}, bf16[128,1152]{1,0:T(8,128)(2,1)S(1)}) custom-call(s32[6]{0:T(128)S(1)} %stack.27.pos_ref, bf16[256,1152]{1,0:T(8,128)(2,1)S(1)} %copy-done, f32[1,1152]{1,0:T(1,128)S(1)} %copy-done.7, bf16[2152,1152]{1,0:T(8,128)(2,1)} %bitcast.18, bf16[2152,1152]{1,0:T(8,128)(2,1)} %bitcast.19), custom_call_target="tpu_custom_call" | custom-call | flops 2538602496 | bytes 11534336 | tf_op jit(solution)/shard_map/pallas_call | solution.py:165
  16.2 0.0 collective-permute-done.recv_ref
  16.2 1.6 %collective-permute-start.1 = (bf16[128,1152]{1,0:T(8,128)(2,1)S(1)}, bf16[128,1152]{1,0:T(8,128)(2,1)S(1)}, u32[]{:S(2)}, u32[]{:S(2)}) collective-permute-start(bf16[128,1152]{1,0:T(8,128)(2,1)S(1)} %get-tuple-element.40), channel_id=1, source_target_pairs={{0,1},{2,3},{1,0},{3,2},{4,5},{6,7},{5,4},{7,6},{8,9},{10,11},{9,8... | collective-permute-start | bytes 884744 | tf_op jit(solution)/shard_map/ppermute | solution.py:34
  17.9 0.2 shard_map.90.refs_0_
  18.0 1.3 %collective-permute-start.3 = (bf16[128,1152]{1,0:T(8,128)(2,1)S(1)}, bf16[128,1152]{1,0:T(8,128)(2,1)S(1)}, u32[]{:S(2)}, u32[]{:S(2)}) collective-permute-start(bf16[128,1152]{1,0:T(8,128)(2,1)S(1)} %shard_map.90.refs_0_), channel_id=1, source_target_pairs={{0,12},{2,14},{1,13},{3,15},{4,0},{6,2},{5,1},{7,3},{8,4},{10,6},{... | collective-permute-start | bytes 884744 | tf_op jit(solution)/shard_map/ppermute | solution.py:34
  19.4 0.2 collective-permute-start.2
  19.6 0.5 shard_map.88
  20.1 0.6 copy-done.2
  20.7 4.8 %collective-permute-done.1.recv_ref = bf16[128,1152]{1,0:T(8,128)(2,1)S(1)} collective-permute-done((bf16[128,1152]{1,0:T(8,128)(2,1)S(1)}, bf16[128,1152]{1,0:T(8,128)(2,1)S(1)}, u32[]{:S(2)}, u32[]{:S(2)}) %collective-permute-start.1) | collective-permute-done | bytes 294944 | tf_op jit(solution)/shard_map/ppermute | solution.py:34
  25.4 0.2 shard_map.89
  25.6 0.0 copy-start.8
  25.7 3.4 %collective-permute-done.3.refs_2_ = bf16[128,1152]{1,0:T(8,128)(2,1)S(1)} collective-permute-done((bf16[128,1152]{1,0:T(8,128)(2,1)S(1)}, bf16[128,1152]{1,0:T(8,128)(2,1)S(1)}, u32[]{:S(2)}, u32[]{:S(2)}) %collective-permute-start.3) | collective-permute-done | bytes 294944 | tf_op jit(solution)/shard_map/ppermute | solution.py:34
  29.0 1.0 collective-permute-done.2.refs_1_
  30.0 5.6 %collective-permute-start.5 = (bf16[128,1152]{1,0:T(8,128)(2,1)S(1)}, bf16[128,1152]{1,0:T(8,128)(2,1)S(1)}, u32[]{:S(2)}, u32[]{:S(2)}) collective-permute-start(bf16[128,1152]{1,0:T(8,128)(2,1)S(1)} %get-tuple-element.44.refs_0_), channel_id=1, source_target_pairs={{0,112},{2,114},{1,113},{3,115},{4,116},{6,118},{5,117},{7,119},{8... | collective-permute-start | bytes 884744 | tf_op jit(solution)/shard_map/ppermute | solution.py:34
  35.6 0.0 collective-permute-start.4
  35.6 1.2 %collective-permute-start.10 = (bf16[128,1152]{1,0:T(8,128)(2,1)S(1)}, bf16[128,1152]{1,0:T(8,128)(2,1)S(1)}, u32[]{:S(2)}, u32[]{:S(2)}) collective-permute-start(bf16[128,1152]{1,0:T(8,128)(2,1)S(1)} %shard_map.90.refs_0_), channel_id=1, source_target_pairs={{0,8},{2,10},{1,9},{3,11},{4,12},{6,14},{5,13},{7,15},{8,0},{10,2}... | collective-permute-start | bytes 884744 | tf_op jit(solution)/shard_map/ppermute | solution.py:34
  36.8 4.5 %collective-permute-done.5.refs_2_ = bf16[128,1152]{1,0:T(8,128)(2,1)S(1)} collective-permute-done((bf16[128,1152]{1,0:T(8,128)(2,1)S(1)}, bf16[128,1152]{1,0:T(8,128)(2,1)S(1)}, u32[]{:S(2)}, u32[]{:S(2)}) %collective-permute-start.5) | collective-permute-done | bytes 294944 | tf_op jit(solution)/shard_map/ppermute | solution.py:34
  41.4 3.1 %collective-permute-done.4.refs_1_ = bf16[128,1152]{1,0:T(8,128)(2,1)S(1)} collective-permute-done((bf16[128,1152]{1,0:T(8,128)(2,1)S(1)}, bf16[128,1152]{1,0:T(8,128)(2,1)S(1)}, u32[]{:S(2)}, u32[]{:S(2)}) %collective-permute-start.4) | collective-permute-done | bytes 294944 | tf_op jit(solution)/shard_map/ppermute | solution.py:34
  44.4 0.1 shard_map.91.refs_7_.refs_8_
  44.5 3.6 %collective-permute-start.12 = (bf16[512,1152]{1,0:T(8,128)(2,1)S(1)}, bf16[512,1152]{1,0:T(8,128)(2,1)S(1)}, u32[]{:S(2)}, u32[]{:S(2)}) collective-permute-start(bf16[512,1152]{1,0:T(8,128)(2,1)S(1)} %shard_map.91.refs_7_.refs_8_), channel_id=1, source_target_pairs={{0,3},{2,0},{1,2},{3,1},{4,7},{6,4},{5,6},{7,5},{8,11},{10,8},{9,1... | collective-permute-start | bytes 3538952 | tf_op jit(solution)/shard_map/ppermute | solution.py:34
  48.1 0.0 collective-permute-start.11
  48.1 0.0 collective-permute-start.6
  48.1 2.7 %collective-permute-start.7 = (bf16[128,1152]{1,0:T(8,128)(2,1)S(1)}, bf16[128,1152]{1,0:T(8,128)(2,1)}, u32[]{:S(2)}, u32[]{:S(2)}) collective-permute-start(bf16[128,1152]{1,0:T(8,128)(2,1)S(1)} %collective-permute-done.5.refs_2_), channel_id=1, source_target_pairs={{0,112},{2,114},{1,113},{3,115},{4,116},{6,118},{5,117},{7,119},{8... | collective-permute-start | bytes 884744 | tf_op jit(solution)/shard_map/ppermute | solution.py:34
  50.8 6.9 %collective-permute-done.6.refs_3_ = bf16[128,1152]{1,0:T(8,128)(2,1)} collective-permute-done((bf16[128,1152]{1,0:T(8,128)(2,1)S(1)}, bf16[128,1152]{1,0:T(8,128)(2,1)}, u32[]{:S(2)}, u32[]{:S(2)}) %collective-permute-start.6) | collective-permute-done | bytes 294944 | tf_op jit(solution)/shard_map/ppermute | solution.py:34
  57.7 0.0 collective-permute-done.7.refs_4_
  57.7 2.7 %collective-permute-start.9 = (bf16[128,1152]{1,0:T(8,128)(2,1)}, bf16[128,1152]{1,0:T(8,128)(2,1)S(1)}, u32[]{:S(2)}, u32[]{:S(2)}) collective-permute-start(bf16[128,1152]{1,0:T(8,128)(2,1)} %collective-permute-done.7.refs_4_), channel_id=1, source_target_pairs={{0,112},{2,114},{1,113},{3,115},{4,116},{6,118},{5,117},{7,119},{8... | collective-permute-start | bytes 884744 | tf_op jit(solution)/shard_map/ppermute | solution.py:34
  60.5 0.8 collective-permute-done.12.refs_9_.refs_10_
  61.3 0.0 copy-start.9
  61.3 3.6 %collective-permute-start.15 = (bf16[256,1152]{1,0:T(8,128)(2,1)S(1)}, bf16[256,1152]{1,0:T(8,128)(2,1)S(1)}, u32[]{:S(2)}, u32[]{:S(2)}) collective-permute-start(bf16[256,1152]{1,0:T(8,128)(2,1)S(1)} %slice.9), channel_id=1, source_target_pairs={{0,3},{2,0},{1,2},{3,1},{4,7},{6,4},{5,6},{7,5},{8,11},{10,8},{9,1... | collective-permute-start | bytes 1769480 | tf_op jit(solution)/shard_map/ppermute | solution.py:34
  64.9 1.1 slice.8
  66.1 0.1 collective-permute-start.14
  66.1 0.3 collective-permute-done.8.refs_5_
  66.5 0.0 collective-permute-done.9.refs_6_
  66.5 2.8 %collective-permute-start.13 = (bf16[128,1152]{1,0:T(8,128)(2,1)S(1)}, bf16[128,1152]{1,0:T(8,128)(2,1)S(1)}, u32[]{:S(2)}, u32[]{:S(2)}) collective-permute-start(bf16[128,1152]{1,0:T(8,128)(2,1)S(1)} %broadcast_select_fusion), channel_id=1, source_target_pairs={{0,16},{2,18},{1,17},{3,19},{4,20},{6,22},{5,21},{7,23},{8,24},{10... | collective-permute-start | bytes 884744 | tf_op jit(solution)/shard_map/ppermute | solution.py:34
  69.3 5.9 %shard_map.92.early_ref = f32[8,128]{1,0:T(8,128)S(1)} custom-call(bf16[128,1152]{1,0:T(8,128)(2,1)S(1)} %copy-done.9, bf16[128,1152]{1,0:T(8,128)(2,1)S(1)} %copy-done.13, bf16[128,1152]{1,0:T(8,128)(2,1)S(1)} %copy-done.11, bf16[128,1152]{1,0:T(8,128)(2,1)} %collective-permute-done.6.refs_3_, bf16[128,1152]{1,0:T(8,128)(2,1)} %collective-permute-done.7.refs_4_, ...), custom_call_target="tpu_custom_call" | custom-call | flops 2415919104 | bytes 1048576 | tf_op jit(solution)/shard_map/pallas_call | solution.py:64
  75.3 1.1 collective-permute-done.14.refs_11_
  76.4 8.4 %shard_map.93 = bf16[256,1280]{1,0:T(8,128)(2,1)} custom-call(s32[6]{0:T(128)S(1)} %stack.27.pos_ref, f32[128,128]{1,0:T(8,128)S(1)} %copy-done.16, f32[128,128]{1,0:T(8,128)S(1)} %copy-done.3, f32[8,128]{1,0:T(8,128)S(1)} %shard_map.92.early_ref, bf16[128,1152]{1,0:T(8,128)(2,1)S(1)} %copy-done.9, bf16[128,1152]{1,0:T(8,128)(2,1)S(1)} %copy-done.13, ...), custom_call_target="tpu_custom_call" | custom-call | flops 4831838208 | bytes 1048576 | tf_op jit(solution)/shard_map/pallas_call | solution.py:64
  84.7 3.7 %all-to-all-start = ((bf16[8,32,1280]{2,1,0:T(8,128)(2,1)}), bf16[8,32,1280]{2,1,0:T(8,128)(2,1)S(1)}, u32[]{:S(2)}, u32[]{:S(2)}) async-start(bf16[8,32,1280]{2,1,0:T(8,128)(2,1)} %bitcast.11), calls=%async_computation | async-start | bytes 1310720 | tf_op jit(solution)/shard_map/all_to_all | solution.py:442
  88.4 1.0 shard_map.94
  89.4 19.7 %all-to-all-done = bf16[8,32,1280]{2,1,0:T(8,128)(2,1)S(1)} async-done(((bf16[8,32,1280]{2,1,0:T(8,128)(2,1)}), bf16[8,32,1280]{2,1,0:T(8,128)(2,1)S(1)}, u32[]{:S(2)}, u32[]{:S(2)}) %all-to-all-start) | async-done | bytes 655392 | tf_op jit(solution)/shard_map/all_to_all | solution.py:442
  109.1 0.2 shard_map.95
  109.3 0.6 collective-permute-start.16
  109.9 0.9 collective-permute-done.16.recv_ref
  110.9 1.7 %shard_map.96 = (f32[1,128]{1,0:T(1,128)}, f32[576,128]{1,0:T(8,128)}) custom-call(s32[6]{0:T(128)S(1)} %stack.27.pos_ref, f32[40,576]{1,0:T(8,128)S(1)} %get-tuple-element.54.keep_ref, f32[40,576]{1,0:T(8,128)S(1)} %collective-permute-done.16.recv_ref, f32[128,128]{1,0:T(8,128)S(1)} %copy-done.4), custom_call_target="tpu_custom_call" | custom-call | flops 29491200 | bytes 1048576 | tf_op jit(solution)/shard_map/pallas_call | solution.py:64
  (37 shorter events, 0.2 us)
Async XLA Ops:
  0.6 7.9 %copy-start = (bf16[256,1152]{1,0:T(8,128)(2,1)S(1)}, bf16[256,1152]{1,0:T(8,128)(2,1)}, u32[]{:S(2)}) copy-start(bf16[256,1152]{1,0:T(8,128)(2,1)} %x_hbm) | copy-start | bytes 1769476
  0.7 1.1 %copy-start.1 = (bf16[256,1152]{1,0:T(8,128)(2,1)S(1)}, bf16[256,1152]{1,0:T(8,128)(2,1)}, u32[]{:S(2)}) copy-start(bf16[256,1152]{1,0:T(8,128)(2,1)} %text_hbm.1) | copy-start | bytes 1769476
  1.9 6.6 %copy-start.7 = (f32[1,1152]{1,0:T(1,128)S(1)}, f32[1,1152]{1,0:T(1,128)}, u32[]{:S(2)}) copy-start(f32[1,1152]{1,0:T(1,128)} %gain_hbm.1) | copy-start | bytes 13828
  4.7 11.6 %collective-permute-start = (bf16[128,1152]{1,0:T(8,128)(2,1)S(1)}, bf16[128,1152]{1,0:T(8,128)(2,1)S(1)}, u32[]{:S(2)}, u32[]{:S(2)}) collective-permute-start(bf16[128,1152]{1,0:T(8,128)(2,1)S(1)} %get-tuple-element.39), channel_id=1, source_target_pairs={{0,1},{2,3},{1,0},{3,2},{4,5},{6,7},{5,4},{7,6},{8,9},{10,11},{9,8... | collective-permute-start | bytes 884744 | tf_op jit(solution)/shard_map/ppermute | solution.py:34
  8.5 11.1 %copy-start.14 = (s32[2048]{0:T(1024)S(1)}, s32[2048]{0:T(1024)}, u32[]{:S(2)}) copy-start(s32[2048]{0:T(1024)} %param.13) | copy-start | bytes 24580
  16.2 9.2 %collective-permute-start.1 = (bf16[128,1152]{1,0:T(8,128)(2,1)S(1)}, bf16[128,1152]{1,0:T(8,128)(2,1)S(1)}, u32[]{:S(2)}, u32[]{:S(2)}) collective-permute-start(bf16[128,1152]{1,0:T(8,128)(2,1)S(1)} %get-tuple-element.40), channel_id=1, source_target_pairs={{0,1},{2,3},{1,0},{3,2},{4,5},{6,7},{5,4},{7,6},{8,9},{10,11},{9,8... | collective-permute-start | bytes 884744 | tf_op jit(solution)/shard_map/ppermute | solution.py:34
  18.0 11.0 %collective-permute-start.3 = (bf16[128,1152]{1,0:T(8,128)(2,1)S(1)}, bf16[128,1152]{1,0:T(8,128)(2,1)S(1)}, u32[]{:S(2)}, u32[]{:S(2)}) collective-permute-start(bf16[128,1152]{1,0:T(8,128)(2,1)S(1)} %shard_map.90.refs_0_), channel_id=1, source_target_pairs={{0,12},{2,14},{1,13},{3,15},{4,0},{6,2},{5,1},{7,3},{8,4},{10,6},{... | collective-permute-start | bytes 884744 | tf_op jit(solution)/shard_map/ppermute | solution.py:34
  19.4 10.6 %collective-permute-start.2 = (bf16[128,1152]{1,0:T(8,128)(2,1)S(1)}, bf16[128,1152]{1,0:T(8,128)(2,1)S(1)}, u32[]{:S(2)}, u32[]{:S(2)}) collective-permute-start(bf16[128,1152]{1,0:T(8,128)(2,1)S(1)} %shard_map.90.refs_0_), channel_id=1, source_target_pairs={{0,4},{2,6},{1,5},{3,7},{4,8},{6,10},{5,9},{7,11},{8,12},{10,14},{... | collective-permute-start | bytes 884744 | tf_op jit(solution)/shard_map/ppermute | solution.py:34
  20.1 0.6 copy-start.2
  20.7 23.9 %copy-start.15 = (f32[128,128]{1,0:T(8,128)}, f32[128,128]{1,0:T(8,128)S(1)}, u32[]{:S(2)}) copy-start(f32[128,128]{1,0:T(8,128)S(1)} %get-tuple-element.35.chosen_ref) | copy-start | bytes 196612
  25.6 32.1 %copy-start.5 = (f32[128,128]{1,0:T(8,128)}, f32[128,128]{1,0:T(8,128)S(1)}, u32[]{:S(2)}) copy-start(f32[128,128]{1,0:T(8,128)S(1)} %get-tuple-element.51.n_ref) | copy-start | bytes 196612
  25.6 32.1 %copy-start.8 = (bf16[128,1152]{1,0:T(8,128)(2,1)}, bf16[128,1152]{1,0:T(8,128)(2,1)S(1)}, u32[]{:S(2)}) copy-start(bf16[128,1152]{1,0:T(8,128)(2,1)S(1)} %get-tuple-element.44.refs_0_) | copy-start | bytes 884740
  30.0 11.3 %collective-permute-start.5 = (bf16[128,1152]{1,0:T(8,128)(2,1)S(1)}, bf16[128,1152]{1,0:T(8,128)(2,1)S(1)}, u32[]{:S(2)}, u32[]{:S(2)}) collective-permute-start(bf16[128,1152]{1,0:T(8,128)(2,1)S(1)} %get-tuple-element.44.refs_0_), channel_id=1, source_target_pairs={{0,112},{2,114},{1,113},{3,115},{4,116},{6,118},{5,117},{7,119},{8... | collective-permute-start | bytes 884744 | tf_op jit(solution)/shard_map/ppermute | solution.py:34
  35.6 8.8 %collective-permute-start.4 = (bf16[128,1152]{1,0:T(8,128)(2,1)S(1)}, bf16[128,1152]{1,0:T(8,128)(2,1)S(1)}, u32[]{:S(2)}, u32[]{:S(2)}) collective-permute-start(bf16[128,1152]{1,0:T(8,128)(2,1)S(1)} %get-tuple-element.44.refs_0_), channel_id=1, source_target_pairs={{0,16},{2,18},{1,17},{3,19},{4,20},{6,22},{5,21},{7,23},{8,24},{10... | collective-permute-start | bytes 884744 | tf_op jit(solution)/shard_map/ppermute | solution.py:34
  35.6 8.8 %collective-permute-start.10 = (bf16[128,1152]{1,0:T(8,128)(2,1)S(1)}, bf16[128,1152]{1,0:T(8,128)(2,1)S(1)}, u32[]{:S(2)}, u32[]{:S(2)}) collective-permute-start(bf16[128,1152]{1,0:T(8,128)(2,1)S(1)} %shard_map.90.refs_0_), channel_id=1, source_target_pairs={{0,8},{2,10},{1,9},{3,11},{4,12},{6,14},{5,13},{7,15},{8,0},{10,2}... | collective-permute-start | bytes 884744 | tf_op jit(solution)/shard_map/ppermute | solution.py:34
  41.4 16.4 %copy-start.10 = (bf16[128,1152]{1,0:T(8,128)(2,1)}, bf16[128,1152]{1,0:T(8,128)(2,1)S(1)}, u32[]{:S(2)}) copy-start(bf16[128,1152]{1,0:T(8,128)(2,1)S(1)} %collective-permute-done.5.refs_2_) | copy-start | bytes 884740
  44.4 6.4 %copy-start.12 = (bf16[128,1152]{1,0:T(8,128)(2,1)}, bf16[128,1152]{1,0:T(8,128)(2,1)S(1)}, u32[]{:S(2)}) copy-start(bf16[128,1152]{1,0:T(8,128)(2,1)S(1)} %collective-permute-done.4.refs_1_) | copy-start | bytes 884740
  44.5 16.7 %collective-permute-start.12 = (bf16[512,1152]{1,0:T(8,128)(2,1)S(1)}, bf16[512,1152]{1,0:T(8,128)(2,1)S(1)}, u32[]{:S(2)}, u32[]{:S(2)}) collective-permute-start(bf16[512,1152]{1,0:T(8,128)(2,1)S(1)} %shard_map.91.refs_7_.refs_8_), channel_id=1, source_target_pairs={{0,3},{2,0},{1,2},{3,1},{4,7},{6,4},{5,6},{7,5},{8,11},{10,8},{9,1... | collective-permute-start | bytes 3538952 | tf_op jit(solution)/shard_map/ppermute | solution.py:34
  48.1 16.8 %collective-permute-start.11 = (bf16[512,1152]{1,0:T(8,128)(2,1)S(1)}, bf16[512,1152]{1,0:T(8,128)(2,1)}, u32[]{:S(2)}, u32[]{:S(2)}) collective-permute-start(bf16[512,1152]{1,0:T(8,128)(2,1)S(1)} %shard_map.91.refs_7_.refs_8_), channel_id=1, source_target_pairs={{0,2},{2,1},{1,3},{3,0},{4,6},{6,5},{5,7},{7,4},{8,10},{10,9},{9,1... | collective-permute-start | bytes 3538952 | tf_op jit(solution)/shard_map/ppermute | solution.py:34
  48.1 9.6 %collective-permute-start.6 = (bf16[128,1152]{1,0:T(8,128)(2,1)S(1)}, bf16[128,1152]{1,0:T(8,128)(2,1)}, u32[]{:S(2)}, u32[]{:S(2)}) collective-permute-start(bf16[128,1152]{1,0:T(8,128)(2,1)S(1)} %collective-permute-done.4.refs_1_), channel_id=1, source_target_pairs={{0,16},{2,18},{1,17},{3,19},{4,20},{6,22},{5,21},{7,23},{8,24},{10... | collective-permute-start | bytes 884744 | tf_op jit(solution)/shard_map/ppermute | solution.py:34
  48.1 9.6 %collective-permute-start.7 = (bf16[128,1152]{1,0:T(8,128)(2,1)S(1)}, bf16[128,1152]{1,0:T(8,128)(2,1)}, u32[]{:S(2)}, u32[]{:S(2)}) collective-permute-start(bf16[128,1152]{1,0:T(8,128)(2,1)S(1)} %collective-permute-done.5.refs_2_), channel_id=1, source_target_pairs={{0,112},{2,114},{1,113},{3,115},{4,116},{6,118},{5,117},{7,119},{8... | collective-permute-start | bytes 884744 | tf_op jit(solution)/shard_map/ppermute | solution.py:34
  57.7 8.8 %collective-permute-start.8 = (bf16[128,1152]{1,0:T(8,128)(2,1)}, bf16[128,1152]{1,0:T(8,128)(2,1)S(1)}, u32[]{:S(2)}, u32[]{:S(2)}) collective-permute-start(bf16[128,1152]{1,0:T(8,128)(2,1)} %collective-permute-done.6.refs_3_), channel_id=1, source_target_pairs={{0,16},{2,18},{1,17},{3,19},{4,20},{6,22},{5,21},{7,23},{8,24},{10... | collective-permute-start | bytes 884744 | tf_op jit(solution)/shard_map/ppermute | solution.py:34
  57.7 8.7 %collective-permute-start.9 = (bf16[128,1152]{1,0:T(8,128)(2,1)}, bf16[128,1152]{1,0:T(8,128)(2,1)S(1)}, u32[]{:S(2)}, u32[]{:S(2)}) collective-permute-start(bf16[128,1152]{1,0:T(8,128)(2,1)} %collective-permute-done.7.refs_4_), channel_id=1, source_target_pairs={{0,112},{2,114},{1,113},{3,115},{4,116},{6,118},{5,117},{7,119},{8... | collective-permute-start | bytes 884744 | tf_op jit(solution)/shard_map/ppermute | solution.py:34
  61.3 8.0 %copy-start.9 = (bf16[128,1152]{1,0:T(8,128)(2,1)S(1)}, bf16[128,1152]{1,0:T(8,128)(2,1)}, u32[]{:S(2)}) copy-start(bf16[128,1152]{1,0:T(8,128)(2,1)} %copy-done.8) | copy-start | bytes 884740
  61.3 8.0 %copy-start.11 = (bf16[128,1152]{1,0:T(8,128)(2,1)S(1)}, bf16[128,1152]{1,0:T(8,128)(2,1)}, u32[]{:S(2)}) copy-start(bf16[128,1152]{1,0:T(8,128)(2,1)} %copy-done.10) | copy-start | bytes 884740
  61.3 8.0 %copy-start.13 = (bf16[128,1152]{1,0:T(8,128)(2,1)S(1)}, bf16[128,1152]{1,0:T(8,128)(2,1)}, u32[]{:S(2)}) copy-start(bf16[128,1152]{1,0:T(8,128)(2,1)} %copy-done.12) | copy-start | bytes 884740
  61.3 13.9 %collective-permute-start.15 = (bf16[256,1152]{1,0:T(8,128)(2,1)S(1)}, bf16[256,1152]{1,0:T(8,128)(2,1)S(1)}, u32[]{:S(2)}, u32[]{:S(2)}) collective-permute-start(bf16[256,1152]{1,0:T(8,128)(2,1)S(1)} %slice.9), channel_id=1, source_target_pairs={{0,3},{2,0},{1,2},{3,1},{4,7},{6,4},{5,6},{7,5},{8,11},{10,8},{9,1... | collective-permute-start | bytes 1769480 | tf_op jit(solution)/shard_map/ppermute | solution.py:34
  66.1 10.3 %collective-permute-start.14 = (bf16[256,1152]{1,0:T(8,128)(2,1)S(1)}, bf16[256,1152]{1,0:T(8,128)(2,1)S(1)}, u32[]{:S(2)}, u32[]{:S(2)}) collective-permute-start(bf16[256,1152]{1,0:T(8,128)(2,1)S(1)} %slice.8), channel_id=1, source_target_pairs={{0,2},{2,1},{1,3},{3,0},{4,6},{6,5},{5,7},{7,4},{8,10},{10,9},{9,1... | collective-permute-start | bytes 1769480 | tf_op jit(solution)/shard_map/ppermute | solution.py:34
  66.5 9.9 %copy-start.3 = (f32[128,128]{1,0:T(8,128)S(1)}, f32[128,128]{1,0:T(8,128)}, u32[]{:S(2)}) copy-start(f32[128,128]{1,0:T(8,128)} %copy-done.2) | copy-start | bytes 196612
  66.5 9.9 %copy-start.16 = (f32[128,128]{1,0:T(8,128)S(1)}, f32[128,128]{1,0:T(8,128)}, u32[]{:S(2)}) copy-start(f32[128,128]{1,0:T(8,128)} %copy-done.15) | copy-start | bytes 196612
  66.5 8.7 %collective-permute-start.13 = (bf16[128,1152]{1,0:T(8,128)(2,1)S(1)}, bf16[128,1152]{1,0:T(8,128)(2,1)S(1)}, u32[]{:S(2)}, u32[]{:S(2)}) collective-permute-start(bf16[128,1152]{1,0:T(8,128)(2,1)S(1)} %broadcast_select_fusion), channel_id=1, source_target_pairs={{0,16},{2,18},{1,17},{3,19},{4,20},{6,22},{5,21},{7,23},{8,24},{10... | collective-permute-start | bytes 884744 | tf_op jit(solution)/shard_map/ppermute | solution.py:34
  84.7 3.7 %copy-start.4 = (f32[128,128]{1,0:T(8,128)S(1)}, f32[128,128]{1,0:T(8,128)}, u32[]{:S(2)}) copy-start(f32[128,128]{1,0:T(8,128)} %copy-done.2) | copy-start | bytes 196612
  84.7 3.7 %copy-start.6 = (f32[128,128]{1,0:T(8,128)S(1)}, f32[128,128]{1,0:T(8,128)}, u32[]{:S(2)}) copy-start(f32[128,128]{1,0:T(8,128)} %copy-done.5) | copy-start | bytes 196612
  84.7 24.4 %all-to-all-start = ((bf16[8,32,1280]{2,1,0:T(8,128)(2,1)}), bf16[8,32,1280]{2,1,0:T(8,128)(2,1)S(1)}, u32[]{:S(2)}, u32[]{:S(2)}) async-start(bf16[8,32,1280]{2,1,0:T(8,128)(2,1)} %bitcast.11), calls=%async_computation | async-start | bytes 1310720 | tf_op jit(solution)/shard_map/all_to_all | solution.py:442
  109.3 1.5 %collective-permute-start.16 = (f32[40,576]{1,0:T(8,128)S(1)}, f32[40,576]{1,0:T(8,128)S(1)}, u32[]{:S(2)}, u32[]{:S(2)}) collective-permute-start(f32[40,576]{1,0:T(8,128)S(1)} %get-tuple-element.55), channel_id=1, source_target_pairs={{0,128},{2,130},{1,129},{3,131},{4,132},{6,134},{5,133},{7,135},{8... | collective-permute-start | bytes 276488 | tf_op jit(solution)/shard_map/ppermute | solution.py:34

commit v7 on v6

--- a/solution.py
+++ b/solution.py
@@ -97,36 +97,18 @@
     other_ref[...] = other.astype(jnp.bfloat16)
 
 
-def text_kernel(
-    pos_ref, text_hbm, head_hbm, own_ref, other_ref, text_ref, head_ref, acc_ref, sems
-):
-    copies = [
-        pltpu.make_async_copy(text_hbm, text_ref, sems.at[0]),
-        pltpu.make_async_copy(head_hbm, head_ref, sems.at[1]),
-    ]
-    for c in copies:
-        c.start()
-    for c in copies:
-        c.wait()
-    depth = head_ref.shape[0]
-    m = pos_ref[0]
-    text = text_ref[...]
-    part = jnp.where(m == 0, text[:, :depth], text[:, depth:])
-    acc_ref[...] = jnp.dot(part, head_ref[...], preferred_element_type=jnp.float32)
-    split_rows(acc_ref, m, own_ref, other_ref)
-
-
-def mlp_kernel(
-    pos_ref, x_hbm, gain_hbm, up_hbm, down_hbm, own_ref, other_ref,
-    x_ref, gain_ref, up_ref, down_ref, normed_ref, hidden_ref, acc_ref, sems,
+def front_kernel(
+    pos_ref, x_hbm, gain_hbm, text_hbm, head_hbm,
+    own_ref, other_ref, normed_ref, own_x_ref,
+    x_ref, gain_ref, text_ref, head_ref, acc_ref, sems,
 ):
     copies = [
         pltpu.make_async_copy(source, target, sems.at[k])
         for k, (source, target) in enumerate(
-            [(x_hbm, x_ref), (gain_hbm, gain_ref), (up_hbm, up_ref), (down_hbm, down_ref)]
+            [(x_hbm, x_ref), (gain_hbm, gain_ref), (text_hbm, text_ref), (head_hbm, head_ref)]
         )
     ]
-    for c in copies[:3]:
+    for c in copies:
         c.start()
     m = pos_ref[0]
     rows = own_ref.shape[0]
@@ -137,8 +119,49 @@
     gap = x - mean
     var = jnp.mean(gap * gap, axis=1, keepdims=True)
     normed_ref[...] = (gap * lax.rsqrt(var + EPS) * gain_ref[...]).astype(jnp.bfloat16)
+    own_x_ref[...] = x_ref[pl.ds(pl.multiple_of(m * rows, rows), rows), :]
     copies[2].wait()
-    copies[3].start()
+    copies[3].wait()
+    depth = head_ref.shape[0]
+    text = text_ref[...]
+    part = jnp.where(m == 0, text[:, :depth], text[:, depth:])
+    acc_ref[...] = jnp.dot(part, head_ref[...], preferred_element_type=jnp.float32)
+    split_rows(acc_ref, m, own_ref, other_ref)
+
+
+def front(pos, x, gain, text, head):
+    arrays = [x, gain, text, head]
+    rows, width = x.shape
+    half, bf16 = rows // 2, jnp.bfloat16
+    vmem, hbm = pl.BlockSpec(memory_space=pltpu.VMEM), pl.BlockSpec(memory_space=pl.ANY)
+    return pl.pallas_call(
+        front_kernel,
+        in_specs=[pl.BlockSpec(memory_space=pltpu.SMEM)] + [hbm] * len(arrays),
+        out_specs=[vmem] * 4,
+        out_shape=[
+            shape((half, width)),
+            shape((half, width), bf16),
+            shape((rows, width), bf16),
+            shape((half, width), bf16),
+        ],
+        scratch_shapes=[pltpu.VMEM(a.shape, a.dtype) for a in arrays]
+        + [pltpu.VMEM((rows, width), jnp.float32), pltpu.SemaphoreType.DMA((len(arrays),))],
+        compiler_params=pltpu.CompilerParams(vmem_limit_bytes=52 * 1024 * 1024),
+        cost_estimate=pl.CostEstimate(
+            flops=2 * rows * width * head.shape[0], bytes_accessed=4 << 20, transcendentals=0
+        ),
+    )(pos, *arrays)
+
+
+def mlp_kernel(
+    pos_ref, normed_ref, own_x_ref, up_hbm, down_hbm, own_ref, other_ref,
+    up_ref, down_ref, hidden_ref, acc_ref, sems,
+):
+    first = pltpu.make_async_copy(up_hbm, up_ref, sems.at[0])
+    second = pltpu.make_async_copy(down_hbm, down_ref, sems.at[1])
+    first.start()
+    first.wait()
+    second.start()
     total, block = up_ref.shape[0], 512
     for start in range(0, total, block):
         stop = min(start + block, total)
@@ -149,30 +172,37 @@
             preferred_element_type=jnp.float32,
         )
         hidden_ref[:, start:stop] = jax.nn.gelu(acc, approximate=True).astype(jnp.bfloat16)
-    copies[3].wait()
+    second.wait()
     block = 384
     for start in range(0, acc_ref.shape[1], block):
         acc_ref[:, start : start + block] = jnp.dot(
             hidden_ref[...], down_ref[:, start : start + block], preferred_element_type=jnp.float32
         )
-    split_rows(acc_ref, m, own_ref, other_ref)
-    x = x_ref[pl.ds(pl.multiple_of(m * rows, rows), rows), :]
-    own_ref[...] = own_ref[...] + x.astype(jnp.float32)
-
-
-def from_hbm(kernel, pos, arrays, rows, width, scratch, flops):
+    split_rows(acc_ref, pos_ref[0], own_ref, other_ref)
+    own_ref[...] = own_ref[...] + own_x_ref[...].astype(jnp.float32)
+
+
+def image_mlp(pos, normed, own_x, up, down):
+    rows, width = normed.shape
+    half, hidden, bf16 = rows // 2, up.shape[0], jnp.bfloat16
     vmem, hbm = pl.BlockSpec(memory_space=pltpu.VMEM), pl.BlockSpec(memory_space=pl.ANY)
     return pl.pallas_call(
-        kernel,
-        in_specs=[pl.BlockSpec(memory_space=pltpu.SMEM)] + [hbm] * len(arrays),
+        mlp_kernel,
+        in_specs=[pl.BlockSpec(memory_space=pltpu.SMEM), vmem, vmem, hbm, hbm],
         out_specs=[vmem, vmem],
-        out_shape=[shape((rows, width)), shape((rows, width), jnp.bfloat16)],
-        scratch_shapes=[pltpu.VMEM(a.shape, a.dtype) for a in arrays]
-        + scratch
-        + [pltpu.VMEM((2 * rows, width), jnp.float32), pltpu.SemaphoreType.DMA((len(arrays),))],
+        out_shape=[shape((half, width)), shape((half, width), bf16)],
+        scratch_shapes=[
+            pltpu.VMEM(up.shape, bf16),
+            pltpu.VMEM(down.shape, bf16),
+            pltpu.VMEM((rows, hidden), bf16),
+            pltpu.VMEM((rows, width), jnp.float32),
+            pltpu.SemaphoreType.DMA((2,)),
+        ],
         compiler_params=pltpu.CompilerParams(vmem_limit_bytes=52 * 1024 * 1024),
-        cost_estimate=pl.CostEstimate(flops=flops, bytes_accessed=11 << 20, transcendentals=0),
-    )(pos, *arrays)
+        cost_estimate=pl.CostEstimate(
+            flops=4 * rows * width * hidden, bytes_accessed=11 << 20, transcendentals=rows * hidden
+        ),
+    )(pos, normed, own_x, up, down)
 
 
 def text_unit_kernel(own_ref, recv_ref, z_ref):
@@ -371,21 +401,11 @@
     pos = jnp.stack([p.astype(jnp.int32) for p in pos])
     cells = rows * width
 
-    own_text, other_text = from_hbm(
-        text_kernel, pos, [text_features, text_head[0]], rows, width, [], 2 * cells * width
+    own_text, other_text, normed, own_x = front(
+        pos, image_features, norm_gain, text_features, text_head[0]
     )
     recv_text = over_mp(other_text)
-    features, own_text = lax.optimization_barrier((image_features, own_text))
-    hidden = up_weight.shape[2]
-    own_img, other_img = from_hbm(
-        mlp_kernel,
-        pos,
-        [features, norm_gain, up_weight[0].T, down_weight[0]],
-        rows,
-        width,
-        [pltpu.VMEM((2 * rows, width), bf16), pltpu.VMEM((2 * rows, hidden), bf16)],
-        8 * cells * hidden,
-    )
+    own_img, other_img = image_mlp(pos, normed, own_x, up_weight[0].T, down_weight[0])
     other_img, recv_text = lax.optimization_barrier((other_img, recv_text))
     recv_img = over_mp(other_img)
     chosen, place_of = call(

time: 113 us -> 114 us (level)
  Pallas kernels: 28.7 us -> 30.5 us
    pallas_call x2, Pallas kernels: 10.5 us -> 12.3 us  [the longest x1 9.31 us: image_mlp(): pl.pallas_call(mlp_kernel, in_specs=[pl.BlockSpec(memory_space=pltpu.SMEM...]
  transfers between devices with their start and end apart: 18 -> 18, of which waited for: 11 -> 11; matrix products, arithmetic and copies ran while one was open for 1% -> 1% of each run, Pallas kernels for 14% -> 15%
where the time goes in v7:
time: 114 us
  waiting for transfers between devices  47.5 us (42%)
  starting transfers between devices  32.4 us (28%)
  Pallas kernels  30.5 us (27%)
  local copies, waits for them, and re-layouts  2.61 us (2%)
    ppermute x17, starting transfers between devices, permute(): return lax.ppermute(v, AXES, perm)  28.7 us
    ppermute x17, waiting for transfers between devices, permute(): return lax.ppermute(v, AXES, perm)  27.9 us
    all_to_all x1, waiting for transfers between devices, shards(): load = lax.all_to_all(load, 'z', 0, 0, tiled=True)  19.7 us
    pallas_call x9, Pallas kernels, call(): pl.pallas_call(kernel, in_specs=[pl.BlockSpec(memory_space=pltpu.SMEM)] *...  18.1 us
    pallas_call x1, Pallas kernels, image_mlp(): pl.pallas_call(mlp_kernel, in_specs=[pl.BlockSpec(memory_space=pltpu.SMEM...  9.31 us
    all_to_all x1, starting transfers between devices, shards(): load = lax.all_to_all(load, 'z', 0, 0, tiled=True)  3.67 us
    pallas_call x1, Pallas kernels, front(): pl.pallas_call(front_kernel, in_specs=[pl.BlockSpec(memory_space=pltpu.SM...  3.04 us
  transfers between devices with their start and end apart: 18, of which 11 were waited for; matrix products, arithmetic and copies ran while one was open for 1% of the time, Pallas kernels for 15%

profile of v7, /device:TPU:1, one launch (start us, length us, event | category | flops | bytes accessed | tf_op | source)
XLA Modules:
  0.0 113.9 jit_solution(3982027315019858073)
XLA Ops:
  0.6 0.1 stack.27.pos_ref
  0.7 0.7 copy-done.5
  1.4 3.0 %shard_map.86 = (f32[128,1152]{1,0:T(8,128)S(1)}, bf16[128,1152]{1,0:T(8,128)(2,1)S(1)}, bf16[256,1152]{1,0:T(8,128)(2,1)S(1)}, bf16[128,1152]{1,0:T(8,128)(2,1)S(1)}) custom-call(s32[6]{0:T(128)S(1)} %stack.27.pos_ref, bf16[256,1152]{1,0:T(8,128)(2,1)} %x_hbm.1, f32[1,1152]{1,0:T(1,128)S(1)} %copy-done.5, bf16[256,1152]{1,0:T(8,128)(2,1)} %text_hbm.1, ...), custom_call_target="tpu_custom_call" | custom-call | flops 339738624 | bytes 4194304 | tf_op jit(solution)/shard_map/pallas_call | solution.py:137
  4.5 3.8 %collective-permute-start = (bf16[128,1152]{1,0:T(8,128)(2,1)S(1)}, bf16[128,1152]{1,0:T(8,128)(2,1)S(1)}, u32[]{:S(2)}, u32[]{:S(2)}) collective-permute-start(bf16[128,1152]{1,0:T(8,128)(2,1)S(1)} %get-tuple-element.39), channel_id=1, source_target_pairs={{0,1},{2,3},{1,0},{3,2},{4,5},{6,7},{5,4},{7,6},{8,9},{10,11},{9,8... | collective-permute-start | bytes 884744 | tf_op jit(solution)/shard_map/ppermute | solution.py:34
  8.3 9.3 %shard_map.87 = (f32[128,1152]{1,0:T(8,128)S(1)}, bf16[128,1152]{1,0:T(8,128)(2,1)S(1)}) custom-call(s32[6]{0:T(128)S(1)} %stack.27.pos_ref, bf16[256,1152]{1,0:T(8,128)(2,1)S(1)} %get-tuple-element.30.normed_ref, bf16[128,1152]{1,0:T(8,128)(2,1)S(1)} %get-tuple-element.31.own_x_ref, bf16[2152,1152]{1,0:T(8,128)(2,1)} %bitcast.18, bf16[2152,1152]{1,0:T(8,128)(2,1)} %bitcast.19), custom_call_target="tpu_custom_call" | custom-call | flops 2538602496 | bytes 11534336 | tf_op jit(solution)/shard_map/pallas_call | solution.py:189
  17.6 0.1 collective-permute-start.1
  17.7 0.2 shard_map.90.refs_0_
  17.9 2.8 %collective-permute-start.3 = (bf16[128,1152]{1,0:T(8,128)(2,1)S(1)}, bf16[128,1152]{1,0:T(8,128)(2,1)S(1)}, u32[]{:S(2)}, u32[]{:S(2)}) collective-permute-start(bf16[128,1152]{1,0:T(8,128)(2,1)S(1)} %shard_map.90.refs_0_), channel_id=1, source_target_pairs={{0,12},{2,14},{1,13},{3,15},{4,0},{6,2},{5,1},{7,3},{8,4},{10,6},{... | collective-permute-start | bytes 884744 | tf_op jit(solution)/shard_map/ppermute | solution.py:34
  20.8 0.5 shard_map.88
  21.3 0.6 copy-done
  21.9 4.9 %collective-permute-done.1.recv_ref = bf16[128,1152]{1,0:T(8,128)(2,1)S(1)} collective-permute-done((bf16[128,1152]{1,0:T(8,128)(2,1)S(1)}, bf16[128,1152]{1,0:T(8,128)(2,1)S(1)}, u32[]{:S(2)}, u32[]{:S(2)}) %collective-permute-start.1) | collective-permute-done | bytes 294944 | tf_op jit(solution)/shard_map/ppermute | solution.py:34
  26.8 0.2 shard_map.89
  27.0 0.0 copy-start.6
  27.0 2.8 %collective-permute-done.3.refs_2_ = bf16[128,1152]{1,0:T(8,128)(2,1)S(1)} collective-permute-done((bf16[128,1152]{1,0:T(8,128)(2,1)S(1)}, bf16[128,1152]{1,0:T(8,128)(2,1)S(1)}, u32[]{:S(2)}, u32[]{:S(2)}) %collective-permute-start.3) | collective-permute-done | bytes 294944 | tf_op jit(solution)/shard_map/ppermute | solution.py:34
  29.8 1.3 %collective-permute-done.2.refs_1_ = bf16[128,1152]{1,0:T(8,128)(2,1)S(1)} collective-permute-done((bf16[128,1152]{1,0:T(8,128)(2,1)S(1)}, bf16[128,1152]{1,0:T(8,128)(2,1)S(1)}, u32[]{:S(2)}, u32[]{:S(2)}) %collective-permute-start.2) | collective-permute-done | bytes 294944 | tf_op jit(solution)/shard_map/ppermute | solution.py:34
  31.1 5.6 %collective-permute-start.5 = (bf16[128,1152]{1,0:T(8,128)(2,1)S(1)}, bf16[128,1152]{1,0:T(8,128)(2,1)S(1)}, u32[]{:S(2)}, u32[]{:S(2)}) collective-permute-start(bf16[128,1152]{1,0:T(8,128)(2,1)S(1)} %get-tuple-element.44.refs_0_), channel_id=1, source_target_pairs={{0,112},{2,114},{1,113},{3,115},{4,116},{6,118},{5,117},{7,119},{8... | collective-permute-start | bytes 884744 | tf_op jit(solution)/shard_map/ppermute | solution.py:34
  36.7 0.0 collective-permute-start.4
  36.7 1.3 %collective-permute-start.10 = (bf16[128,1152]{1,0:T(8,128)(2,1)S(1)}, bf16[128,1152]{1,0:T(8,128)(2,1)S(1)}, u32[]{:S(2)}, u32[]{:S(2)}) collective-permute-start(bf16[128,1152]{1,0:T(8,128)(2,1)S(1)} %shard_map.90.refs_0_), channel_id=1, source_target_pairs={{0,8},{2,10},{1,9},{3,11},{4,12},{6,14},{5,13},{7,15},{8,0},{10,2}... | collective-permute-start | bytes 884744 | tf_op jit(solution)/shard_map/ppermute | solution.py:34
  38.0 5.3 %collective-permute-done.5.refs_2_ = bf16[128,1152]{1,0:T(8,128)(2,1)S(1)} collective-permute-done((bf16[128,1152]{1,0:T(8,128)(2,1)S(1)}, bf16[128,1152]{1,0:T(8,128)(2,1)S(1)}, u32[]{:S(2)}, u32[]{:S(2)}) %collective-permute-start.5) | collective-permute-done | bytes 294944 | tf_op jit(solution)/shard_map/ppermute | solution.py:34
  43.4 3.5 %collective-permute-done.4.refs_1_ = bf16[128,1152]{1,0:T(8,128)(2,1)S(1)} collective-permute-done((bf16[128,1152]{1,0:T(8,128)(2,1)S(1)}, bf16[128,1152]{1,0:T(8,128)(2,1)S(1)}, u32[]{:S(2)}, u32[]{:S(2)}) %collective-permute-start.4) | collective-permute-done | bytes 294944 | tf_op jit(solution)/shard_map/ppermute | solution.py:34
  46.8 0.1 shard_map.91.refs_7_.refs_8_
  46.9 2.6 %collective-permute-start.12 = (bf16[512,1152]{1,0:T(8,128)(2,1)S(1)}, bf16[512,1152]{1,0:T(8,128)(2,1)S(1)}, u32[]{:S(2)}, u32[]{:S(2)}) collective-permute-start(bf16[512,1152]{1,0:T(8,128)(2,1)S(1)} %shard_map.91.refs_7_.refs_8_), channel_id=1, source_target_pairs={{0,3},{2,0},{1,2},{3,1},{4,7},{6,4},{5,6},{7,5},{8,11},{10,8},{9,1... | collective-permute-start | bytes 3538952 | tf_op jit(solution)/shard_map/ppermute | solution.py:34
  49.5 0.0 collective-permute-start.11
  49.5 0.0 collective-permute-start.6
  49.5 2.7 %collective-permute-start.7 = (bf16[128,1152]{1,0:T(8,128)(2,1)S(1)}, bf16[128,1152]{1,0:T(8,128)(2,1)}, u32[]{:S(2)}, u32[]{:S(2)}) collective-permute-start(bf16[128,1152]{1,0:T(8,128)(2,1)S(1)} %collective-permute-done.5.refs_2_), channel_id=1, source_target_pairs={{0,112},{2,114},{1,113},{3,115},{4,116},{6,118},{5,117},{7,119},{8... | collective-permute-start | bytes 884744 | tf_op jit(solution)/shard_map/ppermute | solution.py:34
  52.2 7.2 %collective-permute-done.6.refs_3_ = bf16[128,1152]{1,0:T(8,128)(2,1)} collective-permute-done((bf16[128,1152]{1,0:T(8,128)(2,1)S(1)}, bf16[128,1152]{1,0:T(8,128)(2,1)}, u32[]{:S(2)}, u32[]{:S(2)}) %collective-permute-start.6) | collective-permute-done | bytes 294944 | tf_op jit(solution)/shard_map/ppermute | solution.py:34
  59.4 0.0 collective-permute-start.8
  59.4 0.0 collective-permute-done.7.refs_4_
  59.4 2.7 %collective-permute-start.9 = (bf16[128,1152]{1,0:T(8,128)(2,1)}, bf16[128,1152]{1,0:T(8,128)(2,1)S(1)}, u32[]{:S(2)}, u32[]{:S(2)}) collective-permute-start(bf16[128,1152]{1,0:T(8,128)(2,1)} %collective-permute-done.7.refs_4_), channel_id=1, source_target_pairs={{0,112},{2,114},{1,113},{3,115},{4,116},{6,118},{5,117},{7,119},{8... | collective-permute-start | bytes 884744 | tf_op jit(solution)/shard_map/ppermute | solution.py:34
  62.2 0.5 collective-permute-done.12.refs_9_.refs_10_
  62.7 0.0 copy-start.7
  62.7 3.6 %collective-permute-start.15 = (bf16[256,1152]{1,0:T(8,128)(2,1)S(1)}, bf16[256,1152]{1,0:T(8,128)(2,1)S(1)}, u32[]{:S(2)}, u32[]{:S(2)}) collective-permute-start(bf16[256,1152]{1,0:T(8,128)(2,1)S(1)} %slice.9), channel_id=1, source_target_pairs={{0,3},{2,0},{1,2},{3,1},{4,7},{6,4},{5,6},{7,5},{8,11},{10,8},{9,1... | collective-permute-start | bytes 1769480 | tf_op jit(solution)/shard_map/ppermute | solution.py:34
  66.3 0.0 collective-permute-done.11.refs_8_.refs_9_
  66.3 1.1 slice.8
  67.4 0.1 collective-permute-start.14
  67.5 1.0 collective-permute-done.8.refs_5_
  68.5 0.0 collective-permute-done.9.refs_6_
  68.6 2.8 %collective-permute-start.13 = (bf16[128,1152]{1,0:T(8,128)(2,1)S(1)}, bf16[128,1152]{1,0:T(8,128)(2,1)S(1)}, u32[]{:S(2)}, u32[]{:S(2)}) collective-permute-start(bf16[128,1152]{1,0:T(8,128)(2,1)S(1)} %broadcast_select_fusion), channel_id=1, source_target_pairs={{0,16},{2,18},{1,17},{3,19},{4,20},{6,22},{5,21},{7,23},{8,24},{10... | collective-permute-start | bytes 884744 | tf_op jit(solution)/shard_map/ppermute | solution.py:34
  71.4 5.9 %shard_map.92.early_ref = f32[8,128]{1,0:T(8,128)S(1)} custom-call(bf16[128,1152]{1,0:T(8,128)(2,1)S(1)} %copy-done.7, bf16[128,1152]{1,0:T(8,128)(2,1)S(1)} %copy-done.11, bf16[128,1152]{1,0:T(8,128)(2,1)S(1)} %copy-done.9, bf16[128,1152]{1,0:T(8,128)(2,1)} %collective-permute-done.6.refs_3_, bf16[128,1152]{1,0:T(8,128)(2,1)} %collective-permute-done.7.refs_4_, ...), custom_call_target="tpu_custom_call" | custom-call | flops 2415919104 | bytes 1048576 | tf_op jit(solution)/shard_map/pallas_call | solution.py:64
  77.3 0.4 collective-permute-done.14.refs_11_
  77.8 8.4 %shard_map.93 = bf16[256,1280]{1,0:T(8,128)(2,1)} custom-call(s32[6]{0:T(128)S(1)} %stack.27.pos_ref, f32[128,128]{1,0:T(8,128)S(1)} %copy-done.14, f32[128,128]{1,0:T(8,128)S(1)} %copy-done.1, f32[8,128]{1,0:T(8,128)S(1)} %shard_map.92.early_ref, bf16[128,1152]{1,0:T(8,128)(2,1)S(1)} %copy-done.7, bf16[128,1152]{1,0:T(8,128)(2,1)S(1)} %copy-done.11, ...), custom_call_target="tpu_custom_call" | custom-call | flops 4831838208 | bytes 1048576 | tf_op jit(solution)/shard_map/pallas_call | solution.py:64
  86.1 3.7 %all-to-all-start = ((bf16[8,32,1280]{2,1,0:T(8,128)(2,1)}), bf16[8,32,1280]{2,1,0:T(8,128)(2,1)S(1)}, u32[]{:S(2)}, u32[]{:S(2)}) async-start(bf16[8,32,1280]{2,1,0:T(8,128)(2,1)} %bitcast.11), calls=%async_computation | async-start | bytes 1310720 | tf_op jit(solution)/shard_map/all_to_all | solution.py:462
  89.8 1.0 shard_map.94
  90.8 19.7 %all-to-all-done = bf16[8,32,1280]{2,1,0:T(8,128)(2,1)S(1)} async-done(((bf16[8,32,1280]{2,1,0:T(8,128)(2,1)}), bf16[8,32,1280]{2,1,0:T(8,128)(2,1)S(1)}, u32[]{:S(2)}, u32[]{:S(2)}) %all-to-all-start) | async-done | bytes 655392 | tf_op jit(solution)/shard_map/all_to_all | solution.py:462
  110.5 0.2 shard_map.95
  110.7 0.6 collective-permute-start.16
  111.3 0.9 collective-permute-done.16.recv_ref
  112.2 1.7 %shard_map.96 = (f32[1,128]{1,0:T(1,128)}, f32[576,128]{1,0:T(8,128)}) custom-call(s32[6]{0:T(128)S(1)} %stack.27.pos_ref, f32[40,576]{1,0:T(8,128)S(1)} %get-tuple-element.54.keep_ref, f32[40,576]{1,0:T(8,128)S(1)} %collective-permute-done.16.recv_ref, f32[128,128]{1,0:T(8,128)S(1)} %copy-done.2), custom_call_target="tpu_custom_call" | custom-call | flops 29491200 | bytes 1048576 | tf_op jit(solution)/shard_map/pallas_call | solution.py:64
  (33 shorter events, 0.1 us)
Async XLA Ops:
  0.7 0.7 copy-start.5
  4.5 13.2 %collective-permute-start = (bf16[128,1152]{1,0:T(8,128)(2,1)S(1)}, bf16[128,1152]{1,0:T(8,128)(2,1)S(1)}, u32[]{:S(2)}, u32[]{:S(2)}) collective-permute-start(bf16[128,1152]{1,0:T(8,128)(2,1)S(1)} %get-tuple-element.39), channel_id=1, source_target_pairs={{0,1},{2,3},{1,0},{3,2},{4,5},{6,7},{5,4},{7,6},{8,9},{10,11},{9,8... | collective-permute-start | bytes 884744 | tf_op jit(solution)/shard_map/ppermute | solution.py:34
  8.3 12.5 %copy-start.12 = (s32[2048]{0:T(1024)S(1)}, s32[2048]{0:T(1024)}, u32[]{:S(2)}) copy-start(s32[2048]{0:T(1024)} %param.13) | copy-start | bytes 24580
  17.6 9.2 %collective-permute-start.1 = (bf16[128,1152]{1,0:T(8,128)(2,1)S(1)}, bf16[128,1152]{1,0:T(8,128)(2,1)S(1)}, u32[]{:S(2)}, u32[]{:S(2)}) collective-permute-start(bf16[128,1152]{1,0:T(8,128)(2,1)S(1)} %get-tuple-element.40), channel_id=1, source_target_pairs={{0,1},{2,3},{1,0},{3,2},{4,5},{6,7},{5,4},{7,6},{8,9},{10,11},{9,8... | collective-permute-start | bytes 884744 | tf_op jit(solution)/shard_map/ppermute | solution.py:34
  17.9 11.9 %collective-permute-start.3 = (bf16[128,1152]{1,0:T(8,128)(2,1)S(1)}, bf16[128,1152]{1,0:T(8,128)(2,1)S(1)}, u32[]{:S(2)}, u32[]{:S(2)}) collective-permute-start(bf16[128,1152]{1,0:T(8,128)(2,1)S(1)} %shard_map.90.refs_0_), channel_id=1, source_target_pairs={{0,12},{2,14},{1,13},{3,15},{4,0},{6,2},{5,1},{7,3},{8,4},{10,6},{... | collective-permute-start | bytes 884744 | tf_op jit(solution)/shard_map/ppermute | solution.py:34
  20.8 10.3 %collective-permute-start.2 = (bf16[128,1152]{1,0:T(8,128)(2,1)S(1)}, bf16[128,1152]{1,0:T(8,128)(2,1)S(1)}, u32[]{:S(2)}, u32[]{:S(2)}) collective-permute-start(bf16[128,1152]{1,0:T(8,128)(2,1)S(1)} %shard_map.90.refs_0_), channel_id=1, source_target_pairs={{0,4},{2,6},{1,5},{3,7},{4,8},{6,10},{5,9},{7,11},{8,12},{10,14},{... | collective-permute-start | bytes 884744 | tf_op jit(solution)/shard_map/ppermute | solution.py:34
  21.2 0.6 copy-start
  21.9 25.1 %copy-start.13 = (f32[128,128]{1,0:T(8,128)}, f32[128,128]{1,0:T(8,128)S(1)}, u32[]{:S(2)}) copy-start(f32[128,128]{1,0:T(8,128)S(1)} %get-tuple-element.35.chosen_ref) | copy-start | bytes 196612
  27.0 32.4 %copy-start.3 = (f32[128,128]{1,0:T(8,128)}, f32[128,128]{1,0:T(8,128)S(1)}, u32[]{:S(2)}) copy-start(f32[128,128]{1,0:T(8,128)S(1)} %get-tuple-element.51.n_ref) | copy-start | bytes 196612
  27.0 32.4 %copy-start.6 = (bf16[128,1152]{1,0:T(8,128)(2,1)}, bf16[128,1152]{1,0:T(8,128)(2,1)S(1)}, u32[]{:S(2)}) copy-start(bf16[128,1152]{1,0:T(8,128)(2,1)S(1)} %get-tuple-element.44.refs_0_) | copy-start | bytes 884740
  31.1 12.3 %collective-permute-start.5 = (bf16[128,1152]{1,0:T(8,128)(2,1)S(1)}, bf16[128,1152]{1,0:T(8,128)(2,1)S(1)}, u32[]{:S(2)}, u32[]{:S(2)}) collective-permute-start(bf16[128,1152]{1,0:T(8,128)(2,1)S(1)} %get-tuple-element.44.refs_0_), channel_id=1, source_target_pairs={{0,112},{2,114},{1,113},{3,115},{4,116},{6,118},{5,117},{7,119},{8... | collective-permute-start | bytes 884744 | tf_op jit(solution)/shard_map/ppermute | solution.py:34
  36.7 10.1 %collective-permute-start.4 = (bf16[128,1152]{1,0:T(8,128)(2,1)S(1)}, bf16[128,1152]{1,0:T(8,128)(2,1)S(1)}, u32[]{:S(2)}, u32[]{:S(2)}) collective-permute-start(bf16[128,1152]{1,0:T(8,128)(2,1)S(1)} %get-tuple-element.44.refs_0_), channel_id=1, source_target_pairs={{0,16},{2,18},{1,17},{3,19},{4,20},{6,22},{5,21},{7,23},{8,24},{10... | collective-permute-start | bytes 884744 | tf_op jit(solution)/shard_map/ppermute | solution.py:34
  36.7 10.1 %collective-permute-start.10 = (bf16[128,1152]{1,0:T(8,128)(2,1)S(1)}, bf16[128,1152]{1,0:T(8,128)(2,1)S(1)}, u32[]{:S(2)}, u32[]{:S(2)}) collective-permute-start(bf16[128,1152]{1,0:T(8,128)(2,1)S(1)} %shard_map.90.refs_0_), channel_id=1, source_target_pairs={{0,8},{2,10},{1,9},{3,11},{4,12},{6,14},{5,13},{7,15},{8,0},{10,2}... | collective-permute-start | bytes 884744 | tf_op jit(solution)/shard_map/ppermute | solution.py:34
  43.4 16.0 %copy-start.8 = (bf16[128,1152]{1,0:T(8,128)(2,1)}, bf16[128,1152]{1,0:T(8,128)(2,1)S(1)}, u32[]{:S(2)}) copy-start(bf16[128,1152]{1,0:T(8,128)(2,1)S(1)} %collective-permute-done.5.refs_2_) | copy-start | bytes 884740
  46.8 5.3 %copy-start.10 = (bf16[128,1152]{1,0:T(8,128)(2,1)}, bf16[128,1152]{1,0:T(8,128)(2,1)S(1)}, u32[]{:S(2)}) copy-start(bf16[128,1152]{1,0:T(8,128)(2,1)S(1)} %collective-permute-done.4.refs_1_) | copy-start | bytes 884740
  46.9 15.7 %collective-permute-start.12 = (bf16[512,1152]{1,0:T(8,128)(2,1)S(1)}, bf16[512,1152]{1,0:T(8,128)(2,1)S(1)}, u32[]{:S(2)}, u32[]{:S(2)}) collective-permute-start(bf16[512,1152]{1,0:T(8,128)(2,1)S(1)} %shard_map.91.refs_7_.refs_8_), channel_id=1, source_target_pairs={{0,3},{2,0},{1,2},{3,1},{4,7},{6,4},{5,6},{7,5},{8,11},{10,8},{9,1... | collective-permute-start | bytes 3538952 | tf_op jit(solution)/shard_map/ppermute | solution.py:34
  49.5 16.8 %collective-permute-start.11 = (bf16[512,1152]{1,0:T(8,128)(2,1)S(1)}, bf16[512,1152]{1,0:T(8,128)(2,1)}, u32[]{:S(2)}, u32[]{:S(2)}) collective-permute-start(bf16[512,1152]{1,0:T(8,128)(2,1)S(1)} %shard_map.91.refs_7_.refs_8_), channel_id=1, source_target_pairs={{0,2},{2,1},{1,3},{3,0},{4,6},{6,5},{5,7},{7,4},{8,10},{10,9},{9,1... | collective-permute-start | bytes 3538952 | tf_op jit(solution)/shard_map/ppermute | solution.py:34
  49.5 9.9 %collective-permute-start.6 = (bf16[128,1152]{1,0:T(8,128)(2,1)S(1)}, bf16[128,1152]{1,0:T(8,128)(2,1)}, u32[]{:S(2)}, u32[]{:S(2)}) collective-permute-start(bf16[128,1152]{1,0:T(8,128)(2,1)S(1)} %collective-permute-done.4.refs_1_), channel_id=1, source_target_pairs={{0,16},{2,18},{1,17},{3,19},{4,20},{6,22},{5,21},{7,23},{8,24},{10... | collective-permute-start | bytes 884744 | tf_op jit(solution)/shard_map/ppermute | solution.py:34
  49.5 9.9 %collective-permute-start.7 = (bf16[128,1152]{1,0:T(8,128)(2,1)S(1)}, bf16[128,1152]{1,0:T(8,128)(2,1)}, u32[]{:S(2)}, u32[]{:S(2)}) collective-permute-start(bf16[128,1152]{1,0:T(8,128)(2,1)S(1)} %collective-permute-done.5.refs_2_), channel_id=1, source_target_pairs={{0,112},{2,114},{1,113},{3,115},{4,116},{6,118},{5,117},{7,119},{8... | collective-permute-start | bytes 884744 | tf_op jit(solution)/shard_map/ppermute | solution.py:34
  59.4 9.1 %collective-permute-start.8 = (bf16[128,1152]{1,0:T(8,128)(2,1)}, bf16[128,1152]{1,0:T(8,128)(2,1)S(1)}, u32[]{:S(2)}, u32[]{:S(2)}) collective-permute-start(bf16[128,1152]{1,0:T(8,128)(2,1)} %collective-permute-done.6.refs_3_), channel_id=1, source_target_pairs={{0,16},{2,18},{1,17},{3,19},{4,20},{6,22},{5,21},{7,23},{8,24},{10... | collective-permute-start | bytes 884744 | tf_op jit(solution)/shard_map/ppermute | solution.py:34
  59.4 9.1 %collective-permute-start.9 = (bf16[128,1152]{1,0:T(8,128)(2,1)}, bf16[128,1152]{1,0:T(8,128)(2,1)S(1)}, u32[]{:S(2)}, u32[]{:S(2)}) collective-permute-start(bf16[128,1152]{1,0:T(8,128)(2,1)} %collective-permute-done.7.refs_4_), channel_id=1, source_target_pairs={{0,112},{2,114},{1,113},{3,115},{4,116},{6,118},{5,117},{7,119},{8... | collective-permute-start | bytes 884744 | tf_op jit(solution)/shard_map/ppermute | solution.py:34
  62.7 8.7 %copy-start.7 = (bf16[128,1152]{1,0:T(8,128)(2,1)S(1)}, bf16[128,1152]{1,0:T(8,128)(2,1)}, u32[]{:S(2)}) copy-start(bf16[128,1152]{1,0:T(8,128)(2,1)} %copy-done.6) | copy-start | bytes 884740
  62.7 8.7 %copy-start.9 = (bf16[128,1152]{1,0:T(8,128)(2,1)S(1)}, bf16[128,1152]{1,0:T(8,128)(2,1)}, u32[]{:S(2)}) copy-start(bf16[128,1152]{1,0:T(8,128)(2,1)} %copy-done.8) | copy-start | bytes 884740
  62.7 8.7 %copy-start.11 = (bf16[128,1152]{1,0:T(8,128)(2,1)S(1)}, bf16[128,1152]{1,0:T(8,128)(2,1)}, u32[]{:S(2)}) copy-start(bf16[128,1152]{1,0:T(8,128)(2,1)} %copy-done.10) | copy-start | bytes 884740
  62.7 14.6 %collective-permute-start.15 = (bf16[256,1152]{1,0:T(8,128)(2,1)S(1)}, bf16[256,1152]{1,0:T(8,128)(2,1)S(1)}, u32[]{:S(2)}, u32[]{:S(2)}) collective-permute-start(bf16[256,1152]{1,0:T(8,128)(2,1)S(1)} %slice.9), channel_id=1, source_target_pairs={{0,3},{2,0},{1,2},{3,1},{4,7},{6,4},{5,6},{7,5},{8,11},{10,8},{9,1... | collective-permute-start | bytes 1769480 | tf_op jit(solution)/shard_map/ppermute | solution.py:34
  67.4 10.3 %collective-permute-start.14 = (bf16[256,1152]{1,0:T(8,128)(2,1)S(1)}, bf16[256,1152]{1,0:T(8,128)(2,1)S(1)}, u32[]{:S(2)}, u32[]{:S(2)}) collective-permute-start(bf16[256,1152]{1,0:T(8,128)(2,1)S(1)} %slice.8), channel_id=1, source_target_pairs={{0,2},{2,1},{1,3},{3,0},{4,6},{6,5},{5,7},{7,4},{8,10},{10,9},{9,1... | collective-permute-start | bytes 1769480 | tf_op jit(solution)/shard_map/ppermute | solution.py:34
  68.6 9.2 %copy-start.1 = (f32[128,128]{1,0:T(8,128)S(1)}, f32[128,128]{1,0:T(8,128)}, u32[]{:S(2)}) copy-start(f32[128,128]{1,0:T(8,128)} %copy-done) | copy-start | bytes 196612
  68.6 9.2 %copy-start.14 = (f32[128,128]{1,0:T(8,128)S(1)}, f32[128,128]{1,0:T(8,128)}, u32[]{:S(2)}) copy-start(f32[128,128]{1,0:T(8,128)} %copy-done.13) | copy-start | bytes 196612
  68.6 8.7 %collective-permute-start.13 = (bf16[128,1152]{1,0:T(8,128)(2,1)S(1)}, bf16[128,1152]{1,0:T(8,128)(2,1)S(1)}, u32[]{:S(2)}, u32[]{:S(2)}) collective-permute-start(bf16[128,1152]{1,0:T(8,128)(2,1)S(1)} %broadcast_select_fusion), channel_id=1, source_target_pairs={{0,16},{2,18},{1,17},{3,19},{4,20},{6,22},{5,21},{7,23},{8,24},{10... | collective-permute-start | bytes 884744 | tf_op jit(solution)/shard_map/ppermute | solution.py:34
  86.1 3.7 %copy-start.2 = (f32[128,128]{1,0:T(8,128)S(1)}, f32[128,128]{1,0:T(8,128)}, u32[]{:S(2)}) copy-start(f32[128,128]{1,0:T(8,128)} %copy-done) | copy-start | bytes 196612
  86.1 3.7 %copy-start.4 = (f32[128,128]{1,0:T(8,128)S(1)}, f32[128,128]{1,0:T(8,128)}, u32[]{:S(2)}) copy-start(f32[128,128]{1,0:T(8,128)} %copy-done.3) | copy-start | bytes 196612
  86.1 24.4 %all-to-all-start = ((bf16[8,32,1280]{2,1,0:T(8,128)(2,1)}), bf16[8,32,1280]{2,1,0:T(8,128)(2,1)S(1)}, u32[]{:S(2)}, u32[]{:S(2)}) async-start(bf16[8,32,1280]{2,1,0:T(8,128)(2,1)} %bitcast.11), calls=%async_computation | async-start | bytes 1310720 | tf_op jit(solution)/shard_map/all_to_all | solution.py:462
  110.7 1.5 %collective-permute-start.16 = (f32[40,576]{1,0:T(8,128)S(1)}, f32[40,576]{1,0:T(8,128)S(1)}, u32[]{:S(2)}, u32[]{:S(2)}) collective-permute-start(f32[40,576]{1,0:T(8,128)S(1)} %get-tuple-element.55), channel_id=1, source_target_pairs={{0,128},{2,130},{1,129},{3,131},{4,132},{6,134},{5,133},{7,135},{8... | collective-permute-start | bytes 276488 | tf_op jit(solution)/shard_map/ppermute | solution.py:34

commit v8 on v7

--- a/solution.py
+++ b/solution.py
@@ -97,6 +97,18 @@
     other_ref[...] = other.astype(jnp.bfloat16)
 
 
+CHUNK = 384
+
+
+def chunk_copies(source, target, sems, first):
+    return [
+        pltpu.make_async_copy(
+            source.at[:, pl.ds(start, CHUNK)], target.at[:, pl.ds(start, CHUNK)], sems.at[first + k]
+        )
+        for k, start in enumerate(range(0, target.shape[1], CHUNK))
+    ]
+
+
 def front_kernel(
     pos_ref, x_hbm, gain_hbm, text_hbm, head_hbm,
     own_ref, other_ref, normed_ref, own_x_ref,
@@ -105,9 +117,10 @@
     copies = [
         pltpu.make_async_copy(source, target, sems.at[k])
         for k, (source, target) in enumerate(
-            [(x_hbm, x_ref), (gain_hbm, gain_ref), (text_hbm, text_ref), (head_hbm, head_ref)]
+            [(x_hbm, x_ref), (gain_hbm, gain_ref), (text_hbm, text_ref)]
         )
     ]
+    copies += chunk_copies(head_hbm, head_ref, sems, 3)
     for c in copies:
         c.start()
     m = pos_ref[0]
@@ -121,11 +134,14 @@
     normed_ref[...] = (gap * lax.rsqrt(var + EPS) * gain_ref[...]).astype(jnp.bfloat16)
     own_x_ref[...] = x_ref[pl.ds(pl.multiple_of(m * rows, rows), rows), :]
     copies[2].wait()
-    copies[3].wait()
     depth = head_ref.shape[0]
     text = text_ref[...]
     part = jnp.where(m == 0, text[:, :depth], text[:, depth:])
-    acc_ref[...] = jnp.dot(part, head_ref[...], preferred_element_type=jnp.float32)
+    for k, start in enumerate(range(0, acc_ref.shape[1], CHUNK)):
+        copies[3 + k].wait()
+        acc_ref[:, start : start + CHUNK] = jnp.dot(
+            part, head_ref[:, start : start + CHUNK], preferred_element_type=jnp.float32
+        )
     split_rows(acc_ref, m, own_ref, other_ref)
 
 
@@ -145,7 +161,7 @@
             shape((half, width), bf16),
         ],
         scratch_shapes=[pltpu.VMEM(a.shape, a.dtype) for a in arrays]
-        + [pltpu.VMEM((rows, width), jnp.float32), pltpu.SemaphoreType.DMA((len(arrays),))],
+        + [pltpu.VMEM((rows, width), jnp.float32), pltpu.SemaphoreType.DMA((3 + width // CHUNK,))],
         compiler_params=pltpu.CompilerParams(vmem_limit_bytes=52 * 1024 * 1024),
         cost_estimate=pl.CostEstimate(
             flops=2 * rows * width * head.shape[0], bytes_accessed=4 << 20, transcendentals=0
@@ -157,11 +173,12 @@
     pos_ref, normed_ref, own_x_ref, up_hbm, down_hbm, own_ref, other_ref,
     up_ref, down_ref, hidden_ref, acc_ref, sems,
 ):
-    first = pltpu.make_async_copy(up_hbm, up_ref, sems.at[0])
-    second = pltpu.make_async_copy(down_hbm, down_ref, sems.at[1])
-    first.start()
-    first.wait()
-    second.start()
+    ups = chunk_copies(up_hbm, up_ref, sems, 0)
+    downs = chunk_copies(down_hbm, down_ref, sems, len(ups))
+    for c in ups + downs:
+        c.start()
+    for c in ups:
+        c.wait()
     total, block = up_ref.shape[0], 512
     for start in range(0, total, block):
         stop = min(start + block, total)
@@ -172,11 +189,10 @@
             preferred_element_type=jnp.float32,
         )
         hidden_ref[:, start:stop] = jax.nn.gelu(acc, approximate=True).astype(jnp.bfloat16)
-    second.wait()
-    block = 384
-    for start in range(0, acc_ref.shape[1], block):
-        acc_ref[:, start : start + block] = jnp.dot(
-            hidden_ref[...], down_ref[:, start : start + block], preferred_element_type=jnp.float32
+    for k, start in enumerate(range(0, acc_ref.shape[1], CHUNK)):
+        downs[k].wait()
+        acc_ref[:, start : start + CHUNK] = jnp.dot(
+            hidden_ref[...], down_ref[:, start : start + CHUNK], preferred_element_type=jnp.float32
         )
     split_rows(acc_ref, pos_ref[0], own_ref, other_ref)
     own_ref[...] = own_ref[...] + own_x_ref[...].astype(jnp.float32)
@@ -196,7 +212,7 @@
             pltpu.VMEM(down.shape, bf16),
             pltpu.VMEM((rows, hidden), bf16),
             pltpu.VMEM((rows, width), jnp.float32),
-            pltpu.SemaphoreType.DMA((2,)),
+            pltpu.SemaphoreType.DMA((2 * (width // CHUNK),)),
         ],
         compiler_params=pltpu.CompilerParams(vmem_limit_bytes=52 * 1024 * 1024),
         cost_estimate=pl.CostEstimate(

time: 114 us -> 113 us (level)
  starting transfers between devices: 32.4 us -> 34.6 us
  waiting for transfers between devices: 47.5 us -> 45.3 us
  Pallas kernels: 30.5 us -> 29.1 us
    ppermute x17, starting transfers between devices: 28.7 us -> 31 us  [permute(): return lax.ppermute(v, AXES, perm)]
    pallas_call x1, Pallas kernels: 9.31 us -> 7.61 us  [image_mlp(): pl.pallas_call(mlp_kernel, in_specs=[pl.BlockSpec(memory_space=pltpu.SMEM...]
    ppermute x17, waiting for transfers between devices: 27.9 us -> 26.3 us  [permute(): return lax.ppermute(v, AXES, perm)]
  transfers between devices with their start and end apart: 18 -> 18, of which waited for: 11 -> 11; matrix products, arithmetic and copies ran while one was open for 1% -> 1% of each run, Pallas kernels for 15% -> 14%
where the time goes in v8:
time: 113 us
  waiting for transfers between devices  45.3 us (40%)
  starting transfers between devices  34.6 us (31%)
  Pallas kernels  29.1 us (26%)
  local copies, waits for them, and re-layouts  2.61 us (2%)
    ppermute x17, starting transfers between devices, permute(): return lax.ppermute(v, AXES, perm)  31 us
    ppermute x17, waiting for transfers between devices, permute(): return lax.ppermute(v, AXES, perm)  26.3 us
    all_to_all x1, waiting for transfers between devices, shards(): load = lax.all_to_all(load, 'z', 0, 0, tiled=True)  19 us
    pallas_call x9, Pallas kernels, call(): pl.pallas_call(kernel, in_specs=[pl.BlockSpec(memory_space=pltpu.SMEM)] *...  18.1 us
    pallas_call x1, Pallas kernels, image_mlp(): pl.pallas_call(mlp_kernel, in_specs=[pl.BlockSpec(memory_space=pltpu.SMEM...  7.61 us
    all_to_all x1, starting transfers between devices, shards(): load = lax.all_to_all(load, 'z', 0, 0, tiled=True)  3.67 us
    pallas_call x1, Pallas kernels, front(): pl.pallas_call(front_kernel, in_specs=[pl.BlockSpec(memory_space=pltpu.SM...  3.37 us
  transfers between devices with their start and end apart: 18, of which 11 were waited for; matrix products, arithmetic and copies ran while one was open for 1% of the time, Pallas kernels for 14%

profile of v8, /device:TPU:1, one launch (start us, length us, event | category | flops | bytes accessed | tf_op | source)
XLA Modules:
  0.0 112.6 jit_solution(15880743542628312311)
XLA Ops:
  0.6 0.1 stack.27.pos_ref
  0.7 0.7 copy-done.5
  1.4 3.4 %shard_map.86 = (f32[128,1152]{1,0:T(8,128)S(1)}, bf16[128,1152]{1,0:T(8,128)(2,1)S(1)}, bf16[256,1152]{1,0:T(8,128)(2,1)S(1)}, bf16[128,1152]{1,0:T(8,128)(2,1)S(1)}) custom-call(s32[6]{0:T(128)S(1)} %stack.27.pos_ref, bf16[256,1152]{1,0:T(8,128)(2,1)} %x_hbm.1, f32[1,1152]{1,0:T(1,128)S(1)} %copy-done.5, bf16[256,1152]{1,0:T(8,128)(2,1)} %text_hbm.1, ...), custom_call_target="tpu_custom_call" | custom-call | flops 339738624 | bytes 4194304 | tf_op jit(solution)/shard_map/pallas_call | solution.py:153
  4.8 3.8 %collective-permute-start = (bf16[128,1152]{1,0:T(8,128)(2,1)S(1)}, bf16[128,1152]{1,0:T(8,128)(2,1)S(1)}, u32[]{:S(2)}, u32[]{:S(2)}) collective-permute-start(bf16[128,1152]{1,0:T(8,128)(2,1)S(1)} %get-tuple-element.39), channel_id=1, source_target_pairs={{0,1},{2,3},{1,0},{3,2},{4,5},{6,7},{5,4},{7,6},{8,9},{10,11},{9,8... | collective-permute-start | bytes 884744 | tf_op jit(solution)/shard_map/ppermute | solution.py:34
  8.6 7.6 %shard_map.87 = (f32[128,1152]{1,0:T(8,128)S(1)}, bf16[128,1152]{1,0:T(8,128)(2,1)S(1)}) custom-call(s32[6]{0:T(128)S(1)} %stack.27.pos_ref, bf16[256,1152]{1,0:T(8,128)(2,1)S(1)} %get-tuple-element.30.normed_ref, bf16[128,1152]{1,0:T(8,128)(2,1)S(1)} %get-tuple-element.31.own_x_ref, bf16[2152,1152]{1,0:T(8,128)(2,1)} %bitcast.18, bf16[2152,1152]{1,0:T(8,128)(2,1)} %bitcast.19), custom_call_target="tpu_custom_call" | custom-call | flops 2538602496 | bytes 11534336 | tf_op jit(solution)/shard_map/pallas_call | solution.py:205
  16.2 0.0 collective-permute-done.recv_ref
  16.3 1.8 %collective-permute-start.1 = (bf16[128,1152]{1,0:T(8,128)(2,1)S(1)}, bf16[128,1152]{1,0:T(8,128)(2,1)S(1)}, u32[]{:S(2)}, u32[]{:S(2)}) collective-permute-start(bf16[128,1152]{1,0:T(8,128)(2,1)S(1)} %get-tuple-element.40), channel_id=1, source_target_pairs={{0,1},{2,3},{1,0},{3,2},{4,5},{6,7},{5,4},{7,6},{8,9},{10,11},{9,8... | collective-permute-start | bytes 884744 | tf_op jit(solution)/shard_map/ppermute | solution.py:34
  18.0 0.2 shard_map.90.refs_0_
  18.2 1.2 %collective-permute-start.3 = (bf16[128,1152]{1,0:T(8,128)(2,1)S(1)}, bf16[128,1152]{1,0:T(8,128)(2,1)S(1)}, u32[]{:S(2)}, u32[]{:S(2)}) collective-permute-start(bf16[128,1152]{1,0:T(8,128)(2,1)S(1)} %shard_map.90.refs_0_), channel_id=1, source_target_pairs={{0,12},{2,14},{1,13},{3,15},{4,0},{6,2},{5,1},{7,3},{8,4},{10,6},{... | collective-permute-start | bytes 884744 | tf_op jit(solution)/shard_map/ppermute | solution.py:34
  19.4 0.3 collective-permute-start.2
  19.7 0.5 shard_map.88
  20.2 0.6 copy-done
  20.8 4.6 %collective-permute-done.1.recv_ref = bf16[128,1152]{1,0:T(8,128)(2,1)S(1)} collective-permute-done((bf16[128,1152]{1,0:T(8,128)(2,1)S(1)}, bf16[128,1152]{1,0:T(8,128)(2,1)S(1)}, u32[]{:S(2)}, u32[]{:S(2)}) %collective-permute-start.1) | collective-permute-done | bytes 294944 | tf_op jit(solution)/shard_map/ppermute | solution.py:34
  25.4 0.2 shard_map.89
  25.7 0.0 copy-start.6
  25.7 3.5 %collective-permute-done.3.refs_2_ = bf16[128,1152]{1,0:T(8,128)(2,1)S(1)} collective-permute-done((bf16[128,1152]{1,0:T(8,128)(2,1)S(1)}, bf16[128,1152]{1,0:T(8,128)(2,1)S(1)}, u32[]{:S(2)}, u32[]{:S(2)}) %collective-permute-start.3) | collective-permute-done | bytes 294944 | tf_op jit(solution)/shard_map/ppermute | solution.py:34
  29.2 0.9 collective-permute-done.2.refs_1_
  30.0 5.6 %collective-permute-start.5 = (bf16[128,1152]{1,0:T(8,128)(2,1)S(1)}, bf16[128,1152]{1,0:T(8,128)(2,1)S(1)}, u32[]{:S(2)}, u32[]{:S(2)}) collective-permute-start(bf16[128,1152]{1,0:T(8,128)(2,1)S(1)} %get-tuple-element.44.refs_0_), channel_id=1, source_target_pairs={{0,112},{2,114},{1,113},{3,115},{4,116},{6,118},{5,117},{7,119},{8... | collective-permute-start | bytes 884744 | tf_op jit(solution)/shard_map/ppermute | solution.py:34
  35.6 1.4 %collective-permute-start.10 = (bf16[128,1152]{1,0:T(8,128)(2,1)S(1)}, bf16[128,1152]{1,0:T(8,128)(2,1)S(1)}, u32[]{:S(2)}, u32[]{:S(2)}) collective-permute-start(bf16[128,1152]{1,0:T(8,128)(2,1)S(1)} %shard_map.90.refs_0_), channel_id=1, source_target_pairs={{0,8},{2,10},{1,9},{3,11},{4,12},{6,14},{5,13},{7,15},{8,0},{10,2}... | collective-permute-start | bytes 884744 | tf_op jit(solution)/shard_map/ppermute | solution.py:34
  37.0 4.2 %collective-permute-done.5.refs_2_ = bf16[128,1152]{1,0:T(8,128)(2,1)S(1)} collective-permute-done((bf16[128,1152]{1,0:T(8,128)(2,1)S(1)}, bf16[128,1152]{1,0:T(8,128)(2,1)S(1)}, u32[]{:S(2)}, u32[]{:S(2)}) %collective-permute-start.5) | collective-permute-done | bytes 294944 | tf_op jit(solution)/shard_map/ppermute | solution.py:34
  41.2 3.1 %collective-permute-done.4.refs_1_ = bf16[128,1152]{1,0:T(8,128)(2,1)S(1)} collective-permute-done((bf16[128,1152]{1,0:T(8,128)(2,1)S(1)}, bf16[128,1152]{1,0:T(8,128)(2,1)S(1)}, u32[]{:S(2)}, u32[]{:S(2)}) %collective-permute-start.4) | collective-permute-done | bytes 294944 | tf_op jit(solution)/shard_map/ppermute | solution.py:34
  44.3 0.0 collective-permute-done.10.refs_3_
  44.3 0.1 shard_map.91.refs_7_.refs_8_
  44.4 3.7 %collective-permute-start.12 = (bf16[512,1152]{1,0:T(8,128)(2,1)S(1)}, bf16[512,1152]{1,0:T(8,128)(2,1)S(1)}, u32[]{:S(2)}, u32[]{:S(2)}) collective-permute-start(bf16[512,1152]{1,0:T(8,128)(2,1)S(1)} %shard_map.91.refs_7_.refs_8_), channel_id=1, source_target_pairs={{0,3},{2,0},{1,2},{3,1},{4,7},{6,4},{5,6},{7,5},{8,11},{10,8},{9,1... | collective-permute-start | bytes 3538952 | tf_op jit(solution)/shard_map/ppermute | solution.py:34
  48.1 0.0 collective-permute-start.11
  48.1 2.7 %collective-permute-start.7 = (bf16[128,1152]{1,0:T(8,128)(2,1)S(1)}, bf16[128,1152]{1,0:T(8,128)(2,1)}, u32[]{:S(2)}, u32[]{:S(2)}) collective-permute-start(bf16[128,1152]{1,0:T(8,128)(2,1)S(1)} %collective-permute-done.5.refs_2_), channel_id=1, source_target_pairs={{0,112},{2,114},{1,113},{3,115},{4,116},{6,118},{5,117},{7,119},{8... | collective-permute-start | bytes 884744 | tf_op jit(solution)/shard_map/ppermute | solution.py:34
  50.8 6.9 %collective-permute-done.6.refs_3_ = bf16[128,1152]{1,0:T(8,128)(2,1)} collective-permute-done((bf16[128,1152]{1,0:T(8,128)(2,1)S(1)}, bf16[128,1152]{1,0:T(8,128)(2,1)}, u32[]{:S(2)}, u32[]{:S(2)}) %collective-permute-start.6) | collective-permute-done | bytes 294944 | tf_op jit(solution)/shard_map/ppermute | solution.py:34
  57.7 0.0 collective-permute-done.7.refs_4_
  57.7 2.7 %collective-permute-start.9 = (bf16[128,1152]{1,0:T(8,128)(2,1)}, bf16[128,1152]{1,0:T(8,128)(2,1)S(1)}, u32[]{:S(2)}, u32[]{:S(2)}) collective-permute-start(bf16[128,1152]{1,0:T(8,128)(2,1)} %collective-permute-done.7.refs_4_), channel_id=1, source_target_pairs={{0,112},{2,114},{1,113},{3,115},{4,116},{6,118},{5,117},{7,119},{8... | collective-permute-start | bytes 884744 | tf_op jit(solution)/shard_map/ppermute | solution.py:34
  60.5 0.8 collective-permute-done.12.refs_9_.refs_10_
  61.3 0.0 copy-start.7
  61.3 3.6 %collective-permute-start.15 = (bf16[256,1152]{1,0:T(8,128)(2,1)S(1)}, bf16[256,1152]{1,0:T(8,128)(2,1)S(1)}, u32[]{:S(2)}, u32[]{:S(2)}) collective-permute-start(bf16[256,1152]{1,0:T(8,128)(2,1)S(1)} %slice.9), channel_id=1, source_target_pairs={{0,3},{2,0},{1,2},{3,1},{4,7},{6,4},{5,6},{7,5},{8,11},{10,8},{9,1... | collective-permute-start | bytes 1769480 | tf_op jit(solution)/shard_map/ppermute | solution.py:34
  64.9 1.1 slice.8
  66.1 0.1 collective-permute-start.14
  66.1 0.3 collective-permute-done.8.refs_5_
  66.5 0.0 collective-permute-done.9.refs_6_
  66.5 2.8 %collective-permute-start.13 = (bf16[128,1152]{1,0:T(8,128)(2,1)S(1)}, bf16[128,1152]{1,0:T(8,128)(2,1)S(1)}, u32[]{:S(2)}, u32[]{:S(2)}) collective-permute-start(bf16[128,1152]{1,0:T(8,128)(2,1)S(1)} %broadcast_select_fusion), channel_id=1, source_target_pairs={{0,16},{2,18},{1,17},{3,19},{4,20},{6,22},{5,21},{7,23},{8,24},{10... | collective-permute-start | bytes 884744 | tf_op jit(solution)/shard_map/ppermute | solution.py:34
  69.3 5.9 %shard_map.92.early_ref = f32[8,128]{1,0:T(8,128)S(1)} custom-call(bf16[128,1152]{1,0:T(8,128)(2,1)S(1)} %copy-done.7, bf16[128,1152]{1,0:T(8,128)(2,1)S(1)} %copy-done.11, bf16[128,1152]{1,0:T(8,128)(2,1)S(1)} %copy-done.9, bf16[128,1152]{1,0:T(8,128)(2,1)} %collective-permute-done.6.refs_3_, bf16[128,1152]{1,0:T(8,128)(2,1)} %collective-permute-done.7.refs_4_, ...), custom_call_target="tpu_custom_call" | custom-call | flops 2415919104 | bytes 1048576 | tf_op jit(solution)/shard_map/pallas_call | solution.py:64
  75.3 0.0 collective-permute-done.15.refs_12_
  75.3 1.1 collective-permute-done.14.refs_11_
  76.4 8.4 %shard_map.93 = bf16[256,1280]{1,0:T(8,128)(2,1)} custom-call(s32[6]{0:T(128)S(1)} %stack.27.pos_ref, f32[128,128]{1,0:T(8,128)S(1)} %copy-done.14, f32[128,128]{1,0:T(8,128)S(1)} %copy-done.1, f32[8,128]{1,0:T(8,128)S(1)} %shard_map.92.early_ref, bf16[128,1152]{1,0:T(8,128)(2,1)S(1)} %copy-done.7, bf16[128,1152]{1,0:T(8,128)(2,1)S(1)} %copy-done.11, ...), custom_call_target="tpu_custom_call" | custom-call | flops 4831838208 | bytes 1048576 | tf_op jit(solution)/shard_map/pallas_call | solution.py:64
  84.7 3.7 %all-to-all-start = ((bf16[8,32,1280]{2,1,0:T(8,128)(2,1)}), bf16[8,32,1280]{2,1,0:T(8,128)(2,1)S(1)}, u32[]{:S(2)}, u32[]{:S(2)}) async-start(bf16[8,32,1280]{2,1,0:T(8,128)(2,1)} %bitcast.11), calls=%async_computation | async-start | bytes 1310720 | tf_op jit(solution)/shard_map/all_to_all | solution.py:478
  88.4 1.0 shard_map.94
  89.4 19.0 %all-to-all-done = bf16[8,32,1280]{2,1,0:T(8,128)(2,1)S(1)} async-done(((bf16[8,32,1280]{2,1,0:T(8,128)(2,1)}), bf16[8,32,1280]{2,1,0:T(8,128)(2,1)S(1)}, u32[]{:S(2)}, u32[]{:S(2)}) %all-to-all-start) | async-done | bytes 655392 | tf_op jit(solution)/shard_map/all_to_all | solution.py:478
  108.4 0.2 shard_map.95
  108.7 1.3 %collective-permute-start.16 = (f32[40,576]{1,0:T(8,128)S(1)}, f32[40,576]{1,0:T(8,128)S(1)}, u32[]{:S(2)}, u32[]{:S(2)}) collective-permute-start(f32[40,576]{1,0:T(8,128)S(1)} %get-tuple-element.55), channel_id=1, source_target_pairs={{0,128},{2,130},{1,129},{3,131},{4,132},{6,134},{5,133},{7,135},{8... | collective-permute-start | bytes 276488 | tf_op jit(solution)/shard_map/ppermute | solution.py:34
  109.9 0.9 collective-permute-done.16.recv_ref
  110.9 1.7 %shard_map.96 = (f32[1,128]{1,0:T(1,128)}, f32[576,128]{1,0:T(8,128)}) custom-call(s32[6]{0:T(128)S(1)} %stack.27.pos_ref, f32[40,576]{1,0:T(8,128)S(1)} %get-tuple-element.54.keep_ref, f32[40,576]{1,0:T(8,128)S(1)} %collective-permute-done.16.recv_ref, f32[128,128]{1,0:T(8,128)S(1)} %copy-done.2), custom_call_target="tpu_custom_call" | custom-call | flops 29491200 | bytes 1048576 | tf_op jit(solution)/shard_map/pallas_call | solution.py:64
  (33 shorter events, 0.1 us)
Async XLA Ops:
  0.7 0.7 copy-start.5
  4.8 11.5 %collective-permute-start = (bf16[128,1152]{1,0:T(8,128)(2,1)S(1)}, bf16[128,1152]{1,0:T(8,128)(2,1)S(1)}, u32[]{:S(2)}, u32[]{:S(2)}) collective-permute-start(bf16[128,1152]{1,0:T(8,128)(2,1)S(1)} %get-tuple-element.39), channel_id=1, source_target_pairs={{0,1},{2,3},{1,0},{3,2},{4,5},{6,7},{5,4},{7,6},{8,9},{10,11},{9,8... | collective-permute-start | bytes 884744 | tf_op jit(solution)/shard_map/ppermute | solution.py:34
  8.6 11.1 %copy-start.12 = (s32[2048]{0:T(1024)S(1)}, s32[2048]{0:T(1024)}, u32[]{:S(2)}) copy-start(s32[2048]{0:T(1024)} %param.13) | copy-start | bytes 24580
  16.3 9.2 %collective-permute-start.1 = (bf16[128,1152]{1,0:T(8,128)(2,1)S(1)}, bf16[128,1152]{1,0:T(8,128)(2,1)S(1)}, u32[]{:S(2)}, u32[]{:S(2)}) collective-permute-start(bf16[128,1152]{1,0:T(8,128)(2,1)S(1)} %get-tuple-element.40), channel_id=1, source_target_pairs={{0,1},{2,3},{1,0},{3,2},{4,5},{6,7},{5,4},{7,6},{8,9},{10,11},{9,8... | collective-permute-start | bytes 884744 | tf_op jit(solution)/shard_map/ppermute | solution.py:34
  18.2 11.0 %collective-permute-start.3 = (bf16[128,1152]{1,0:T(8,128)(2,1)S(1)}, bf16[128,1152]{1,0:T(8,128)(2,1)S(1)}, u32[]{:S(2)}, u32[]{:S(2)}) collective-permute-start(bf16[128,1152]{1,0:T(8,128)(2,1)S(1)} %shard_map.90.refs_0_), channel_id=1, source_target_pairs={{0,12},{2,14},{1,13},{3,15},{4,0},{6,2},{5,1},{7,3},{8,4},{10,6},{... | collective-permute-start | bytes 884744 | tf_op jit(solution)/shard_map/ppermute | solution.py:34
  19.4 10.6 %collective-permute-start.2 = (bf16[128,1152]{1,0:T(8,128)(2,1)S(1)}, bf16[128,1152]{1,0:T(8,128)(2,1)S(1)}, u32[]{:S(2)}, u32[]{:S(2)}) collective-permute-start(bf16[128,1152]{1,0:T(8,128)(2,1)S(1)} %shard_map.90.refs_0_), channel_id=1, source_target_pairs={{0,4},{2,6},{1,5},{3,7},{4,8},{6,10},{5,9},{7,11},{8,12},{10,14},{... | collective-permute-start | bytes 884744 | tf_op jit(solution)/shard_map/ppermute | solution.py:34
  20.2 0.6 copy-start
  20.8 23.5 %copy-start.13 = (f32[128,128]{1,0:T(8,128)}, f32[128,128]{1,0:T(8,128)S(1)}, u32[]{:S(2)}) copy-start(f32[128,128]{1,0:T(8,128)S(1)} %get-tuple-element.35.chosen_ref) | copy-start | bytes 196612
  25.6 32.1 %copy-start.3 = (f32[128,128]{1,0:T(8,128)}, f32[128,128]{1,0:T(8,128)S(1)}, u32[]{:S(2)}) copy-start(f32[128,128]{1,0:T(8,128)S(1)} %get-tuple-element.51.n_ref) | copy-start | bytes 196612
  25.7 32.1 %copy-start.6 = (bf16[128,1152]{1,0:T(8,128)(2,1)}, bf16[128,1152]{1,0:T(8,128)(2,1)S(1)}, u32[]{:S(2)}) copy-start(bf16[128,1152]{1,0:T(8,128)(2,1)S(1)} %get-tuple-element.44.refs_0_) | copy-start | bytes 884740
  30.0 11.2 %collective-permute-start.5 = (bf16[128,1152]{1,0:T(8,128)(2,1)S(1)}, bf16[128,1152]{1,0:T(8,128)(2,1)S(1)}, u32[]{:S(2)}, u32[]{:S(2)}) collective-permute-start(bf16[128,1152]{1,0:T(8,128)(2,1)S(1)} %get-tuple-element.44.refs_0_), channel_id=1, source_target_pairs={{0,112},{2,114},{1,113},{3,115},{4,116},{6,118},{5,117},{7,119},{8... | collective-permute-start | bytes 884744 | tf_op jit(solution)/shard_map/ppermute | solution.py:34
  35.6 8.7 %collective-permute-start.4 = (bf16[128,1152]{1,0:T(8,128)(2,1)S(1)}, bf16[128,1152]{1,0:T(8,128)(2,1)S(1)}, u32[]{:S(2)}, u32[]{:S(2)}) collective-permute-start(bf16[128,1152]{1,0:T(8,128)(2,1)S(1)} %get-tuple-element.44.refs_0_), channel_id=1, source_target_pairs={{0,16},{2,18},{1,17},{3,19},{4,20},{6,22},{5,21},{7,23},{8,24},{10... | collective-permute-start | bytes 884744 | tf_op jit(solution)/shard_map/ppermute | solution.py:34
  35.6 8.7 %collective-permute-start.10 = (bf16[128,1152]{1,0:T(8,128)(2,1)S(1)}, bf16[128,1152]{1,0:T(8,128)(2,1)S(1)}, u32[]{:S(2)}, u32[]{:S(2)}) collective-permute-start(bf16[128,1152]{1,0:T(8,128)(2,1)S(1)} %shard_map.90.refs_0_), channel_id=1, source_target_pairs={{0,8},{2,10},{1,9},{3,11},{4,12},{6,14},{5,13},{7,15},{8,0},{10,2}... | collective-permute-start | bytes 884744 | tf_op jit(solution)/shard_map/ppermute | solution.py:34
  41.2 16.5 %copy-start.8 = (bf16[128,1152]{1,0:T(8,128)(2,1)}, bf16[128,1152]{1,0:T(8,128)(2,1)S(1)}, u32[]{:S(2)}) copy-start(bf16[128,1152]{1,0:T(8,128)(2,1)S(1)} %collective-permute-done.5.refs_2_) | copy-start | bytes 884740
  44.3 6.5 %copy-start.10 = (bf16[128,1152]{1,0:T(8,128)(2,1)}, bf16[128,1152]{1,0:T(8,128)(2,1)S(1)}, u32[]{:S(2)}) copy-start(bf16[128,1152]{1,0:T(8,128)(2,1)S(1)} %collective-permute-done.4.refs_1_) | copy-start | bytes 884740
  44.4 16.9 %collective-permute-start.12 = (bf16[512,1152]{1,0:T(8,128)(2,1)S(1)}, bf16[512,1152]{1,0:T(8,128)(2,1)S(1)}, u32[]{:S(2)}, u32[]{:S(2)}) collective-permute-start(bf16[512,1152]{1,0:T(8,128)(2,1)S(1)} %shard_map.91.refs_7_.refs_8_), channel_id=1, source_target_pairs={{0,3},{2,0},{1,2},{3,1},{4,7},{6,4},{5,6},{7,5},{8,11},{10,8},{9,1... | collective-permute-start | bytes 3538952 | tf_op jit(solution)/shard_map/ppermute | solution.py:34
  48.1 16.8 %collective-permute-start.11 = (bf16[512,1152]{1,0:T(8,128)(2,1)S(1)}, bf16[512,1152]{1,0:T(8,128)(2,1)}, u32[]{:S(2)}, u32[]{:S(2)}) collective-permute-start(bf16[512,1152]{1,0:T(8,128)(2,1)S(1)} %shard_map.91.refs_7_.refs_8_), channel_id=1, source_target_pairs={{0,2},{2,1},{1,3},{3,0},{4,6},{6,5},{5,7},{7,4},{8,10},{10,9},{9,1... | collective-permute-start | bytes 3538952 | tf_op jit(solution)/shard_map/ppermute | solution.py:34
  48.1 9.6 %collective-permute-start.6 = (bf16[128,1152]{1,0:T(8,128)(2,1)S(1)}, bf16[128,1152]{1,0:T(8,128)(2,1)}, u32[]{:S(2)}, u32[]{:S(2)}) collective-permute-start(bf16[128,1152]{1,0:T(8,128)(2,1)S(1)} %collective-permute-done.4.refs_1_), channel_id=1, source_target_pairs={{0,16},{2,18},{1,17},{3,19},{4,20},{6,22},{5,21},{7,23},{8,24},{10... | collective-permute-start | bytes 884744 | tf_op jit(solution)/shard_map/ppermute | solution.py:34
  48.1 9.6 %collective-permute-start.7 = (bf16[128,1152]{1,0:T(8,128)(2,1)S(1)}, bf16[128,1152]{1,0:T(8,128)(2,1)}, u32[]{:S(2)}, u32[]{:S(2)}) collective-permute-start(bf16[128,1152]{1,0:T(8,128)(2,1)S(1)} %collective-permute-done.5.refs_2_), channel_id=1, source_target_pairs={{0,112},{2,114},{1,113},{3,115},{4,116},{6,118},{5,117},{7,119},{8... | collective-permute-start | bytes 884744 | tf_op jit(solution)/shard_map/ppermute | solution.py:34
  57.7 8.8 %collective-permute-start.8 = (bf16[128,1152]{1,0:T(8,128)(2,1)}, bf16[128,1152]{1,0:T(8,128)(2,1)S(1)}, u32[]{:S(2)}, u32[]{:S(2)}) collective-permute-start(bf16[128,1152]{1,0:T(8,128)(2,1)} %collective-permute-done.6.refs_3_), channel_id=1, source_target_pairs={{0,16},{2,18},{1,17},{3,19},{4,20},{6,22},{5,21},{7,23},{8,24},{10... | collective-permute-start | bytes 884744 | tf_op jit(solution)/shard_map/ppermute | solution.py:34
  57.7 8.7 %collective-permute-start.9 = (bf16[128,1152]{1,0:T(8,128)(2,1)}, bf16[128,1152]{1,0:T(8,128)(2,1)S(1)}, u32[]{:S(2)}, u32[]{:S(2)}) collective-permute-start(bf16[128,1152]{1,0:T(8,128)(2,1)} %collective-permute-done.7.refs_4_), channel_id=1, source_target_pairs={{0,112},{2,114},{1,113},{3,115},{4,116},{6,118},{5,117},{7,119},{8... | collective-permute-start | bytes 884744 | tf_op jit(solution)/shard_map/ppermute | solution.py:34
  61.3 8.0 %copy-start.7 = (bf16[128,1152]{1,0:T(8,128)(2,1)S(1)}, bf16[128,1152]{1,0:T(8,128)(2,1)}, u32[]{:S(2)}) copy-start(bf16[128,1152]{1,0:T(8,128)(2,1)} %copy-done.6) | copy-start | bytes 884740
  61.3 8.0 %copy-start.9 = (bf16[128,1152]{1,0:T(8,128)(2,1)S(1)}, bf16[128,1152]{1,0:T(8,128)(2,1)}, u32[]{:S(2)}) copy-start(bf16[128,1152]{1,0:T(8,128)(2,1)} %copy-done.8) | copy-start | bytes 884740
  61.3 8.0 %copy-start.11 = (bf16[128,1152]{1,0:T(8,128)(2,1)S(1)}, bf16[128,1152]{1,0:T(8,128)(2,1)}, u32[]{:S(2)}) copy-start(bf16[128,1152]{1,0:T(8,128)(2,1)} %copy-done.10) | copy-start | bytes 884740
  61.3 13.9 %collective-permute-start.15 = (bf16[256,1152]{1,0:T(8,128)(2,1)S(1)}, bf16[256,1152]{1,0:T(8,128)(2,1)S(1)}, u32[]{:S(2)}, u32[]{:S(2)}) collective-permute-start(bf16[256,1152]{1,0:T(8,128)(2,1)S(1)} %slice.9), channel_id=1, source_target_pairs={{0,3},{2,0},{1,2},{3,1},{4,7},{6,4},{5,6},{7,5},{8,11},{10,8},{9,1... | collective-permute-start | bytes 1769480 | tf_op jit(solution)/shard_map/ppermute | solution.py:34
  66.1 10.3 %collective-permute-start.14 = (bf16[256,1152]{1,0:T(8,128)(2,1)S(1)}, bf16[256,1152]{1,0:T(8,128)(2,1)S(1)}, u32[]{:S(2)}, u32[]{:S(2)}) collective-permute-start(bf16[256,1152]{1,0:T(8,128)(2,1)S(1)} %slice.8), channel_id=1, source_target_pairs={{0,2},{2,1},{1,3},{3,0},{4,6},{6,5},{5,7},{7,4},{8,10},{10,9},{9,1... | collective-permute-start | bytes 1769480 | tf_op jit(solution)/shard_map/ppermute | solution.py:34
  66.5 9.9 %copy-start.1 = (f32[128,128]{1,0:T(8,128)S(1)}, f32[128,128]{1,0:T(8,128)}, u32[]{:S(2)}) copy-start(f32[128,128]{1,0:T(8,128)} %copy-done) | copy-start | bytes 196612
  66.5 9.9 %copy-start.14 = (f32[128,128]{1,0:T(8,128)S(1)}, f32[128,128]{1,0:T(8,128)}, u32[]{:S(2)}) copy-start(f32[128,128]{1,0:T(8,128)} %copy-done.13) | copy-start | bytes 196612
  66.5 8.7 %collective-permute-start.13 = (bf16[128,1152]{1,0:T(8,128)(2,1)S(1)}, bf16[128,1152]{1,0:T(8,128)(2,1)S(1)}, u32[]{:S(2)}, u32[]{:S(2)}) collective-permute-start(bf16[128,1152]{1,0:T(8,128)(2,1)S(1)} %broadcast_select_fusion), channel_id=1, source_target_pairs={{0,16},{2,18},{1,17},{3,19},{4,20},{6,22},{5,21},{7,23},{8,24},{10... | collective-permute-start | bytes 884744 | tf_op jit(solution)/shard_map/ppermute | solution.py:34
  84.7 3.7 %copy-start.2 = (f32[128,128]{1,0:T(8,128)S(1)}, f32[128,128]{1,0:T(8,128)}, u32[]{:S(2)}) copy-start(f32[128,128]{1,0:T(8,128)} %copy-done) | copy-start | bytes 196612
  84.7 3.7 %copy-start.4 = (f32[128,128]{1,0:T(8,128)S(1)}, f32[128,128]{1,0:T(8,128)}, u32[]{:S(2)}) copy-start(f32[128,128]{1,0:T(8,128)} %copy-done.3) | copy-start | bytes 196612
  84.7 23.7 %all-to-all-start = ((bf16[8,32,1280]{2,1,0:T(8,128)(2,1)}), bf16[8,32,1280]{2,1,0:T(8,128)(2,1)S(1)}, u32[]{:S(2)}, u32[]{:S(2)}) async-start(bf16[8,32,1280]{2,1,0:T(8,128)(2,1)} %bitcast.11), calls=%async_computation | async-start | bytes 1310720 | tf_op jit(solution)/shard_map/all_to_all | solution.py:478
  108.7 2.2 %collective-permute-start.16 = (f32[40,576]{1,0:T(8,128)S(1)}, f32[40,576]{1,0:T(8,128)S(1)}, u32[]{:S(2)}, u32[]{:S(2)}) collective-permute-start(f32[40,576]{1,0:T(8,128)S(1)} %get-tuple-element.55), channel_id=1, source_target_pairs={{0,128},{2,130},{1,129},{3,131},{4,132},{6,134},{5,133},{7,135},{8... | collective-permute-start | bytes 276488 | tf_op jit(solution)/shard_map/ppermute | solution.py:34

commit v9 on v6

--- a/solution.py
+++ b/solution.py
@@ -417,9 +417,8 @@
     z_step()
     z_step()
     last = over_z(jnp.where(g_idx == 0, back[3], ahead[3]), (1, -1))
-    far_top = over_plane(text_back[: 2 * rows], 1, 1)
-    far_low = over_plane(text_ahead[2 * rows :], -1, 1)
-    texts = [joined, text_back, text_ahead, far_top, far_low]
+    far = over_plane(text_ahead, -1, 1)
+    texts = [joined, text_back, text_ahead, far]
     images = [z_img, back[1], ahead[1], back[2], ahead[2], back[3], ahead[3], last]
 
     all_img, n_text = NZ * rows, NX * NY * rows

time: 113 us -> 120 us (1.062)
  waiting for transfers between devices: 46.4 us -> 55.4 us
  local copies, waits for them, and re-layouts: 3.05 us -> 1.23 us
    ppermute x17 -> x16, waiting for transfers between devices: 26.8 us -> 35.7 us  [permute(): return lax.ppermute(v, AXES, perm)]
    ppermute x17 -> x16, starting transfers between devices: 29.8 us -> 29.4 us  [permute(): return lax.ppermute(v, AXES, perm)]
  transfers between devices with their start and end apart: 18 -> 17, of which waited for: 11 -> 9; matrix products, arithmetic and copies ran while one was open for 1% -> 0% of each run, Pallas kernels for 14% -> 13%
where the time goes in v9:
time: 120 us
  waiting for transfers between devices  55.4 us (46%)
  starting transfers between devices  33 us (28%)
  Pallas kernels  29.5 us (25%)
  local copies, waits for them, and re-layouts  1.23 us (1%)
    ppermute x16, waiting for transfers between devices, permute(): return lax.ppermute(v, AXES, perm)  35.7 us
    ppermute x16, starting transfers between devices, permute(): return lax.ppermute(v, AXES, perm)  29.4 us
    all_to_all x1, waiting for transfers between devices, shards(): load = lax.all_to_all(load, 'z', 0, 0, tiled=True)  19.7 us
    pallas_call x9, Pallas kernels, call(): pl.pallas_call(kernel, in_specs=[pl.BlockSpec(memory_space=pltpu.SMEM)] *...  19 us
    pallas_call x2, Pallas kernels, from_hbm(): pl.pallas_call(kernel, in_specs=[pl.BlockSpec(memory_space=pltpu.SMEM)] +...  10.5 us
    all_to_all x1, starting transfers between devices, shards(): load = lax.all_to_all(load, 'z', 0, 0, tiled=True)  3.54 us
  transfers between devices with their start and end apart: 17, of which 9 were waited for; matrix products, arithmetic and copies ran while one was open for 0% of the time, Pallas kernels for 13%

profile of v9, /device:TPU:1, one launch (start us, length us, event | category | flops | bytes accessed | tf_op | source)
XLA Modules:
  0.0 119.9 jit_solution(7071739215078805553)
XLA Ops:
  0.7 0.1 stack.27.pos_ref
  0.7 1.1 copy-done.1
  1.9 2.8 %shard_map.86 = (f32[128,1152]{1,0:T(8,128)S(1)}, bf16[128,1152]{1,0:T(8,128)(2,1)S(1)}) custom-call(s32[6]{0:T(128)S(1)} %stack.27.pos_ref, bf16[256,1152]{1,0:T(8,128)(2,1)S(1)} %copy-done.1, bf16[576,1152]{1,0:T(8,128)(2,1)} %bitcast.20), custom_call_target="tpu_custom_call" | custom-call | flops 339738624 | bytes 11534336 | tf_op jit(solution)/shard_map/pallas_call | solution.py:165
  4.7 3.8 %collective-permute-start = (bf16[128,1152]{1,0:T(8,128)(2,1)S(1)}, bf16[128,1152]{1,0:T(8,128)(2,1)S(1)}, u32[]{:S(2)}, u32[]{:S(2)}) collective-permute-start(bf16[128,1152]{1,0:T(8,128)(2,1)S(1)} %get-tuple-element.39), channel_id=1, source_target_pairs={{0,1},{2,3},{1,0},{3,2},{4,5},{6,7},{5,4},{7,6},{8,9},{10,11},{9,8... | collective-permute-start | bytes 884744 | tf_op jit(solution)/shard_map/ppermute | solution.py:34
  8.5 7.7 %shard_map.87 = (f32[128,1152]{1,0:T(8,128)S(1)}, bf16[128,1152]{1,0:T(8,128)(2,1)S(1)}) custom-call(s32[6]{0:T(128)S(1)} %stack.27.pos_ref, bf16[256,1152]{1,0:T(8,128)(2,1)S(1)} %copy-done, f32[1,1152]{1,0:T(1,128)S(1)} %copy-done.2, bf16[2152,1152]{1,0:T(8,128)(2,1)} %bitcast.18, bf16[2152,1152]{1,0:T(8,128)(2,1)} %bitcast.19), custom_call_target="tpu_custom_call" | custom-call | flops 2538602496 | bytes 11534336 | tf_op jit(solution)/shard_map/pallas_call | solution.py:165
  16.2 0.0 copy-start.3
  16.2 0.0 collective-permute-done.recv_ref
  16.3 1.6 %collective-permute-start.1 = (bf16[128,1152]{1,0:T(8,128)(2,1)S(1)}, bf16[128,1152]{1,0:T(8,128)(2,1)S(1)}, u32[]{:S(2)}, u32[]{:S(2)}) collective-permute-start(bf16[128,1152]{1,0:T(8,128)(2,1)S(1)} %get-tuple-element.40), channel_id=1, source_target_pairs={{0,1},{2,3},{1,0},{3,2},{4,5},{6,7},{5,4},{7,6},{8,9},{10,11},{9,8... | collective-permute-start | bytes 884744 | tf_op jit(solution)/shard_map/ppermute | solution.py:34
  17.9 0.2 shard_map.90.refs_0_
  18.0 1.4 %collective-permute-start.3 = (bf16[128,1152]{1,0:T(8,128)(2,1)S(1)}, bf16[128,1152]{1,0:T(8,128)(2,1)S(1)}, u32[]{:S(2)}, u32[]{:S(2)}) collective-permute-start(bf16[128,1152]{1,0:T(8,128)(2,1)S(1)} %shard_map.90.refs_0_), channel_id=1, source_target_pairs={{0,12},{2,14},{1,13},{3,15},{4,0},{6,2},{5,1},{7,3},{8,4},{10,6},{... | collective-permute-start | bytes 884744 | tf_op jit(solution)/shard_map/ppermute | solution.py:34
  19.4 0.2 collective-permute-start.2
  19.6 0.5 shard_map.88
  20.1 5.4 %collective-permute-done.1.recv_ref = bf16[128,1152]{1,0:T(8,128)(2,1)S(1)} collective-permute-done((bf16[128,1152]{1,0:T(8,128)(2,1)S(1)}, bf16[128,1152]{1,0:T(8,128)(2,1)S(1)}, u32[]{:S(2)}, u32[]{:S(2)}) %collective-permute-start.1) | collective-permute-done | bytes 294944 | tf_op jit(solution)/shard_map/ppermute | solution.py:34
  25.5 0.2 shard_map.89
  25.6 3.4 %collective-permute-done.3.refs_2_ = bf16[128,1152]{1,0:T(8,128)(2,1)S(1)} collective-permute-done((bf16[128,1152]{1,0:T(8,128)(2,1)S(1)}, bf16[128,1152]{1,0:T(8,128)(2,1)S(1)}, u32[]{:S(2)}, u32[]{:S(2)}) %collective-permute-start.3) | collective-permute-done | bytes 294944 | tf_op jit(solution)/shard_map/ppermute | solution.py:34
  29.0 1.0 collective-permute-done.2.refs_1_
  30.0 5.6 %collective-permute-start.5 = (bf16[128,1152]{1,0:T(8,128)(2,1)S(1)}, bf16[128,1152]{1,0:T(8,128)(2,1)S(1)}, u32[]{:S(2)}, u32[]{:S(2)}) collective-permute-start(bf16[128,1152]{1,0:T(8,128)(2,1)S(1)} %get-tuple-element.44.refs_0_), channel_id=1, source_target_pairs={{0,112},{2,114},{1,113},{3,115},{4,116},{6,118},{5,117},{7,119},{8... | collective-permute-start | bytes 884744 | tf_op jit(solution)/shard_map/ppermute | solution.py:34
  35.6 0.0 collective-permute-start.4
  35.6 1.2 %collective-permute-start.10 = (bf16[128,1152]{1,0:T(8,128)(2,1)S(1)}, bf16[128,1152]{1,0:T(8,128)(2,1)S(1)}, u32[]{:S(2)}, u32[]{:S(2)}) collective-permute-start(bf16[128,1152]{1,0:T(8,128)(2,1)S(1)} %shard_map.90.refs_0_), channel_id=1, source_target_pairs={{0,8},{2,10},{1,9},{3,11},{4,12},{6,14},{5,13},{7,15},{8,0},{10,2}... | collective-permute-start | bytes 884744 | tf_op jit(solution)/shard_map/ppermute | solution.py:34
  36.8 4.5 %collective-permute-done.5.refs_2_ = bf16[128,1152]{1,0:T(8,128)(2,1)S(1)} collective-permute-done((bf16[128,1152]{1,0:T(8,128)(2,1)S(1)}, bf16[128,1152]{1,0:T(8,128)(2,1)S(1)}, u32[]{:S(2)}, u32[]{:S(2)}) %collective-permute-start.5) | collective-permute-done | bytes 294944 | tf_op jit(solution)/shard_map/ppermute | solution.py:34
  41.4 3.1 %collective-permute-done.4.refs_1_ = bf16[128,1152]{1,0:T(8,128)(2,1)S(1)} collective-permute-done((bf16[128,1152]{1,0:T(8,128)(2,1)S(1)}, bf16[128,1152]{1,0:T(8,128)(2,1)S(1)}, u32[]{:S(2)}, u32[]{:S(2)}) %collective-permute-start.4) | collective-permute-done | bytes 294944 | tf_op jit(solution)/shard_map/ppermute | solution.py:34
  44.5 0.0 collective-permute-done.10.refs_3_
  44.5 0.1 shard_map.91.refs_7_.refs_8_
  44.6 3.6 %collective-permute-start.12 = (bf16[512,1152]{1,0:T(8,128)(2,1)S(1)}, bf16[512,1152]{1,0:T(8,128)(2,1)}, u32[]{:S(2)}, u32[]{:S(2)}) collective-permute-start(bf16[512,1152]{1,0:T(8,128)(2,1)S(1)} %shard_map.91.refs_7_.refs_8_), channel_id=1, source_target_pairs={{0,3},{2,0},{1,2},{3,1},{4,7},{6,4},{5,6},{7,5},{8,11},{10,8},{9,1... | collective-permute-start | bytes 3538952 | tf_op jit(solution)/shard_map/ppermute | solution.py:34
  48.1 0.0 collective-permute-start.11
  48.1 0.0 collective-permute-start.6
  48.1 2.7 %collective-permute-start.7 = (bf16[128,1152]{1,0:T(8,128)(2,1)S(1)}, bf16[128,1152]{1,0:T(8,128)(2,1)}, u32[]{:S(2)}, u32[]{:S(2)}) collective-permute-start(bf16[128,1152]{1,0:T(8,128)(2,1)S(1)} %collective-permute-done.5.refs_2_), channel_id=1, source_target_pairs={{0,112},{2,114},{1,113},{3,115},{4,116},{6,118},{5,117},{7,119},{8... | collective-permute-start | bytes 884744 | tf_op jit(solution)/shard_map/ppermute | solution.py:34
  50.8 10.5 %collective-permute-done.12.refs_9_.refs_10_ = bf16[512,1152]{1,0:T(8,128)(2,1)} collective-permute-done((bf16[512,1152]{1,0:T(8,128)(2,1)S(1)}, bf16[512,1152]{1,0:T(8,128)(2,1)}, u32[]{:S(2)}, u32[]{:S(2)}) %collective-permute-start.12) | collective-permute-done | bytes 1179680 | tf_op jit(solution)/shard_map/ppermute | solution.py:34
  61.3 3.5 %collective-permute-start.14 = (bf16[512,1152]{1,0:T(8,128)(2,1)}, bf16[512,1152]{1,0:T(8,128)(2,1)}, u32[]{:S(2)}, u32[]{:S(2)}) collective-permute-start(bf16[512,1152]{1,0:T(8,128)(2,1)} %collective-permute-done.12.refs_9_.refs_10_), channel_id=1, source_target_pairs={{0,3},{2,0},{1,2},{3,1},{4,7},{6,4},{5,6},{7,5},{8,11},{10,8},{9,1... | collective-permute-start | bytes 3538952 | tf_op jit(solution)/shard_map/ppermute | solution.py:34
  64.8 0.0 collective-permute-done.6.refs_3_
  64.8 0.0 collective-permute-start.8
  64.8 0.0 collective-permute-done.7.refs_4_
  64.8 2.7 %collective-permute-start.9 = (bf16[128,1152]{1,0:T(8,128)(2,1)}, bf16[128,1152]{1,0:T(8,128)(2,1)S(1)}, u32[]{:S(2)}, u32[]{:S(2)}) collective-permute-start(bf16[128,1152]{1,0:T(8,128)(2,1)} %collective-permute-done.7.refs_4_), channel_id=1, source_target_pairs={{0,112},{2,114},{1,113},{3,115},{4,116},{6,118},{5,117},{7,119},{8... | collective-permute-start | bytes 884744 | tf_op jit(solution)/shard_map/ppermute | solution.py:34
  67.5 6.9 %collective-permute-done.8.refs_5_ = bf16[128,1152]{1,0:T(8,128)(2,1)S(1)} collective-permute-done((bf16[128,1152]{1,0:T(8,128)(2,1)}, bf16[128,1152]{1,0:T(8,128)(2,1)S(1)}, u32[]{:S(2)}, u32[]{:S(2)}) %collective-permute-start.8) | collective-permute-done | bytes 294944 | tf_op jit(solution)/shard_map/ppermute | solution.py:34
  74.3 0.0 collective-permute-done.9.refs_6_
  74.4 2.7 %collective-permute-start.13 = (bf16[128,1152]{1,0:T(8,128)(2,1)S(1)}, bf16[128,1152]{1,0:T(8,128)(2,1)S(1)}, u32[]{:S(2)}, u32[]{:S(2)}) collective-permute-start(bf16[128,1152]{1,0:T(8,128)(2,1)S(1)} %broadcast_select_fusion), channel_id=1, source_target_pairs={{0,16},{2,18},{1,17},{3,19},{4,20},{6,22},{5,21},{7,23},{8,24},{10... | collective-permute-start | bytes 884744 | tf_op jit(solution)/shard_map/ppermute | solution.py:34
  77.0 0.0 collective-permute-done.11.refs_8_.refs_9_
  77.0 6.3 %shard_map.92.early_ref = f32[8,128]{1,0:T(8,128)S(1)} custom-call(bf16[128,1152]{1,0:T(8,128)(2,1)S(1)} %get-tuple-element.44.refs_0_, bf16[128,1152]{1,0:T(8,128)(2,1)S(1)} %collective-permute-done.4.refs_1_, bf16[128,1152]{1,0:T(8,128)(2,1)S(1)} %collective-permute-done.5.refs_2_, bf16[128,1152]{1,0:T(8,128)(2,1)} %collective-permute-done.6.refs_3_, ...), custom_call_target="tpu_custom_call" | custom-call | flops 2415919104 | bytes 1048576 | tf_op jit(solution)/shard_map/pallas_call | solution.py:64
  83.3 0.0 collective-permute-done.13.refs_7_
  83.3 0.0 collective-permute-done.14.refs_11_
  83.3 8.9 %shard_map.93 = bf16[256,1280]{1,0:T(8,128)(2,1)} custom-call(s32[6]{0:T(128)S(1)} %stack.27.pos_ref, f32[128,128]{1,0:T(8,128)S(1)} %get-tuple-element.35.chosen_ref, f32[128,128]{1,0:T(8,128)S(1)} %get-tuple-element.36.place_ref, f32[8,128]{1,0:T(8,128)S(1)} %shard_map.92.early_ref, bf16[128,1152]{1,0:T(8,128)(2,1)S(1)} %get-tuple-element.44.refs_0_, ...), custom_call_target="tpu_custom_call" | custom-call | flops 4831838208 | bytes 1048576 | tf_op jit(solution)/shard_map/pallas_call | solution.py:64
  92.2 3.5 %all-to-all-start = ((bf16[8,32,1280]{2,1,0:T(8,128)(2,1)}), bf16[8,32,1280]{2,1,0:T(8,128)(2,1)S(1)}, u32[]{:S(2)}, u32[]{:S(2)}) async-start(bf16[8,32,1280]{2,1,0:T(8,128)(2,1)} %bitcast.11), calls=%async_computation | async-start | bytes 1310720 | tf_op jit(solution)/shard_map/all_to_all | solution.py:441
  95.8 1.0 shard_map.94
  96.8 19.7 %all-to-all-done = bf16[8,32,1280]{2,1,0:T(8,128)(2,1)S(1)} async-done(((bf16[8,32,1280]{2,1,0:T(8,128)(2,1)}), bf16[8,32,1280]{2,1,0:T(8,128)(2,1)S(1)}, u32[]{:S(2)}, u32[]{:S(2)}) %all-to-all-start) | async-done | bytes 655392 | tf_op jit(solution)/shard_map/all_to_all | solution.py:441
  116.4 0.2 shard_map.95
  116.7 0.6 collective-permute-start.15
  117.2 0.9 collective-permute-done.15.recv_ref
  118.2 1.7 %shard_map.96 = (f32[1,128]{1,0:T(1,128)}, f32[576,128]{1,0:T(8,128)}) custom-call(s32[6]{0:T(128)S(1)} %stack.27.pos_ref, f32[40,576]{1,0:T(8,128)S(1)} %get-tuple-element.54.keep_ref, f32[40,576]{1,0:T(8,128)S(1)} %collective-permute-done.15.recv_ref, f32[128,128]{1,0:T(8,128)S(1)} %get-tuple-element.36.place_ref), custom_call_target="tpu_custom_call" | custom-call | flops 29491200 | bytes 1048576 | tf_op jit(solution)/shard_map/pallas_call | solution.py:64
  (7 shorter events, 0.0 us)
Async XLA Ops:
  0.6 7.9 %copy-start = (bf16[256,1152]{1,0:T(8,128)(2,1)S(1)}, bf16[256,1152]{1,0:T(8,128)(2,1)}, u32[]{:S(2)}) copy-start(bf16[256,1152]{1,0:T(8,128)(2,1)} %x_hbm) | copy-start | bytes 1769476
  0.7 1.1 copy-start.1
  1.9 6.6 %copy-start.2 = (f32[1,1152]{1,0:T(1,128)S(1)}, f32[1,1152]{1,0:T(1,128)}, u32[]{:S(2)}) copy-start(f32[1,1152]{1,0:T(1,128)} %gain_hbm.1) | copy-start | bytes 13828
  4.7 11.6 %collective-permute-start = (bf16[128,1152]{1,0:T(8,128)(2,1)S(1)}, bf16[128,1152]{1,0:T(8,128)(2,1)S(1)}, u32[]{:S(2)}, u32[]{:S(2)}) collective-permute-start(bf16[128,1152]{1,0:T(8,128)(2,1)S(1)} %get-tuple-element.39), channel_id=1, source_target_pairs={{0,1},{2,3},{1,0},{3,2},{4,5},{6,7},{5,4},{7,6},{8,9},{10,11},{9,8... | collective-permute-start | bytes 884744 | tf_op jit(solution)/shard_map/ppermute | solution.py:34
  16.2 3.4 %copy-start.3 = (s32[2048]{0:T(1024)S(1)}, s32[2048]{0:T(1024)}, u32[]{:S(2)}) copy-start(s32[2048]{0:T(1024)} %param.13) | copy-start | bytes 24580
  16.3 9.2 %collective-permute-start.1 = (bf16[128,1152]{1,0:T(8,128)(2,1)S(1)}, bf16[128,1152]{1,0:T(8,128)(2,1)S(1)}, u32[]{:S(2)}, u32[]{:S(2)}) collective-permute-start(bf16[128,1152]{1,0:T(8,128)(2,1)S(1)} %get-tuple-element.40), channel_id=1, source_target_pairs={{0,1},{2,3},{1,0},{3,2},{4,5},{6,7},{5,4},{7,6},{8,9},{10,11},{9,8... | collective-permute-start | bytes 884744 | tf_op jit(solution)/shard_map/ppermute | solution.py:34
  18.0 11.0 %collective-permute-start.3 = (bf16[128,1152]{1,0:T(8,128)(2,1)S(1)}, bf16[128,1152]{1,0:T(8,128)(2,1)S(1)}, u32[]{:S(2)}, u32[]{:S(2)}) collective-permute-start(bf16[128,1152]{1,0:T(8,128)(2,1)S(1)} %shard_map.90.refs_0_), channel_id=1, source_target_pairs={{0,12},{2,14},{1,13},{3,15},{4,0},{6,2},{5,1},{7,3},{8,4},{10,6},{... | collective-permute-start | bytes 884744 | tf_op jit(solution)/shard_map/ppermute | solution.py:34
  19.4 10.6 %collective-permute-start.2 = (bf16[128,1152]{1,0:T(8,128)(2,1)S(1)}, bf16[128,1152]{1,0:T(8,128)(2,1)S(1)}, u32[]{:S(2)}, u32[]{:S(2)}) collective-permute-start(bf16[128,1152]{1,0:T(8,128)(2,1)S(1)} %shard_map.90.refs_0_), channel_id=1, source_target_pairs={{0,4},{2,6},{1,5},{3,7},{4,8},{6,10},{5,9},{7,11},{8,12},{10,14},{... | collective-permute-start | bytes 884744 | tf_op jit(solution)/shard_map/ppermute | solution.py:34
  30.0 11.3 %collective-permute-start.5 = (bf16[128,1152]{1,0:T(8,128)(2,1)S(1)}, bf16[128,1152]{1,0:T(8,128)(2,1)S(1)}, u32[]{:S(2)}, u32[]{:S(2)}) collective-permute-start(bf16[128,1152]{1,0:T(8,128)(2,1)S(1)} %get-tuple-element.44.refs_0_), channel_id=1, source_target_pairs={{0,112},{2,114},{1,113},{3,115},{4,116},{6,118},{5,117},{7,119},{8... | collective-permute-start | bytes 884744 | tf_op jit(solution)/shard_map/ppermute | solution.py:34
  35.6 8.9 %collective-permute-start.4 = (bf16[128,1152]{1,0:T(8,128)(2,1)S(1)}, bf16[128,1152]{1,0:T(8,128)(2,1)S(1)}, u32[]{:S(2)}, u32[]{:S(2)}) collective-permute-start(bf16[128,1152]{1,0:T(8,128)(2,1)S(1)} %get-tuple-element.44.refs_0_), channel_id=1, source_target_pairs={{0,16},{2,18},{1,17},{3,19},{4,20},{6,22},{5,21},{7,23},{8,24},{10... | collective-permute-start | bytes 884744 | tf_op jit(solution)/shard_map/ppermute | solution.py:34
  35.6 8.9 %collective-permute-start.10 = (bf16[128,1152]{1,0:T(8,128)(2,1)S(1)}, bf16[128,1152]{1,0:T(8,128)(2,1)S(1)}, u32[]{:S(2)}, u32[]{:S(2)}) collective-permute-start(bf16[128,1152]{1,0:T(8,128)(2,1)S(1)} %shard_map.90.refs_0_), channel_id=1, source_target_pairs={{0,8},{2,10},{1,9},{3,11},{4,12},{6,14},{5,13},{7,15},{8,0},{10,2}... | collective-permute-start | bytes 884744 | tf_op jit(solution)/shard_map/ppermute | solution.py:34
  44.6 16.7 %collective-permute-start.12 = (bf16[512,1152]{1,0:T(8,128)(2,1)S(1)}, bf16[512,1152]{1,0:T(8,128)(2,1)}, u32[]{:S(2)}, u32[]{:S(2)}) collective-permute-start(bf16[512,1152]{1,0:T(8,128)(2,1)S(1)} %shard_map.91.refs_7_.refs_8_), channel_id=1, source_target_pairs={{0,3},{2,0},{1,2},{3,1},{4,7},{6,4},{5,6},{7,5},{8,11},{10,8},{9,1... | collective-permute-start | bytes 3538952 | tf_op jit(solution)/shard_map/ppermute | solution.py:34
  48.1 28.9 %collective-permute-start.11 = (bf16[512,1152]{1,0:T(8,128)(2,1)S(1)}, bf16[512,1152]{1,0:T(8,128)(2,1)}, u32[]{:S(2)}, u32[]{:S(2)}) collective-permute-start(bf16[512,1152]{1,0:T(8,128)(2,1)S(1)} %shard_map.91.refs_7_.refs_8_), channel_id=1, source_target_pairs={{0,2},{2,1},{1,3},{3,0},{4,6},{6,5},{5,7},{7,4},{8,10},{10,9},{9,1... | collective-permute-start | bytes 3538952 | tf_op jit(solution)/shard_map/ppermute | solution.py:34
  48.1 16.7 %collective-permute-start.6 = (bf16[128,1152]{1,0:T(8,128)(2,1)S(1)}, bf16[128,1152]{1,0:T(8,128)(2,1)}, u32[]{:S(2)}, u32[]{:S(2)}) collective-permute-start(bf16[128,1152]{1,0:T(8,128)(2,1)S(1)} %collective-permute-done.4.refs_1_), channel_id=1, source_target_pairs={{0,16},{2,18},{1,17},{3,19},{4,20},{6,22},{5,21},{7,23},{8,24},{10... | collective-permute-start | bytes 884744 | tf_op jit(solution)/shard_map/ppermute | solution.py:34
  48.1 16.7 %collective-permute-start.7 = (bf16[128,1152]{1,0:T(8,128)(2,1)S(1)}, bf16[128,1152]{1,0:T(8,128)(2,1)}, u32[]{:S(2)}, u32[]{:S(2)}) collective-permute-start(bf16[128,1152]{1,0:T(8,128)(2,1)S(1)} %collective-permute-done.5.refs_2_), channel_id=1, source_target_pairs={{0,112},{2,114},{1,113},{3,115},{4,116},{6,118},{5,117},{7,119},{8... | collective-permute-start | bytes 884744 | tf_op jit(solution)/shard_map/ppermute | solution.py:34
  61.3 22.0 %collective-permute-start.14 = (bf16[512,1152]{1,0:T(8,128)(2,1)}, bf16[512,1152]{1,0:T(8,128)(2,1)}, u32[]{:S(2)}, u32[]{:S(2)}) collective-permute-start(bf16[512,1152]{1,0:T(8,128)(2,1)} %collective-permute-done.12.refs_9_.refs_10_), channel_id=1, source_target_pairs={{0,3},{2,0},{1,2},{3,1},{4,7},{6,4},{5,6},{7,5},{8,11},{10,8},{9,1... | collective-permute-start | bytes 3538952 | tf_op jit(solution)/shard_map/ppermute | solution.py:34
  64.8 9.5 %collective-permute-start.8 = (bf16[128,1152]{1,0:T(8,128)(2,1)}, bf16[128,1152]{1,0:T(8,128)(2,1)S(1)}, u32[]{:S(2)}, u32[]{:S(2)}) collective-permute-start(bf16[128,1152]{1,0:T(8,128)(2,1)} %collective-permute-done.6.refs_3_), channel_id=1, source_target_pairs={{0,16},{2,18},{1,17},{3,19},{4,20},{6,22},{5,21},{7,23},{8,24},{10... | collective-permute-start | bytes 884744 | tf_op jit(solution)/shard_map/ppermute | solution.py:34
  64.8 9.5 %collective-permute-start.9 = (bf16[128,1152]{1,0:T(8,128)(2,1)}, bf16[128,1152]{1,0:T(8,128)(2,1)S(1)}, u32[]{:S(2)}, u32[]{:S(2)}) collective-permute-start(bf16[128,1152]{1,0:T(8,128)(2,1)} %collective-permute-done.7.refs_4_), channel_id=1, source_target_pairs={{0,112},{2,114},{1,113},{3,115},{4,116},{6,118},{5,117},{7,119},{8... | collective-permute-start | bytes 884744 | tf_op jit(solution)/shard_map/ppermute | solution.py:34
  74.4 8.9 %collective-permute-start.13 = (bf16[128,1152]{1,0:T(8,128)(2,1)S(1)}, bf16[128,1152]{1,0:T(8,128)(2,1)S(1)}, u32[]{:S(2)}, u32[]{:S(2)}) collective-permute-start(bf16[128,1152]{1,0:T(8,128)(2,1)S(1)} %broadcast_select_fusion), channel_id=1, source_target_pairs={{0,16},{2,18},{1,17},{3,19},{4,20},{6,22},{5,21},{7,23},{8,24},{10... | collective-permute-start | bytes 884744 | tf_op jit(solution)/shard_map/ppermute | solution.py:34
  92.2 24.2 %all-to-all-start = ((bf16[8,32,1280]{2,1,0:T(8,128)(2,1)}), bf16[8,32,1280]{2,1,0:T(8,128)(2,1)S(1)}, u32[]{:S(2)}, u32[]{:S(2)}) async-start(bf16[8,32,1280]{2,1,0:T(8,128)(2,1)} %bitcast.11), calls=%async_computation | async-start | bytes 1310720 | tf_op jit(solution)/shard_map/all_to_all | solution.py:441
  116.7 1.5 %collective-permute-start.15 = (f32[40,576]{1,0:T(8,128)S(1)}, f32[40,576]{1,0:T(8,128)S(1)}, u32[]{:S(2)}, u32[]{:S(2)}) collective-permute-start(f32[40,576]{1,0:T(8,128)S(1)} %get-tuple-element.55), channel_id=1, source_target_pairs={{0,128},{2,130},{1,129},{3,131},{4,132},{6,134},{5,133},{7,135},{8... | collective-permute-start | bytes 276488 | tf_op jit(solution)/shard_map/ppermute | solution.py:34
